TPU v7x, 32 devices: a whole 2x2x4 slice. The times are simulated.
32 devices in a mesh: dom: 8 (over y, x, core), grp: 4 (over z).
Axes of the slice: x: 2, y: 2, z: 4, core: 2. Of those that a mesh axis runs over, the one named last changes fastest.
Arguments:
- orbitals: float32 [512, 48, 512], P('grp', 'dom'), may hold values from -10 to 10, as said below
- potential: float32 [48, 512], P('dom'), may hold values from -2 to 2
Outputs:
- filtered: float32 [512, 48, 512], P('grp', 'dom')
- correlation: float32 [512, 512], P('grp', 'dom')
Inputs may be any that keep to these rules, and one draw needn't show every extreme that they name: `orbitals`: entries of order one.
All inputs are finite; a program needn't handle non-finite values.
Results may differ from a plain program's by a relative error of at most 0.003.
Values may be sent and summed in bfloat16 or wider, within the bound.
No kernel may reach another device: no remote copies, remote signals or barrier semaphores. Data moves between devices by JAX's collectives and lax.ppermute only.
A program may use at most 64 MiB of HBM per device.

v0:
```python
import functools

import jax
import jax.numpy as jnp
import numpy as np
from jax import lax
from jax.experimental import pallas as pl
from jax.experimental.pallas import tpu as pltpu
from jax.sharding import PartitionSpec as P

NX = 32
NY = 16


COEFFS = [
    -5369.0 / 1800.0,
    12.0 / 7.0,
    -15.0 / 56.0,
    10.0 / 189.0,
    -1.0 / 112.0,
    2.0 / 1925.0,
    -1.0 / 16632.0,
]
CENTER = 13.0
HALF_WIDTH = 11.0
SCALE = -0.5 / 0.25 / HALF_WIDTH

RANGE_STEP = 25.0
RANGE_BASE = 125.0
ROWS = 8
ORBITALS = 16
POT_ROWS = 8
VMEM_BYTES = 48 * 1024 * 1024


def plane_stencil():
    cells = np.arange(NY * NX)
    row_of = cells // NX
    col_of = cells % NX
    row_gap = (row_of[:, None] - row_of[None, :]) % NY
    col_gap = (col_of[:, None] - col_of[None, :]) % NX
    same_row = row_of[:, None] == row_of[None, :]
    same_col = col_of[:, None] == col_of[None, :]
    stencil = np.zeros((NY * NX, NY * NX))
    for reach in range(1, 7):
        along_rows = same_col & ((row_gap == reach) | (row_gap == NY - reach))
        along_cols = same_row & ((col_gap == reach) | (col_gap == NX - reach))
        stencil += COEFFS[reach] * along_rows + COEFFS[reach] * along_cols
    return stencil


def with_sign(magnitude, value):
    return jnp.where(value < 0, -magnitude, magnitude)


def range_code(value):
    return with_sign(jnp.exp2(jnp.abs(value) * RANGE_STEP - RANGE_BASE), value).astype(jnp.bfloat16)


def range_decode(code):
    code = code.astype(jnp.float32)
    return with_sign((jnp.log2(jnp.abs(code)) + RANGE_BASE) * (1.0 / RANGE_STEP), code)


def power_code(value, squarings):
    magnitude = value
    for _ in range(squarings):
        magnitude = magnitude * magnitude
    return with_sign(magnitude, value).astype(jnp.bfloat16)


def power_decode(code, squarings):
    code = code.astype(jnp.float32)
    return with_sign(jnp.exp2(jnp.log2(jnp.abs(code)) * (0.5**squarings)), code)


def whole_call(kernel, out_shape, in_specs, scratch=(), flops=0):
    spaces = {"s": pltpu.SMEM, "v": pltpu.VMEM, "h": pltpu.HBM}
    return pl.pallas_call(
        kernel,
        out_shape=out_shape,
        in_specs=[pl.BlockSpec(memory_space=spaces[space]) for space in in_specs],
        scratch_shapes=list(scratch),
        compiler_params=pltpu.CompilerParams(vmem_limit_bytes=VMEM_BYTES),
        cost_estimate=pl.CostEstimate(flops=flops, bytes_accessed=1 << 20, transcendentals=0),
    )


def pack_kernel(domains, place, orbitals, potential, *refs):
    outs, (held, field, sems) = refs[:domains], refs[domains:]
    planes, own, cells = held.shape
    copies = [pltpu.make_async_copy(potential, field, sems.at[planes])]
    copies += [pltpu.make_async_copy(orbitals.at[plane], held.at[plane], sems.at[plane]) for plane in range(planes)]
    for copy in copies:
        copy.start()
    copies[0].wait()
    tail = jnp.concatenate([field[...], jnp.zeros((POT_ROWS - planes, cells), jnp.float32)], axis=0)
    for plane in range(planes):
        copies[1 + plane].wait()
        for gap in range(domains):
            start = pl.multiple_of((place[0] ^ gap) * ORBITALS, ORBITALS)
            rows = held[plane, pl.ds(start, ORBITALS)]
            if plane == planes - 1:
                rows = jnp.concatenate([rows, tail], axis=0)
            outs[gap][plane * ORBITALS : plane * ORBITALS + rows.shape[0]] = range_code(rows)


def filter_kernel(domains, planes, order, place, *refs):
    coded, weights, outs = refs[:domains], refs[domains], refs[domains + 1 : 2 * domains + 1]
    field, first, second, left, product = refs[2 * domains + 1 :]
    cells = coded[0].shape[1]
    total = domains * planes
    length = planes * ORBITALS
    for ref, gap in zip(coded, order):
        part = place[0] ^ gap
        value = range_decode(ref[...])
        for plane in range(planes):
            row = pl.multiple_of((part * planes + plane) * ROWS, ROWS)
            for half in range(2):
                start = (2 * plane + half) * ROWS
                first[half, pl.ds(row, ROWS)] = value[start : start + ROWS]
        field[pl.ds(pl.multiple_of(part * POT_ROWS, POT_ROWS), POT_ROWS)] = (
            2.0 * (value[length:] - CENTER) * (1.0 / HALF_WIDTH) + 6.0 * COEFFS[0] * SCALE
        )

    def prepare(half, source):
        value = source[half]
        upper = value.astype(jnp.bfloat16)
        left[half, :, :cells] = upper
        left[half, :, cells : 2 * cells] = (value - upper.astype(jnp.float32)).astype(jnp.bfloat16)
        left[half, :, 2 * cells :] = upper

    def multiply(half, lanes):
        product[half, :, lanes] = jnp.dot(left[half], weights[:, lanes], preferred_element_type=jnp.float32)

    def add_along_z(half, lanes, source, target, opening):
        for lane in range(lanes.start, lanes.stop, 128):

            def column(plane):
                start = (plane % total) * ROWS
                return half, slice(start, start + ROWS), slice(lane, lane + 128)

            line = [source[column(plane)] for plane in range(total)]
            for plane in range(total):
                row = plane // planes * POT_ROWS + plane % planes
                sum_ = product[column(plane)] + field[row : row + 1, lane : lane + 128] * line[plane]
                for reach in range(1, 7):
                    sum_ += (2.0 * SCALE * COEFFS[reach]) * (
                        line[(plane + reach) % total] + line[(plane - reach) % total]
                    )
                target[column(plane)] = 0.5 * sum_ if opening else sum_ - target[column(plane)]

    tiles = [slice(lane, lane + 256) for lane in range(0, cells, 256)]
    prepare(0, first)
    for lanes in tiles:
        multiply(0, lanes)
    prepare(1, first)
    for degree in range(4):
        source, target = (first, second) if degree % 2 == 0 else (second, first)
        for lanes in tiles:
            multiply(1, lanes)
            add_along_z(0, lanes, source, target, degree == 0)
        if degree < 3:
            prepare(0, target)
        for lanes in tiles:
            if degree < 3:
                multiply(0, lanes)
            add_along_z(1, lanes, source, target, degree == 0)
        if degree < 3:
            prepare(1, target)
    for gap in range(domains):
        for plane in range(planes):
            row = pl.multiple_of(((place[0] ^ gap) * planes + plane) * ROWS, ROWS)
            value = jnp.concatenate([first[half, pl.ds(row, ROWS)] for half in range(2)], axis=0)
            outs[gap][plane * ORBITALS : (plane + 1) * ORBITALS] = power_code(value, 3)


def quarter_kernel(groups, planes, spot, *refs):
    coded, outs, rounded = refs[: -groups - 1], refs[-groups - 1 : -1], refs[-1]
    lanes = outs[0].shape[2]
    for index, ref in enumerate(coded):
        value = power_decode(ref[...], 3).astype(jnp.bfloat16)
        for plane in range(planes):
            rounded[plane, index * ORBITALS : (index + 1) * ORBITALS] = value[
                plane * ORBITALS : (plane + 1) * ORBITALS
            ]
    for gap in range(groups):
        start = pl.multiple_of((spot[0] ^ gap) * lanes, lanes)
        outs[gap][...] = rounded[:, :, pl.ds(start, lanes)]


def write_kernel(planes, order, place, *refs):
    coded, filtered = refs[:-1], refs[-1]
    for ref, gap in zip(coded, order):
        start = pl.multiple_of((place[0] ^ gap) * ORBITALS, ORBITALS)
        value = power_decode(ref[...], 3)
        for plane in range(planes):
            filtered[plane, pl.ds(start, ORBITALS)] = value[plane * ORBITALS : (plane + 1) * ORBITALS]


def gram_kernel(domains, along, sets, scale, place, spot, *refs):
    quarters, (kept, sent, rows, tile) = refs[:-4], refs[-4:]
    planes, _, lanes = quarters[0].shape
    own = domains * ORBITALS
    for index, gaps in enumerate(sets):
        for turn, far in enumerate(along):
            for slot, gap in enumerate(gaps):
                start = (spot[0] ^ far) * own + (place[0] ^ gap) * ORBITALS
                start = pl.multiple_of(start, ORBITALS)
                for plane in range(planes):
                    rows[pl.ds(start, ORBITALS), plane * lanes : (plane + 1) * lanes] = quarters[
                        index * len(along) + turn
                    ][plane, slot * ORBITALS : (slot + 1) * ORBITALS]
    right = rows[...]
    tile[...] = scale * lax.dot_general(
        right, right, (((1,), (1,)), ((), ())), preferred_element_type=jnp.float32
    )
    length = tile.shape[0] // domains
    for index in range(domains // 2):
        near = pl.multiple_of((place[0] ^ (2 * index)) * length, length)
        far = pl.multiple_of((place[0] ^ (2 * index + 1)) * length, length)
        kept[index * length : (index + 1) * length] = tile[pl.ds(near, length)]
        sent[index * length : (index + 1) * length] = power_code(tile[pl.ds(far, length)], 2)


def merge_kernel(kept, came, *outs):
    length = outs[0].shape[0]
    for index, out in enumerate(outs):
        rows = slice(index * length, (index + 1) * length)
        value = kept[rows] + power_decode(came[rows], 2)
        out[...] = power_code(value, 2) if index else value


def combine_kernel(groups, spot, *refs):
    parts, outs, total = refs[: -groups - 1], refs[-groups - 1 : -1], refs[-1]
    sum_ = parts[0][...]
    for part in parts[1:]:
        sum_ += power_decode(part[...], 2)
    total[...] = sum_
    lanes = outs[0].shape[1]
    for gap in range(groups):
        start = pl.multiple_of((spot[0] ^ gap) * lanes, lanes)
        outs[gap][...] = total[:, pl.ds(start, lanes)]


def finish_kernel(*refs):
    sum_ = refs[0][...]
    for part in refs[1:-1]:
        sum_ += part[...]
    refs[-1][...] = sum_


def swap(block, axis, gap):
    count = lax.axis_size(axis)
    return lax.ppermute(block, axis, [(i, i ^ gap) for i in range(count)])


def exchange(blocks, axis, order):
    came = list(blocks)
    for gap in order:
        came[gap] = swap(blocks[gap], axis, gap)
    return came


def transposed_shards(domains, groups, orbitals, potential):
    own, planes, cells = orbitals.shape
    stencil = 2.0 * SCALE * plane_stencil()
    high = stencil.astype(jnp.bfloat16)
    low = (stencil - high.astype(np.float64)).astype(jnp.bfloat16)
    weights = jnp.asarray(np.concatenate([high, high, low], axis=0))
    place = lax.axis_index("dom").astype(jnp.int32).reshape(1)
    spot = lax.axis_index("grp").astype(jnp.int32).reshape(1)
    length = planes * ORBITALS
    half_rows = domains * planes * ROWS
    lanes = cells // groups
    orbs = own * groups
    columns = orbs // domains
    hops = lambda gap: bin(gap >> 1).count("1")
    order = sorted(range(1, domains), key=lambda gap: (-hops(gap), gap))
    along = sorted(range(1, groups), key=lambda gap: (-(gap >> 1), gap))

    def arrays(count, shape, dtype):
        return (jax.ShapeDtypeStruct(shape, dtype),) * count

    packed = whole_call(
        functools.partial(pack_kernel, domains),
        arrays(domains, (length + POT_ROWS, cells), jnp.bfloat16),
        "shh",
        (
            pltpu.VMEM((planes, own, cells), jnp.float32),
            pltpu.VMEM((planes, cells), jnp.float32),
            pltpu.SemaphoreType.DMA((planes + 1,)),
        ),
        flops=1 << 20,
    )(place, orbitals.transpose(1, 0, 2), potential)
    arrived = exchange(packed, "dom", order)
    order = [0] + order
    coded = whole_call(
        functools.partial(filter_kernel, domains, planes, order),
        arrays(domains, (length, cells), jnp.bfloat16),
        "s" + "v" * domains + "v",
        (
            pltpu.VMEM((domains * POT_ROWS, cells), jnp.float32),
            pltpu.VMEM((2, half_rows, cells), jnp.float32),
            pltpu.VMEM((2, half_rows, cells), jnp.float32),
            pltpu.VMEM((2, half_rows, 3 * cells), jnp.bfloat16),
            pltpu.VMEM((2, half_rows, cells), jnp.float32),
        ),
        flops=4 * 3 * 4 * half_rows * cells * cells,
    )(place, *[arrived[gap] for gap in order], weights)
    late = [gap for gap in order if hops(gap) == 1]
    early = [gap for gap in order if gap not in late]
    coded = exchange(coded, "dom", early[1:] + late)
    quarters = []
    for gaps in (early, late):
        quarter = whole_call(
            functools.partial(quarter_kernel, groups, planes),
            arrays(groups, (planes, len(gaps) * ORBITALS, lanes), jnp.bfloat16),
            "s" + "v" * len(gaps),
            (pltpu.VMEM((planes, len(gaps) * ORBITALS, cells), jnp.bfloat16),),
            flops=1 << 24,
        )(spot, *[coded[gap] for gap in gaps])
        if gaps is early:
            quarter = list(quarter)
            quarter[0], coded[late[0]] = lax.optimization_barrier((quarter[0], coded[late[0]]))
        quarter = exchange(quarter, "grp", along)
        quarters += [quarter[gap] for gap in [0] + along]
    filtered = whole_call(
        functools.partial(write_kernel, planes, early + late),
        arrays(1, (planes, own, cells), jnp.float32)[0],
        "s" + "v" * domains,
        flops=1 << 24,
    )(place, *[coded[gap] for gap in early + late])
    filtered, quarters[0] = lax.optimization_barrier((filtered, quarters[0]))
    kept, sent = whole_call(
        functools.partial(gram_kernel, domains, [0] + along, (early, late), 1.0 / (domains * planes * cells)),
        arrays(1, (orbs // 2, orbs), jnp.float32) + arrays(1, (orbs // 2, orbs), jnp.bfloat16),
        "ss" + "v" * len(quarters),
        (pltpu.VMEM((orbs, planes * lanes), jnp.bfloat16), pltpu.VMEM((orbs, orbs), jnp.float32)),
        flops=1 << 28,
    )(place, spot, *quarters)
    chips = domains // 2
    merged = whole_call(
        merge_kernel,
        arrays(1, (columns, orbs), jnp.float32) + arrays(chips - 1, (columns, orbs), jnp.bfloat16),
        "vv",
        flops=1 << 20,
    )(kept, swap(sent, "dom", 1))
    parts = [merged[0]] + [swap(merged[gap // 2], "dom", gap) for gap in order if gap and gap % 2 == 0]
    combined = whole_call(
        functools.partial(combine_kernel, groups),
        arrays(groups, (columns, own), jnp.float32),
        "s" + "v" * chips,
        (pltpu.VMEM((columns, orbs), jnp.float32),),
        flops=1 << 20,
    )(spot, *parts)
    combined = exchange(combined, "grp", along)
    correlation = whole_call(
        finish_kernel, arrays(1, (columns, own), jnp.float32)[0], "v" * groups, flops=1 << 16
    )(*[combined[gap] for gap in [0] + along])
    return filtered.transpose(1, 0, 2), correlation.T


def padded_2(cells, sides, width):
    for axis, dim in sides:
        count = lax.axis_size(axis)
        head = lax.slice_in_dim(cells, 0, width, axis=dim)
        tail = lax.slice_in_dim(cells, cells.shape[dim] - width, cells.shape[dim], axis=dim)
        cells = jnp.concatenate(
            [
                lax.ppermute(tail, axis, [(i, (i + 1) % count) for i in range(count)]),
                cells,
                lax.ppermute(head, axis, [((i + 1) % count, i) for i in range(count)]),
            ],
            axis=dim,
        )
    return cells


def hamiltonian(block, field, stencil):
    count, planes, cells = block.shape
    padded = padded_2(block, (("dom", 1),), 6)
    in_plane = jnp.dot(
        block.reshape((count * planes, cells)),
        stencil,
        precision=lax.Precision.HIGHEST,
        preferred_element_type=jnp.float32,
    ).reshape(block.shape)
    laplace = in_plane + 3.0 * COEFFS[0] * block
    for reach in range(1, 7):
        along_z = (
            padded[:, 6 + reach : 6 + reach + planes] + padded[:, 6 - reach : 6 - reach + planes]
        )
        laplace = laplace + COEFFS[reach] * along_z
    return -0.5 / 0.25 * laplace + field[None] * block


def halo_shards(orbitals, potential):
    stencil = jnp.asarray(plane_stencil().astype(np.float32))
    previous = orbitals
    current = (hamiltonian(orbitals, potential, stencil) - CENTER * orbitals) / HALF_WIDTH
    for degree in range(3):
        following = (
            2.0 * (hamiltonian(current, potential, stencil) - CENTER * current) / HALF_WIDTH
            - previous
        )
        previous = current
        current = following
    own_count = current.shape[0]
    local_cells = current.shape[1] * current.shape[2]
    total_cells = local_cells * lax.axis_size("dom")
    mine = current.astype(jnp.bfloat16).reshape(own_count, local_cells)
    tile = lax.dot_general(
        mine,
        lax.all_gather(mine, "grp", axis=0, tiled=True),
        (((1,), (1,)), ((), ())),
        preferred_element_type=jnp.float32,
    )
    summed = lax.psum_scatter(tile, "dom", scatter_dimension=1, tiled=True)
    correlation = summed / total_cells
    return (current, correlation)


def solution(mesh):
    domains, groups = mesh.shape["dom"], mesh.shape["grp"]
    in_specs = (P("grp", "dom", None), P("dom", None))
    out_specs = (P("grp", "dom", None), P("grp", "dom"))

    def shards(orbitals, potential):
        own, planes, cells = orbitals.shape
        pairs = domains > 1 and domains & (domains - 1) == 0 and groups & (groups - 1) == 0
        fits = own == ORBITALS * domains and own % 128 == 0 and planes <= POT_ROWS
        if pairs and fits and cells % 256 == 0 and cells == 128 * groups and own * groups % (16 * domains) == 0:
            return transposed_shards(domains, groups, orbitals, potential)
        return halo_shards(orbitals, potential)

    return jax.shard_map(shards, mesh=mesh, in_specs=in_specs, out_specs=out_specs, check_vma=False)
```

profile of v0, /device:TPU:0, one launch (start us, length us, event | category | flops | bytes accessed | tf_op | source)
XLA Modules:
  0.0 76.9 jit_solution(9733963552087184295)
XLA Ops:
  0.6 1.4 %copy-done = f32[128,6,512]{2,0,1:T(8,128)S(1)} copy-done((f32[128,6,512]{2,0,1:T(8,128)S(1)}, f32[128,6,512]{2,0,1:T(8,128)}, u32[]{:S(2)}) %copy-start) | copy-done | bytes 1572888
  2.0 0.7 copy-done.1
  2.8 0.6 shard_map.50
  3.4 4.0 %collective-permute-start = (bf16[104,512]{1,0:T(8,128)(2,1)S(1)}, bf16[104,512]{1,0:T(8,128)(2,1)S(1)}, u32[]{:S(2)}, u32[]{:S(2)}) collective-permute-start(bf16[104,512]{1,0:T(8,128)(2,1)S(1)} %get-tuple-element.41), channel_id=1, source_target_pairs={{0,24},{4,28},{8,16},{12,20},{16,8},{20,12},{24,0},{28,4},{1,25},{... | collective-permute-start | bytes 319496 | tf_op jit(solution)/shard_map/ppermute | solution.py:255
  7.4 0.0 collective-permute-start.1
  7.4 1.1 %collective-permute-start.2 = (bf16[104,512]{1,0:T(8,128)(2,1)S(1)}, bf16[104,512]{1,0:T(8,128)(2,1)S(1)}, u32[]{:S(2)}, u32[]{:S(2)}) collective-permute-start(bf16[104,512]{1,0:T(8,128)(2,1)S(1)} %get-tuple-element.43), channel_id=1, source_target_pairs={{0,8},{4,12},{8,0},{12,4},{16,24},{20,28},{24,16},{28,20},{1,9},{5... | collective-permute-start | bytes 319496 | tf_op jit(solution)/shard_map/ppermute | solution.py:255
  8.5 0.6 collective-permute-start.3
  9.1 1.7 %collective-permute-start.4 = (bf16[104,512]{1,0:T(8,128)(2,1)S(1)}, bf16[104,512]{1,0:T(8,128)(2,1)S(1)}, u32[]{:S(2)}, u32[]{:S(2)}) collective-permute-start(bf16[104,512]{1,0:T(8,128)(2,1)S(1)} %get-tuple-element.45), channel_id=1, source_target_pairs={{0,16},{4,20},{8,24},{12,28},{16,0},{20,4},{24,8},{28,12},{1,17},{... | collective-permute-start | bytes 319496 | tf_op jit(solution)/shard_map/ppermute | solution.py:255
  10.8 0.0 collective-permute-done.refs_1_
  10.8 0.0 collective-permute-start.5
  10.9 2.7 %collective-permute-done.1.refs_2_ = bf16[104,512]{1,0:T(8,128)(2,1)S(1)} collective-permute-done((bf16[104,512]{1,0:T(8,128)(2,1)S(1)}, bf16[104,512]{1,0:T(8,128)(2,1)S(1)}, u32[]{:S(2)}, u32[]{:S(2)}) %collective-permute-start.1) | collective-permute-done | bytes 106528 | tf_op jit(solution)/shard_map/ppermute | solution.py:255
  13.5 0.0 collective-permute-start.6
  13.5 1.9 %collective-permute-done.2.refs_3_ = bf16[104,512]{1,0:T(8,128)(2,1)S(1)} collective-permute-done((bf16[104,512]{1,0:T(8,128)(2,1)S(1)}, bf16[104,512]{1,0:T(8,128)(2,1)S(1)}, u32[]{:S(2)}, u32[]{:S(2)}) %collective-permute-start.2) | collective-permute-done | bytes 106528 | tf_op jit(solution)/shard_map/ppermute | solution.py:255
  15.5 1.7 %collective-permute-done.3.refs_4_ = bf16[104,512]{1,0:T(8,128)(2,1)S(1)} collective-permute-done((bf16[104,512]{1,0:T(8,128)(2,1)S(1)}, bf16[104,512]{1,0:T(8,128)(2,1)S(1)}, u32[]{:S(2)}, u32[]{:S(2)}) %collective-permute-start.3) | collective-permute-done | bytes 106528 | tf_op jit(solution)/shard_map/ppermute | solution.py:255
  17.1 0.0 collective-permute-done.4.refs_5_
  17.1 0.7 collective-permute-done.5.refs_6_
  17.8 0.0 collective-permute-done.6.refs_7_
  17.8 10.6 %shard_map.51 = (bf16[96,512]{1,0:T(8,128)(2,1)S(1)}, bf16[96,512]{1,0:T(8,128)(2,1)S(1)}, bf16[96,512]{1,0:T(8,128)(2,1)S(1)}, bf16[96,512]{1,0:T(8,128)(2,1)S(...) custom-call(s32[1]{0:T(128)} %bitcast.place, ...), custom_call_target="tpu_custom_call" | custom-call | flops 4831838208 | bytes 1048576 | tf_op jit(solution)/shard_map/pallas_call | solution.py:298
  28.4 1.7 %collective-permute-start.7 = (bf16[96,512]{1,0:T(8,128)(2,1)S(1)}, bf16[96,512]{1,0:T(8,128)(2,1)S(1)}, u32[]{:S(2)}, u32[]{:S(2)}) collective-permute-start(bf16[96,512]{1,0:T(8,128)(2,1)S(1)} %get-tuple-element.49), channel_id=1, source_target_pairs={{0,24},{4,28},{8,16},{12,20},{16,8},{20,12},{24,0},{28,4},{1,25},{... | collective-permute-start | bytes 294920 | tf_op jit(solution)/shard_map/ppermute | solution.py:255
  30.2 0.7 collective-permute-start.8
  30.8 0.7 collective-permute-start.9
  31.5 0.9 %collective-permute-start.10 = (bf16[96,512]{1,0:T(8,128)(2,1)S(1)}, bf16[96,512]{1,0:T(8,128)(2,1)S(1)}, u32[]{:S(2)}, u32[]{:S(2)}) collective-permute-start(bf16[96,512]{1,0:T(8,128)(2,1)S(1)} %get-tuple-element.53), channel_id=1, source_target_pairs={{0,8},{4,12},{8,0},{12,4},{16,24},{20,28},{24,16},{28,20},{1,9},{5... | collective-permute-start | bytes 294920 | tf_op jit(solution)/shard_map/ppermute | solution.py:255
  32.5 0.4 collective-permute-start.11
  32.9 1.4 %collective-permute-done.7.refs_1_ = bf16[96,512]{1,0:T(8,128)(2,1)S(1)} collective-permute-done((bf16[96,512]{1,0:T(8,128)(2,1)S(1)}, bf16[96,512]{1,0:T(8,128)(2,1)S(1)}, u32[]{:S(2)}, u32[]{:S(2)}) %collective-permute-start.7) | collective-permute-done | bytes 98336 | tf_op jit(solution)/shard_map/ppermute | solution.py:255
  34.3 1.2 %collective-permute-start.12 = (bf16[96,512]{1,0:T(8,128)(2,1)S(1)}, bf16[96,512]{1,0:T(8,128)(2,1)S(1)}, u32[]{:S(2)}, u32[]{:S(2)}) collective-permute-start(bf16[96,512]{1,0:T(8,128)(2,1)S(1)} %get-tuple-element.56), channel_id=1, source_target_pairs={{0,16},{4,20},{8,24},{12,28},{16,0},{20,4},{24,8},{28,12},{1,17},{... | collective-permute-start | bytes 294920 | tf_op jit(solution)/shard_map/ppermute | solution.py:255
  35.5 0.7 collective-permute-done.8.refs_2_
  36.2 0.9 %collective-permute-start.13 = (bf16[96,512]{1,0:T(8,128)(2,1)S(1)}, bf16[96,512]{1,0:T(8,128)(2,1)S(1)}, u32[]{:S(2)}, u32[]{:S(2)}) collective-permute-start(bf16[96,512]{1,0:T(8,128)(2,1)S(1)} %get-tuple-element.57), channel_id=1, source_target_pairs={{0,20},{4,16},{8,28},{12,24},{16,4},{20,0},{24,12},{28,8},{1,21},{... | collective-permute-start | bytes 294920 | tf_op jit(solution)/shard_map/ppermute | solution.py:255
  37.0 0.0 collective-permute-done.9.refs_3_
  37.0 0.3 shard_map.52
  37.4 2.6 %collective-permute-start.14 = (bf16[6,64,128]{2,1,0:T(8,128)(2,1)S(1)}, bf16[6,64,128]{2,1,0:T(8,128)(2,1)S(1)}, u32[]{:S(2)}, u32[]{:S(2)}) collective-permute-start(bf16[6,64,128]{2,1,0:T(8,128)(2,1)S(1)} %get-tuple-element.61), channel_id=1, source_target_pairs={{0,2},{1,3},{2,0},{3,1},{4,6},{5,7},{6,4},{7,5},{8,10},{9,11},{10,... | collective-permute-start | bytes 294920 | tf_op jit(solution)/shard_map/ppermute | solution.py:255
  40.0 0.0 collective-permute-done.10.refs_4_.refs_0_
  40.0 1.8 %collective-permute-start.15 = (bf16[6,64,128]{2,1,0:T(8,128)(2,1)S(1)}, bf16[6,64,128]{2,1,0:T(8,128)(2,1)S(1)}, u32[]{:S(2)}, u32[]{:S(2)}) collective-permute-start(bf16[6,64,128]{2,1,0:T(8,128)(2,1)S(1)} %get-tuple-element.62), channel_id=1, source_target_pairs={{0,3},{1,2},{2,1},{3,0},{4,7},{5,6},{6,5},{7,4},{8,11},{9,10},{10,... | collective-permute-start | bytes 294920 | tf_op jit(solution)/shard_map/ppermute | solution.py:255
  41.9 0.0 collective-permute-done.11.refs_5_.refs_1_
  41.9 0.0 collective-permute-start.16
  41.9 0.0 collective-permute-done.12.refs_6_.refs_2_
  41.9 0.0 collective-permute-done.13.refs_7_.refs_3_
  41.9 0.3 shard_map.54
  42.2 2.6 %collective-permute-start.17 = (bf16[6,64,128]{2,1,0:T(8,128)(2,1)S(1)}, bf16[6,64,128]{2,1,0:T(8,128)(2,1)S(1)}, u32[]{:S(2)}, u32[]{:S(2)}) collective-permute-start(bf16[6,64,128]{2,1,0:T(8,128)(2,1)S(1)} %get-tuple-element.65), channel_id=1, source_target_pairs={{0,2},{1,3},{2,0},{3,1},{4,6},{5,7},{6,4},{7,5},{8,10},{9,11},{10,... | collective-permute-start | bytes 294920 | tf_op jit(solution)/shard_map/ppermute | solution.py:255
  44.8 1.8 %collective-permute-start.18 = (bf16[6,64,128]{2,1,0:T(8,128)(2,1)S(1)}, bf16[6,64,128]{2,1,0:T(8,128)(2,1)S(1)}, u32[]{:S(2)}, u32[]{:S(2)}) collective-permute-start(bf16[6,64,128]{2,1,0:T(8,128)(2,1)S(1)} %get-tuple-element.66), channel_id=1, source_target_pairs={{0,3},{1,2},{2,1},{3,0},{4,7},{5,6},{6,5},{7,4},{8,11},{9,10},{10,... | collective-permute-start | bytes 294920 | tf_op jit(solution)/shard_map/ppermute | solution.py:255
  46.7 2.8 %collective-permute-done.14.refs_1_ = bf16[6,64,128]{2,1,0:T(8,128)(2,1)S(1)} collective-permute-done((bf16[6,64,128]{2,1,0:T(8,128)(2,1)S(1)}, bf16[6,64,128]{2,1,0:T(8,128)(2,1)S(1)}, u32[]{:S(2)}, u32[]{:S(2)}) %collective-permute-start.14) | collective-permute-done | bytes 98336 | tf_op jit(solution)/shard_map/ppermute | solution.py:255
  49.5 0.0 collective-permute-start.19
  49.5 1.6 %shard_map.53 = f32[6,128,512]{2,1,0:T(8,128)} custom-call(s32[1]{0:T(128)} %bitcast.place, bf16[96,512]{1,0:T(8,128)(2,1)S(1)} %get-tuple-element.48.refs_0_, bf16[96,512]{1,0:T(8,128)(2,1)S(1)} %collective-permute-done.7.refs_1_, bf16[96,512]{1,0:T(8,128)(2,1)S(1)} %collective-permute-done.8.refs_2_, bf16[96,512]{1,0:T(8,128)(2,1)S(1)} %collective-permute-done.9.refs_3_, ...), custom_call_target="tpu_custom_call" | custom-call | flops 16777216 | bytes 1048576 | tf_op jit(solution)/shard_map/pallas_call | solution.py:328
  51.0 0.0 collective-permute-done.15.refs_2_
  51.0 0.0 collective-permute-done.16.refs_3_
  51.0 5.6 %collective-permute-done.17.refs_5_ = bf16[6,64,128]{2,1,0:T(8,128)(2,1)S(1)} collective-permute-done((bf16[6,64,128]{2,1,0:T(8,128)(2,1)S(1)}, bf16[6,64,128]{2,1,0:T(8,128)(2,1)S(1)}, u32[]{:S(2)}, u32[]{:S(2)}) %collective-permute-start.17) | collective-permute-done | bytes 98336 | tf_op jit(solution)/shard_map/ppermute | solution.py:255
  56.6 0.0 collective-permute-done.18.refs_6_
  56.6 0.9 %shard_map.55 = (f32[256,512]{1,0:T(8,128)S(1)}, bf16[256,512]{1,0:T(8,128)(2,1)S(1)}) custom-call(s32[1]{0:T(128)} %bitcast.place, s32[1]{0:T(128)} %bitcast.2.spot, bf16[6,64,128]{2,1,0:T(8,128)(2,1)S(1)} %get-tuple-element.60.refs_0_, bf16[6,64,128]{2,1,0:T(8,128)(2,1)S(1)} %collective-permute-done.14.refs_1_, ...), custom_call_target="tpu_custom_call" | custom-call | flops 268435456 | bytes 1048576 | tf_op jit(solution)/shard_map/pallas_call | solution.py:335
  57.5 0.1 collective-permute-start.20
  57.6 1.5 %collective-permute-done.20.came = bf16[256,512]{1,0:T(8,128)(2,1)S(1)} collective-permute-done((bf16[256,512]{1,0:T(8,128)(2,1)S(1)}, bf16[256,512]{1,0:T(8,128)(2,1)S(1)}, u32[]{:S(2)}, u32[]{:S(2)}) %collective-permute-start.20) | collective-permute-done | bytes 262176 | tf_op jit(solution)/shard_map/ppermute | solution.py:255
  59.1 0.2 shard_map.56
  59.4 1.6 %collective-permute-start.21 = (bf16[64,512]{1,0:T(8,128)(2,1)S(1)}, bf16[64,512]{1,0:T(8,128)(2,1)S(1)}, u32[]{:S(2)}, u32[]{:S(2)}) collective-permute-start(bf16[64,512]{1,0:T(8,128)(2,1)S(1)} %get-tuple-element.71), channel_id=1, source_target_pairs={{0,24},{4,28},{8,16},{12,20},{16,8},{20,12},{24,0},{28,4},{1,25},{... | collective-permute-start | bytes 196616 | tf_op jit(solution)/shard_map/ppermute | solution.py:255
  60.9 0.8 %collective-permute-start.22 = (bf16[64,512]{1,0:T(8,128)(2,1)S(1)}, bf16[64,512]{1,0:T(8,128)(2,1)S(1)}, u32[]{:S(2)}, u32[]{:S(2)}) collective-permute-start(bf16[64,512]{1,0:T(8,128)(2,1)S(1)} %get-tuple-element.72), channel_id=1, source_target_pairs={{0,8},{4,12},{8,0},{12,4},{16,24},{20,28},{24,16},{28,20},{1,9},{5... | collective-permute-start | bytes 196616 | tf_op jit(solution)/shard_map/ppermute | solution.py:255
  61.8 1.2 %collective-permute-start.23 = (bf16[64,512]{1,0:T(8,128)(2,1)S(1)}, bf16[64,512]{1,0:T(8,128)(2,1)S(1)}, u32[]{:S(2)}, u32[]{:S(2)}) collective-permute-start(bf16[64,512]{1,0:T(8,128)(2,1)S(1)} %get-tuple-element.73), channel_id=1, source_target_pairs={{0,16},{4,20},{8,24},{12,28},{16,0},{20,4},{24,8},{28,12},{1,17},{... | collective-permute-start | bytes 196616 | tf_op jit(solution)/shard_map/ppermute | solution.py:255
  62.9 2.3 %collective-permute-done.21.refs_1_ = bf16[64,512]{1,0:T(8,128)(2,1)S(1)} collective-permute-done((bf16[64,512]{1,0:T(8,128)(2,1)S(1)}, bf16[64,512]{1,0:T(8,128)(2,1)S(1)}, u32[]{:S(2)}, u32[]{:S(2)}) %collective-permute-start.21) | collective-permute-done | bytes 65568 | tf_op jit(solution)/shard_map/ppermute | solution.py:255
  65.3 0.1 collective-permute-done.22.refs_2_
  65.4 0.6 collective-permute-done.23.refs_3_
  66.0 0.2 shard_map.57
  66.2 4.3 %collective-permute-start.24 = (f32[64,128]{1,0:T(8,128)S(1)}, f32[64,128]{1,0:T(8,128)S(1)}, u32[]{:S(2)}, u32[]{:S(2)}) collective-permute-start(f32[64,128]{1,0:T(8,128)S(1)} %get-tuple-element.75), channel_id=1, source_target_pairs={{0,2},{1,3},{2,0},{3,1},{4,6},{5,7},{6,4},{7,5},{8,10},{9,11},{10,... | collective-permute-start | bytes 98312 | tf_op jit(solution)/shard_map/ppermute | solution.py:255
  70.5 0.5 collective-permute-start.25
  71.0 0.2 collective-permute-start.26
  71.2 1.3 %collective-permute-done.24.refs_1_ = f32[64,128]{1,0:T(8,128)S(1)} collective-permute-done((f32[64,128]{1,0:T(8,128)S(1)}, f32[64,128]{1,0:T(8,128)S(1)}, u32[]{:S(2)}, u32[]{:S(2)}) %collective-permute-start.24) | collective-permute-done | bytes 32800 | tf_op jit(solution)/shard_map/ppermute | solution.py:255
  72.4 3.8 %collective-permute-done.25.refs_2_ = f32[64,128]{1,0:T(8,128)S(1)} collective-permute-done((f32[64,128]{1,0:T(8,128)S(1)}, f32[64,128]{1,0:T(8,128)S(1)}, u32[]{:S(2)}, u32[]{:S(2)}) %collective-permute-start.25) | collective-permute-done | bytes 32800 | tf_op jit(solution)/shard_map/ppermute | solution.py:255
  76.2 0.0 collective-permute-done.26.refs_3_
  76.2 0.6 shard_map.58
  (5 shorter events, 0.0 us)
Async XLA Ops:
  0.6 1.4 %copy-start = (f32[128,6,512]{2,0,1:T(8,128)S(1)}, f32[128,6,512]{2,0,1:T(8,128)}, u32[]{:S(2)}) copy-start(f32[128,6,512]{2,0,1:T(8,128)} %param.3) | copy-start | bytes 4718596
  2.0 0.7 copy-start.1
  2.8 15.0 %copy-start.2 = (bf16[1536,512]{1,0:T(8,128)(2,1)S(1)}, bf16[1536,512]{1,0:T(8,128)(2,1)}, u32[]{:S(2)}) copy-start(bf16[1536,512]{1,0:T(8,128)(2,1)} %constant.11.clone.refs_8_) | copy-start | bytes 4718596
  3.4 7.4 %collective-permute-start = (bf16[104,512]{1,0:T(8,128)(2,1)S(1)}, bf16[104,512]{1,0:T(8,128)(2,1)S(1)}, u32[]{:S(2)}, u32[]{:S(2)}) collective-permute-start(bf16[104,512]{1,0:T(8,128)(2,1)S(1)} %get-tuple-element.41), channel_id=1, source_target_pairs={{0,24},{4,28},{8,16},{12,20},{16,8},{20,12},{24,0},{28,4},{1,25},{... | collective-permute-start | bytes 319496 | tf_op jit(solution)/shard_map/ppermute | solution.py:255
  7.4 6.2 %collective-permute-start.1 = (bf16[104,512]{1,0:T(8,128)(2,1)S(1)}, bf16[104,512]{1,0:T(8,128)(2,1)S(1)}, u32[]{:S(2)}, u32[]{:S(2)}) collective-permute-start(bf16[104,512]{1,0:T(8,128)(2,1)S(1)} %get-tuple-element.42), channel_id=1, source_target_pairs={{0,28},{4,24},{8,20},{12,16},{16,12},{20,8},{24,4},{28,0},{1,29},{... | collective-permute-start | bytes 319496 | tf_op jit(solution)/shard_map/ppermute | solution.py:255
  7.4 8.1 %collective-permute-start.2 = (bf16[104,512]{1,0:T(8,128)(2,1)S(1)}, bf16[104,512]{1,0:T(8,128)(2,1)S(1)}, u32[]{:S(2)}, u32[]{:S(2)}) collective-permute-start(bf16[104,512]{1,0:T(8,128)(2,1)S(1)} %get-tuple-element.43), channel_id=1, source_target_pairs={{0,8},{4,12},{8,0},{12,4},{16,24},{20,28},{24,16},{28,20},{1,9},{5... | collective-permute-start | bytes 319496 | tf_op jit(solution)/shard_map/ppermute | solution.py:255
  8.5 8.6 %collective-permute-start.3 = (bf16[104,512]{1,0:T(8,128)(2,1)S(1)}, bf16[104,512]{1,0:T(8,128)(2,1)S(1)}, u32[]{:S(2)}, u32[]{:S(2)}) collective-permute-start(bf16[104,512]{1,0:T(8,128)(2,1)S(1)} %get-tuple-element.44), channel_id=1, source_target_pairs={{0,12},{4,8},{8,4},{12,0},{16,28},{20,24},{24,20},{28,16},{1,13},{... | collective-permute-start | bytes 319496 | tf_op jit(solution)/shard_map/ppermute | solution.py:255
  9.1 8.0 %collective-permute-start.4 = (bf16[104,512]{1,0:T(8,128)(2,1)S(1)}, bf16[104,512]{1,0:T(8,128)(2,1)S(1)}, u32[]{:S(2)}, u32[]{:S(2)}) collective-permute-start(bf16[104,512]{1,0:T(8,128)(2,1)S(1)} %get-tuple-element.45), channel_id=1, source_target_pairs={{0,16},{4,20},{8,24},{12,28},{16,0},{20,4},{24,8},{28,12},{1,17},{... | collective-permute-start | bytes 319496 | tf_op jit(solution)/shard_map/ppermute | solution.py:255
  10.8 7.0 %collective-permute-start.5 = (bf16[104,512]{1,0:T(8,128)(2,1)S(1)}, bf16[104,512]{1,0:T(8,128)(2,1)S(1)}, u32[]{:S(2)}, u32[]{:S(2)}) collective-permute-start(bf16[104,512]{1,0:T(8,128)(2,1)S(1)} %get-tuple-element.46), channel_id=1, source_target_pairs={{0,20},{4,16},{8,28},{12,24},{16,4},{20,0},{24,12},{28,8},{1,21},{... | collective-permute-start | bytes 319496 | tf_op jit(solution)/shard_map/ppermute | solution.py:255
  13.5 4.3 %collective-permute-start.6 = (bf16[104,512]{1,0:T(8,128)(2,1)S(1)}, bf16[104,512]{1,0:T(8,128)(2,1)S(1)}, u32[]{:S(2)}, u32[]{:S(2)}) collective-permute-start(bf16[104,512]{1,0:T(8,128)(2,1)S(1)} %get-tuple-element.47), channel_id=1, source_target_pairs={{0,4},{4,0},{8,12},{12,8},{16,20},{20,16},{24,28},{28,24},{1,5},{5... | collective-permute-start | bytes 319496 | tf_op jit(solution)/shard_map/ppermute | solution.py:255
  28.4 5.9 %collective-permute-start.7 = (bf16[96,512]{1,0:T(8,128)(2,1)S(1)}, bf16[96,512]{1,0:T(8,128)(2,1)S(1)}, u32[]{:S(2)}, u32[]{:S(2)}) collective-permute-start(bf16[96,512]{1,0:T(8,128)(2,1)S(1)} %get-tuple-element.49), channel_id=1, source_target_pairs={{0,24},{4,28},{8,16},{12,20},{16,8},{20,12},{24,0},{28,4},{1,25},{... | collective-permute-start | bytes 294920 | tf_op jit(solution)/shard_map/ppermute | solution.py:255
  30.2 6.0 %collective-permute-start.8 = (bf16[96,512]{1,0:T(8,128)(2,1)S(1)}, bf16[96,512]{1,0:T(8,128)(2,1)S(1)}, u32[]{:S(2)}, u32[]{:S(2)}) collective-permute-start(bf16[96,512]{1,0:T(8,128)(2,1)S(1)} %get-tuple-element.50), channel_id=1, source_target_pairs={{0,28},{4,24},{8,20},{12,16},{16,12},{20,8},{24,4},{28,0},{1,29},{... | collective-permute-start | bytes 294920 | tf_op jit(solution)/shard_map/ppermute | solution.py:255
  30.8 6.2 %collective-permute-start.9 = (bf16[96,512]{1,0:T(8,128)(2,1)S(1)}, bf16[96,512]{1,0:T(8,128)(2,1)S(1)}, u32[]{:S(2)}, u32[]{:S(2)}) collective-permute-start(bf16[96,512]{1,0:T(8,128)(2,1)S(1)} %get-tuple-element.51), channel_id=1, source_target_pairs={{0,4},{4,0},{8,12},{12,8},{16,20},{20,16},{24,28},{28,24},{1,5},{5... | collective-permute-start | bytes 294920 | tf_op jit(solution)/shard_map/ppermute | solution.py:255
  31.5 8.5 %collective-permute-start.10 = (bf16[96,512]{1,0:T(8,128)(2,1)S(1)}, bf16[96,512]{1,0:T(8,128)(2,1)S(1)}, u32[]{:S(2)}, u32[]{:S(2)}) collective-permute-start(bf16[96,512]{1,0:T(8,128)(2,1)S(1)} %get-tuple-element.53), channel_id=1, source_target_pairs={{0,8},{4,12},{8,0},{12,4},{16,24},{20,28},{24,16},{28,20},{1,9},{5... | collective-permute-start | bytes 294920 | tf_op jit(solution)/shard_map/ppermute | solution.py:255
  32.5 9.4 %collective-permute-start.11 = (bf16[96,512]{1,0:T(8,128)(2,1)S(1)}, bf16[96,512]{1,0:T(8,128)(2,1)S(1)}, u32[]{:S(2)}, u32[]{:S(2)}) collective-permute-start(bf16[96,512]{1,0:T(8,128)(2,1)S(1)} %get-tuple-element.55), channel_id=1, source_target_pairs={{0,12},{4,8},{8,4},{12,0},{16,28},{20,24},{24,20},{28,16},{1,13},{... | collective-permute-start | bytes 294920 | tf_op jit(solution)/shard_map/ppermute | solution.py:255
  34.3 7.5 %collective-permute-start.12 = (bf16[96,512]{1,0:T(8,128)(2,1)S(1)}, bf16[96,512]{1,0:T(8,128)(2,1)S(1)}, u32[]{:S(2)}, u32[]{:S(2)}) collective-permute-start(bf16[96,512]{1,0:T(8,128)(2,1)S(1)} %get-tuple-element.56), channel_id=1, source_target_pairs={{0,16},{4,20},{8,24},{12,28},{16,0},{20,4},{24,8},{28,12},{1,17},{... | collective-permute-start | bytes 294920 | tf_op jit(solution)/shard_map/ppermute | solution.py:255
  36.2 5.7 %collective-permute-start.13 = (bf16[96,512]{1,0:T(8,128)(2,1)S(1)}, bf16[96,512]{1,0:T(8,128)(2,1)S(1)}, u32[]{:S(2)}, u32[]{:S(2)}) collective-permute-start(bf16[96,512]{1,0:T(8,128)(2,1)S(1)} %get-tuple-element.57), channel_id=1, source_target_pairs={{0,20},{4,16},{8,28},{12,24},{16,4},{20,0},{24,12},{28,8},{1,21},{... | collective-permute-start | bytes 294920 | tf_op jit(solution)/shard_map/ppermute | solution.py:255
  37.4 12.1 %collective-permute-start.14 = (bf16[6,64,128]{2,1,0:T(8,128)(2,1)S(1)}, bf16[6,64,128]{2,1,0:T(8,128)(2,1)S(1)}, u32[]{:S(2)}, u32[]{:S(2)}) collective-permute-start(bf16[6,64,128]{2,1,0:T(8,128)(2,1)S(1)} %get-tuple-element.61), channel_id=1, source_target_pairs={{0,2},{1,3},{2,0},{3,1},{4,6},{5,7},{6,4},{7,5},{8,10},{9,11},{10,... | collective-permute-start | bytes 294920 | tf_op jit(solution)/shard_map/ppermute | solution.py:255
  40.0 11.0 %collective-permute-start.15 = (bf16[6,64,128]{2,1,0:T(8,128)(2,1)S(1)}, bf16[6,64,128]{2,1,0:T(8,128)(2,1)S(1)}, u32[]{:S(2)}, u32[]{:S(2)}) collective-permute-start(bf16[6,64,128]{2,1,0:T(8,128)(2,1)S(1)} %get-tuple-element.62), channel_id=1, source_target_pairs={{0,3},{1,2},{2,1},{3,0},{4,7},{5,6},{6,5},{7,4},{8,11},{9,10},{10,... | collective-permute-start | bytes 294920 | tf_op jit(solution)/shard_map/ppermute | solution.py:255
  41.9 9.2 %collective-permute-start.16 = (bf16[6,64,128]{2,1,0:T(8,128)(2,1)S(1)}, bf16[6,64,128]{2,1,0:T(8,128)(2,1)S(1)}, u32[]{:S(2)}, u32[]{:S(2)}) collective-permute-start(bf16[6,64,128]{2,1,0:T(8,128)(2,1)S(1)} %get-tuple-element.63), channel_id=1, source_target_pairs={{0,1},{1,0},{2,3},{3,2},{4,5},{5,4},{6,7},{7,6},{8,9},{9,8},{10,11... | collective-permute-start | bytes 294920 | tf_op jit(solution)/shard_map/ppermute | solution.py:255
  42.2 14.4 %collective-permute-start.17 = (bf16[6,64,128]{2,1,0:T(8,128)(2,1)S(1)}, bf16[6,64,128]{2,1,0:T(8,128)(2,1)S(1)}, u32[]{:S(2)}, u32[]{:S(2)}) collective-permute-start(bf16[6,64,128]{2,1,0:T(8,128)(2,1)S(1)} %get-tuple-element.65), channel_id=1, source_target_pairs={{0,2},{1,3},{2,0},{3,1},{4,6},{5,7},{6,4},{7,5},{8,10},{9,11},{10,... | collective-permute-start | bytes 294920 | tf_op jit(solution)/shard_map/ppermute | solution.py:255
  44.8 11.8 %collective-permute-start.18 = (bf16[6,64,128]{2,1,0:T(8,128)(2,1)S(1)}, bf16[6,64,128]{2,1,0:T(8,128)(2,1)S(1)}, u32[]{:S(2)}, u32[]{:S(2)}) collective-permute-start(bf16[6,64,128]{2,1,0:T(8,128)(2,1)S(1)} %get-tuple-element.66), channel_id=1, source_target_pairs={{0,3},{1,2},{2,1},{3,0},{4,7},{5,6},{6,5},{7,4},{8,11},{9,10},{10,... | collective-permute-start | bytes 294920 | tf_op jit(solution)/shard_map/ppermute | solution.py:255
  49.5 7.2 %collective-permute-start.19 = (bf16[6,64,128]{2,1,0:T(8,128)(2,1)S(1)}, bf16[6,64,128]{2,1,0:T(8,128)(2,1)S(1)}, u32[]{:S(2)}, u32[]{:S(2)}) collective-permute-start(bf16[6,64,128]{2,1,0:T(8,128)(2,1)S(1)} %get-tuple-element.67), channel_id=1, source_target_pairs={{0,1},{1,0},{2,3},{3,2},{4,5},{5,4},{6,7},{7,6},{8,9},{9,8},{10,11... | collective-permute-start | bytes 294920 | tf_op jit(solution)/shard_map/ppermute | solution.py:255
  57.5 1.6 %collective-permute-start.20 = (bf16[256,512]{1,0:T(8,128)(2,1)S(1)}, bf16[256,512]{1,0:T(8,128)(2,1)S(1)}, u32[]{:S(2)}, u32[]{:S(2)}) collective-permute-start(bf16[256,512]{1,0:T(8,128)(2,1)S(1)} %get-tuple-element.69), channel_id=1, source_target_pairs={{0,4},{4,0},{8,12},{12,8},{16,20},{20,16},{24,28},{28,24},{1,5},{5... | collective-permute-start | bytes 786440 | tf_op jit(solution)/shard_map/ppermute | solution.py:255
  59.4 5.9 %collective-permute-start.21 = (bf16[64,512]{1,0:T(8,128)(2,1)S(1)}, bf16[64,512]{1,0:T(8,128)(2,1)S(1)}, u32[]{:S(2)}, u32[]{:S(2)}) collective-permute-start(bf16[64,512]{1,0:T(8,128)(2,1)S(1)} %get-tuple-element.71), channel_id=1, source_target_pairs={{0,24},{4,28},{8,16},{12,20},{16,8},{20,12},{24,0},{28,4},{1,25},{... | collective-permute-start | bytes 196616 | tf_op jit(solution)/shard_map/ppermute | solution.py:255
  60.9 4.5 %collective-permute-start.22 = (bf16[64,512]{1,0:T(8,128)(2,1)S(1)}, bf16[64,512]{1,0:T(8,128)(2,1)S(1)}, u32[]{:S(2)}, u32[]{:S(2)}) collective-permute-start(bf16[64,512]{1,0:T(8,128)(2,1)S(1)} %get-tuple-element.72), channel_id=1, source_target_pairs={{0,8},{4,12},{8,0},{12,4},{16,24},{20,28},{24,16},{28,20},{1,9},{5... | collective-permute-start | bytes 196616 | tf_op jit(solution)/shard_map/ppermute | solution.py:255
  61.8 4.3 %collective-permute-start.23 = (bf16[64,512]{1,0:T(8,128)(2,1)S(1)}, bf16[64,512]{1,0:T(8,128)(2,1)S(1)}, u32[]{:S(2)}, u32[]{:S(2)}) collective-permute-start(bf16[64,512]{1,0:T(8,128)(2,1)S(1)} %get-tuple-element.73), channel_id=1, source_target_pairs={{0,16},{4,20},{8,24},{12,28},{16,0},{20,4},{24,8},{28,12},{1,17},{... | collective-permute-start | bytes 196616 | tf_op jit(solution)/shard_map/ppermute | solution.py:255
  66.2 6.2 %collective-permute-start.24 = (f32[64,128]{1,0:T(8,128)S(1)}, f32[64,128]{1,0:T(8,128)S(1)}, u32[]{:S(2)}, u32[]{:S(2)}) collective-permute-start(f32[64,128]{1,0:T(8,128)S(1)} %get-tuple-element.75), channel_id=1, source_target_pairs={{0,2},{1,3},{2,0},{3,1},{4,6},{5,7},{6,4},{7,5},{8,10},{9,11},{10,... | collective-permute-start | bytes 98312 | tf_op jit(solution)/shard_map/ppermute | solution.py:255
  70.5 5.7 %collective-permute-start.25 = (f32[64,128]{1,0:T(8,128)S(1)}, f32[64,128]{1,0:T(8,128)S(1)}, u32[]{:S(2)}, u32[]{:S(2)}) collective-permute-start(f32[64,128]{1,0:T(8,128)S(1)} %get-tuple-element.76), channel_id=1, source_target_pairs={{0,3},{1,2},{2,1},{3,0},{4,7},{5,6},{6,5},{7,4},{8,11},{9,10},{10,... | collective-permute-start | bytes 98312 | tf_op jit(solution)/shard_map/ppermute | solution.py:255
  71.0 5.3 %collective-permute-start.26 = (f32[64,128]{1,0:T(8,128)S(1)}, f32[64,128]{1,0:T(8,128)S(1)}, u32[]{:S(2)}, u32[]{:S(2)}) collective-permute-start(f32[64,128]{1,0:T(8,128)S(1)} %get-tuple-element.77), channel_id=1, source_target_pairs={{0,1},{1,0},{2,3},{3,2},{4,5},{5,4},{6,7},{7,6},{8,9},{9,8},{10,11... | collective-permute-start | bytes 98312 | tf_op jit(solution)/shard_map/ppermute | solution.py:255
where the time goes:
time: 77.1 us; the launch traced here: 76.9 us
  starting transfers between devices  31.5 us (41%)
  waiting for transfers between devices  27.1 us (35%)
  Pallas kernels  15.4 us (20%)
  local copies, waits for them, and re-layouts  2.12 us (3%)
    ppermute x27, starting transfers between devices, swap(): return lax.ppermute(block, axis, [(i, i ^ gap) for i in range(count)])  31.5 us
    ppermute x27, waiting for transfers between devices, swap(): return lax.ppermute(block, axis, [(i, i ^ gap) for i in range(count)])  27.1 us
    pallas_call x1, Pallas kernels, transposed_shards(): whole_call(functools.partial(filter_kernel, domains, planes, order), arra...  10.6 us
    unnamed x6, local copies, waits for them, and re-layouts  2.12 us
    pallas_call x1, Pallas kernels, transposed_shards(): whole_call(functools.partial(write_kernel, planes, early + late), arrays(...  1.56 us
  transfers between devices with their start and end apart: 27, of which 14 were waited for; matrix products, arithmetic and copies ran while one was open for 0% of the time, Pallas kernels for 3%

commit v1 on v0

--- a/solution.py
+++ b/solution.py
@@ -24,6 +24,7 @@
 CENTER = 13.0
 HALF_WIDTH = 11.0
 SCALE = -0.5 / 0.25 / HALF_WIDTH
+LIFT = 240.0 / 128.0 / abs(2.0 * SCALE * COEFFS[1])
 
 RANGE_STEP = 25.0
 RANGE_BASE = 125.0
@@ -74,14 +75,14 @@
     return with_sign(jnp.exp2(jnp.log2(jnp.abs(code)) * (0.5**squarings)), code)
 
 
-def whole_call(kernel, out_shape, in_specs, scratch=(), flops=0):
+def whole_call(kernel, out_shape, in_specs, scratch=(), flops=0, grant=VMEM_BYTES):
     spaces = {"s": pltpu.SMEM, "v": pltpu.VMEM, "h": pltpu.HBM}
     return pl.pallas_call(
         kernel,
         out_shape=out_shape,
         in_specs=[pl.BlockSpec(memory_space=spaces[space]) for space in in_specs],
         scratch_shapes=list(scratch),
-        compiler_params=pltpu.CompilerParams(vmem_limit_bytes=VMEM_BYTES),
+        compiler_params=pltpu.CompilerParams(vmem_limit_bytes=grant),
         cost_estimate=pl.CostEstimate(flops=flops, bytes_accessed=1 << 20, transcendentals=0),
     )
 
@@ -114,65 +115,46 @@
     for ref, gap in zip(coded, order):
         part = place[0] ^ gap
         value = range_decode(ref[...])
-        for plane in range(planes):
-            row = pl.multiple_of((part * planes + plane) * ROWS, ROWS)
-            for half in range(2):
-                start = (2 * plane + half) * ROWS
-                first[half, pl.ds(row, ROWS)] = value[start : start + ROWS]
-        field[pl.ds(pl.multiple_of(part * POT_ROWS, POT_ROWS), POT_ROWS)] = (
+        first[pl.ds(pl.multiple_of(part * length, length), length)] = value[:length]
+        field[pl.ds(pl.multiple_of(part * POT_ROWS, POT_ROWS), POT_ROWS)] = LIFT * (
             2.0 * (value[length:] - CENTER) * (1.0 / HALF_WIDTH) + 6.0 * COEFFS[0] * SCALE
         )
 
-    def prepare(half, source):
-        value = source[half]
+    def step(source, target, opening):
+        value = source[...]
         upper = value.astype(jnp.bfloat16)
-        left[half, :, :cells] = upper
-        left[half, :, cells : 2 * cells] = (value - upper.astype(jnp.float32)).astype(jnp.bfloat16)
-        left[half, :, 2 * cells :] = upper
-
-    def multiply(half, lanes):
-        product[half, :, lanes] = jnp.dot(left[half], weights[:, lanes], preferred_element_type=jnp.float32)
-
-    def add_along_z(half, lanes, source, target, opening):
-        for lane in range(lanes.start, lanes.stop, 128):
-
-            def column(plane):
-                start = (plane % total) * ROWS
-                return half, slice(start, start + ROWS), slice(lane, lane + 128)
-
-            line = [source[column(plane)] for plane in range(total)]
-            for plane in range(total):
-                row = plane // planes * POT_ROWS + plane % planes
-                sum_ = product[column(plane)] + field[row : row + 1, lane : lane + 128] * line[plane]
-                for reach in range(1, 7):
-                    sum_ += (2.0 * SCALE * COEFFS[reach]) * (
-                        line[(plane + reach) % total] + line[(plane - reach) % total]
-                    )
-                target[column(plane)] = 0.5 * sum_ if opening else sum_ - target[column(plane)]
-
-    tiles = [slice(lane, lane + 256) for lane in range(0, cells, 256)]
-    prepare(0, first)
-    for lanes in tiles:
-        multiply(0, lanes)
-    prepare(1, first)
-    for degree in range(4):
-        source, target = (first, second) if degree % 2 == 0 else (second, first)
+        left[:, :cells] = upper
+        left[:, cells:] = (value - upper.astype(jnp.float32)).astype(jnp.bfloat16)
+        tiles = [slice(lane, lane + 256) for lane in range(0, cells, 256)]
         for lanes in tiles:
-            multiply(1, lanes)
-            add_along_z(0, lanes, source, target, degree == 0)
-        if degree < 3:
-            prepare(0, target)
-        for lanes in tiles:
-            if degree < 3:
-                multiply(0, lanes)
-            add_along_z(1, lanes, source, target, degree == 0)
-        if degree < 3:
-            prepare(1, target)
+            product[:, lanes] = jnp.dot(left[...], weights[:, lanes], preferred_element_type=jnp.float32)
+        for lane in range(0, cells, 128):
+            for offset in range(0, ORBITALS, ROWS):
+
+                def column(plane):
+                    start = (plane % total) * ORBITALS + offset
+                    return slice(start, start + ROWS), slice(lane, lane + 128)
+
+                line = [source[column(plane)] for plane in range(total)]
+                for plane in range(total):
+                    row = plane // planes * POT_ROWS + plane % planes
+                    sum_ = product[column(plane)] + field[row : row + 1, lane : lane + 128] * line[plane]
+                    for reach in range(1, 7):
+                        sum_ += (2.0 * LIFT * SCALE * COEFFS[reach]) * (
+                            line[(plane + reach) % total] + line[(plane - reach) % total]
+                        )
+                    if opening:
+                        target[column(plane)] = (0.5 / LIFT) * sum_
+                    else:
+                        target[column(plane)] = (1.0 / LIFT) * sum_ - target[column(plane)]
+
+    step(first, second, True)
+    step(second, first, False)
+    step(first, second, False)
+    step(second, first, False)
     for gap in range(domains):
-        for plane in range(planes):
-            row = pl.multiple_of(((place[0] ^ gap) * planes + plane) * ROWS, ROWS)
-            value = jnp.concatenate([first[half, pl.ds(row, ROWS)] for half in range(2)], axis=0)
-            outs[gap][plane * ORBITALS : (plane + 1) * ORBITALS] = power_code(value, 3)
+        start = pl.multiple_of((place[0] ^ gap) * length, length)
+        outs[gap][...] = power_code(first[pl.ds(start, length)], 3)
 
 
 def quarter_kernel(groups, planes, spot, *refs):
@@ -240,13 +222,14 @@
     lanes = outs[0].shape[1]
     for gap in range(groups):
         start = pl.multiple_of((spot[0] ^ gap) * lanes, lanes)
-        outs[gap][...] = total[:, pl.ds(start, lanes)]
+        value = total[:, pl.ds(start, lanes)]
+        outs[gap][...] = power_code(value, 2) if gap else value
 
 
 def finish_kernel(*refs):
     sum_ = refs[0][...]
     for part in refs[1:-1]:
-        sum_ += part[...]
+        sum_ += power_decode(part[...], 2)
     refs[-1][...] = sum_
 
 
@@ -264,14 +247,12 @@
 
 def transposed_shards(domains, groups, orbitals, potential):
     own, planes, cells = orbitals.shape
-    stencil = 2.0 * SCALE * plane_stencil()
-    high = stencil.astype(jnp.bfloat16)
-    low = (stencil - high.astype(np.float64)).astype(jnp.bfloat16)
-    weights = jnp.asarray(np.concatenate([high, high, low], axis=0))
+    stencil = (2.0 * LIFT * SCALE * plane_stencil()).astype(jnp.bfloat16)
+    weights = jnp.asarray(np.concatenate([stencil, stencil], axis=0))
     place = lax.axis_index("dom").astype(jnp.int32).reshape(1)
     spot = lax.axis_index("grp").astype(jnp.int32).reshape(1)
     length = planes * ORBITALS
-    half_rows = domains * planes * ROWS
+    rows = domains * length
     lanes = cells // groups
     orbs = own * groups
     columns = orbs // domains
@@ -292,6 +273,7 @@
             pltpu.SemaphoreType.DMA((planes + 1,)),
         ),
         flops=1 << 20,
+        grant=53 * 1024 * 1024,
     )(place, orbitals.transpose(1, 0, 2), potential)
     arrived = exchange(packed, "dom", order)
     order = [0] + order
@@ -301,16 +283,17 @@
         "s" + "v" * domains + "v",
         (
             pltpu.VMEM((domains * POT_ROWS, cells), jnp.float32),
-            pltpu.VMEM((2, half_rows, cells), jnp.float32),
-            pltpu.VMEM((2, half_rows, cells), jnp.float32),
-            pltpu.VMEM((2, half_rows, 3 * cells), jnp.bfloat16),
-            pltpu.VMEM((2, half_rows, cells), jnp.float32),
+            pltpu.VMEM((rows, cells), jnp.float32),
+            pltpu.VMEM((rows, cells), jnp.float32),
+            pltpu.VMEM((rows, 2 * cells), jnp.bfloat16),
+            pltpu.VMEM((rows, cells), jnp.float32),
         ),
-        flops=4 * 3 * 4 * half_rows * cells * cells,
+        flops=4 * 4 * rows * cells * cells,
     )(place, *[arrived[gap] for gap in order], weights)
     late = [gap for gap in order if hops(gap) == 1]
     early = [gap for gap in order if gap not in late]
-    coded = exchange(coded, "dom", early[1:] + late)
+    last = late[len(late) // 2 :]
+    coded = exchange(coded, "dom", early[1:] + late[: len(late) // 2])
     quarters = []
     for gaps in (early, late):
         quarter = whole_call(
@@ -322,7 +305,10 @@
         )(spot, *[coded[gap] for gap in gaps])
         if gaps is early:
             quarter = list(quarter)
-            quarter[0], coded[late[0]] = lax.optimization_barrier((quarter[0], coded[late[0]]))
+            held = lax.optimization_barrier((quarter[0], *[coded[gap] for gap in last]))
+            quarter[0] = held[0]
+            for gap, block in zip(last, held[1:]):
+                coded[gap] = swap(block, "dom", gap)
         quarter = exchange(quarter, "grp", along)
         quarters += [quarter[gap] for gap in [0] + along]
     filtered = whole_call(
@@ -349,7 +335,7 @@
     parts = [merged[0]] + [swap(merged[gap // 2], "dom", gap) for gap in order if gap and gap % 2 == 0]
     combined = whole_call(
         functools.partial(combine_kernel, groups),
-        arrays(groups, (columns, own), jnp.float32),
+        arrays(1, (columns, own), jnp.float32) + arrays(groups - 1, (columns, own), jnp.bfloat16),
         "s" + "v" * chips,
         (pltpu.VMEM((columns, orbs), jnp.float32),),
         flops=1 << 20,

time: 77.1 us -> 75.9 us (0.984)
  local copies, waits for them, and re-layouts: 2.12 us -> 0.71 us
  waiting for transfers between devices: 27.1 us -> 28.5 us
  starting transfers between devices: 31.5 us -> 30.6 us
    unnamed x6 -> x4, local copies, waits for them, and re-layouts: 2.12 us -> 0.71 us
    ppermute x27, waiting for transfers between devices: 27.1 us -> 28.5 us  [swap(): return lax.ppermute(block, axis, [(i, i ^ gap) for i in range(count)])]
    pallas_call x1, Pallas kernels: 10.6 us -> 9.33 us  [transposed_shards(): whole_call(functools.partial(filter_kernel, domains, planes, order), arra...]
    pallas_call x1, Pallas kernels: 0.63 us -> 1.57 us  [transposed_shards(): whole_call(functools.partial(pack_kernel, domains), arrays(domains, (leng...]
    ppermute x27, starting transfers between devices: 31.5 us -> 30.6 us  [swap(): return lax.ppermute(block, axis, [(i, i ^ gap) for i in range(count)])]
  transfers between devices with their start and end apart: 27 -> 27, of which waited for: 14 -> 15; matrix products, arithmetic and copies ran while one was open for 0% -> 0% of each run, Pallas kernels for 3% -> 3%
where the time goes in v1:
time: 75.9 us; the launch traced here: 75.6 us
  starting transfers between devices  30.6 us (40%)
  waiting for transfers between devices  28.5 us (38%)
  Pallas kernels  15 us (20%)
    ppermute x27, starting transfers between devices, swap(): return lax.ppermute(block, axis, [(i, i ^ gap) for i in range(count)])  30.6 us
    ppermute x27, waiting for transfers between devices, swap(): return lax.ppermute(block, axis, [(i, i ^ gap) for i in range(count)])  28.5 us
    pallas_call x1, Pallas kernels, transposed_shards(): whole_call(functools.partial(filter_kernel, domains, planes, order), arra...  9.33 us
    pallas_call x1, Pallas kernels, transposed_shards(): whole_call(functools.partial(pack_kernel, domains), arrays(domains, (leng...  1.57 us
    pallas_call x1, Pallas kernels, transposed_shards(): whole_call(functools.partial(write_kernel, planes, early + late), arrays(...  1.56 us
  transfers between devices with their start and end apart: 27, of which 15 were waited for; matrix products, arithmetic and copies ran while one was open for 0% of the time, Pallas kernels for 3%

profile of v1, /device:TPU:0, one launch (start us, length us, event | category | flops | bytes accessed | tf_op | source)
XLA Modules:
  0.0 75.6 jit_solution(13964210243378589387)
XLA Ops:
  0.6 0.7 copy-done
  1.4 1.6 %shard_map.50 = (bf16[104,512]{1,0:T(8,128)(2,1)S(1)}, bf16[104,512]{1,0:T(8,128)(2,1)S(1)}, bf16[104,512]{1,0:T(8,128)(2,1)S(1)}, bf16[104,512]{1,0:T(8,128)(2,...) custom-call(s32[1]{0:T(128)} %bitcast.place, ...), custom_call_target="tpu_custom_call" | custom-call | flops 1048576 | bytes 1048576 | tf_op jit(solution)/shard_map/pallas_call | solution.py:266
  2.9 4.0 %collective-permute-start = (bf16[104,512]{1,0:T(8,128)(2,1)S(1)}, bf16[104,512]{1,0:T(8,128)(2,1)S(1)}, u32[]{:S(2)}, u32[]{:S(2)}) collective-permute-start(bf16[104,512]{1,0:T(8,128)(2,1)S(1)} %get-tuple-element.42), channel_id=1, source_target_pairs={{0,24},{4,28},{8,16},{12,20},{16,8},{20,12},{24,0},{28,4},{1,25},{... | collective-permute-start | bytes 319496 | tf_op jit(solution)/shard_map/ppermute | solution.py:238
  6.9 0.0 collective-permute-start.1
  6.9 1.1 %collective-permute-start.2 = (bf16[104,512]{1,0:T(8,128)(2,1)S(1)}, bf16[104,512]{1,0:T(8,128)(2,1)S(1)}, u32[]{:S(2)}, u32[]{:S(2)}) collective-permute-start(bf16[104,512]{1,0:T(8,128)(2,1)S(1)} %get-tuple-element.44), channel_id=1, source_target_pairs={{0,8},{4,12},{8,0},{12,4},{16,24},{20,28},{24,16},{28,20},{1,9},{5... | collective-permute-start | bytes 319496 | tf_op jit(solution)/shard_map/ppermute | solution.py:238
  8.0 0.6 collective-permute-start.3
  8.6 1.7 %collective-permute-start.4 = (bf16[104,512]{1,0:T(8,128)(2,1)S(1)}, bf16[104,512]{1,0:T(8,128)(2,1)S(1)}, u32[]{:S(2)}, u32[]{:S(2)}) collective-permute-start(bf16[104,512]{1,0:T(8,128)(2,1)S(1)} %get-tuple-element.46), channel_id=1, source_target_pairs={{0,16},{4,20},{8,24},{12,28},{16,0},{20,4},{24,8},{28,12},{1,17},{... | collective-permute-start | bytes 319496 | tf_op jit(solution)/shard_map/ppermute | solution.py:238
  10.4 0.0 collective-permute-done.refs_1_
  10.4 0.0 collective-permute-start.5
  10.4 2.7 %collective-permute-done.1.refs_2_ = bf16[104,512]{1,0:T(8,128)(2,1)S(1)} collective-permute-done((bf16[104,512]{1,0:T(8,128)(2,1)S(1)}, bf16[104,512]{1,0:T(8,128)(2,1)S(1)}, u32[]{:S(2)}, u32[]{:S(2)}) %collective-permute-start.1) | collective-permute-done | bytes 106528 | tf_op jit(solution)/shard_map/ppermute | solution.py:238
  13.1 0.0 collective-permute-start.6
  13.1 1.9 %collective-permute-done.2.refs_3_ = bf16[104,512]{1,0:T(8,128)(2,1)S(1)} collective-permute-done((bf16[104,512]{1,0:T(8,128)(2,1)S(1)}, bf16[104,512]{1,0:T(8,128)(2,1)S(1)}, u32[]{:S(2)}, u32[]{:S(2)}) %collective-permute-start.2) | collective-permute-done | bytes 106528 | tf_op jit(solution)/shard_map/ppermute | solution.py:238
  15.0 1.7 %collective-permute-done.3.refs_4_ = bf16[104,512]{1,0:T(8,128)(2,1)S(1)} collective-permute-done((bf16[104,512]{1,0:T(8,128)(2,1)S(1)}, bf16[104,512]{1,0:T(8,128)(2,1)S(1)}, u32[]{:S(2)}, u32[]{:S(2)}) %collective-permute-start.3) | collective-permute-done | bytes 106528 | tf_op jit(solution)/shard_map/ppermute | solution.py:238
  16.6 0.0 collective-permute-done.4.refs_5_
  16.7 0.7 collective-permute-done.5.refs_6_
  17.3 0.0 collective-permute-done.6.refs_7_
  17.3 9.3 %shard_map.51 = (bf16[96,512]{1,0:T(8,128)(2,1)S(1)}, bf16[96,512]{1,0:T(8,128)(2,1)S(1)}, bf16[96,512]{1,0:T(8,128)(2,1)S(1)}, bf16[96,512]{1,0:T(8,128)(2,1)S(...) custom-call(s32[1]{0:T(128)} %bitcast.place, ...), custom_call_target="tpu_custom_call" | custom-call | flops 3221225472 | bytes 1048576 | tf_op jit(solution)/shard_map/pallas_call | solution.py:280
  26.7 1.7 %collective-permute-start.7 = (bf16[96,512]{1,0:T(8,128)(2,1)S(1)}, bf16[96,512]{1,0:T(8,128)(2,1)S(1)}, u32[]{:S(2)}, u32[]{:S(2)}) collective-permute-start(bf16[96,512]{1,0:T(8,128)(2,1)S(1)} %get-tuple-element.50), channel_id=1, source_target_pairs={{0,24},{4,28},{8,16},{12,20},{16,8},{20,12},{24,0},{28,4},{1,25},{... | collective-permute-start | bytes 294920 | tf_op jit(solution)/shard_map/ppermute | solution.py:238
  28.4 0.7 collective-permute-start.8
  29.1 0.7 collective-permute-start.9
  29.8 0.9 %collective-permute-start.10 = (bf16[96,512]{1,0:T(8,128)(2,1)S(1)}, bf16[96,512]{1,0:T(8,128)(2,1)S(1)}, u32[]{:S(2)}, u32[]{:S(2)}) collective-permute-start(bf16[96,512]{1,0:T(8,128)(2,1)S(1)} %get-tuple-element.53), channel_id=1, source_target_pairs={{0,8},{4,12},{8,0},{12,4},{16,24},{20,28},{24,16},{28,20},{1,9},{5... | collective-permute-start | bytes 294920 | tf_op jit(solution)/shard_map/ppermute | solution.py:238
  30.7 0.4 collective-permute-start.11
  31.1 1.5 %collective-permute-done.7.refs_1_ = bf16[96,512]{1,0:T(8,128)(2,1)S(1)} collective-permute-done((bf16[96,512]{1,0:T(8,128)(2,1)S(1)}, bf16[96,512]{1,0:T(8,128)(2,1)S(1)}, u32[]{:S(2)}, u32[]{:S(2)}) %collective-permute-start.7) | collective-permute-done | bytes 98336 | tf_op jit(solution)/shard_map/ppermute | solution.py:238
  32.6 1.8 %collective-permute-done.8.refs_2_ = bf16[96,512]{1,0:T(8,128)(2,1)S(1)} collective-permute-done((bf16[96,512]{1,0:T(8,128)(2,1)S(1)}, bf16[96,512]{1,0:T(8,128)(2,1)S(1)}, u32[]{:S(2)}, u32[]{:S(2)}) %collective-permute-start.8) | collective-permute-done | bytes 98336 | tf_op jit(solution)/shard_map/ppermute | solution.py:238
  34.4 0.0 collective-permute-done.9.refs_3_
  34.4 0.3 shard_map.52
  34.7 0.8 %collective-permute-start.12 = (bf16[96,512]{1,0:T(8,128)(2,1)S(1)}, bf16[96,512]{1,0:T(8,128)(2,1)S(1)}, u32[]{:S(2)}, u32[]{:S(2)}) collective-permute-start(bf16[96,512]{1,0:T(8,128)(2,1)S(1)} %get-tuple-element.58), channel_id=1, source_target_pairs={{0,16},{4,20},{8,24},{12,28},{16,0},{20,4},{24,8},{28,12},{1,17},{... | collective-permute-start | bytes 294920 | tf_op jit(solution)/shard_map/ppermute | solution.py:238
  35.5 0.8 %collective-permute-start.13 = (bf16[96,512]{1,0:T(8,128)(2,1)S(1)}, bf16[96,512]{1,0:T(8,128)(2,1)S(1)}, u32[]{:S(2)}, u32[]{:S(2)}) collective-permute-start(bf16[96,512]{1,0:T(8,128)(2,1)S(1)} %get-tuple-element.59), channel_id=1, source_target_pairs={{0,20},{4,16},{8,28},{12,24},{16,4},{20,0},{24,12},{28,8},{1,21},{... | collective-permute-start | bytes 294920 | tf_op jit(solution)/shard_map/ppermute | solution.py:238
  36.3 2.6 %collective-permute-start.14 = (bf16[6,64,128]{2,1,0:T(8,128)(2,1)S(1)}, bf16[6,64,128]{2,1,0:T(8,128)(2,1)S(1)}, u32[]{:S(2)}, u32[]{:S(2)}) collective-permute-start(bf16[6,64,128]{2,1,0:T(8,128)(2,1)S(1)} %get-tuple-element.63), channel_id=1, source_target_pairs={{0,2},{1,3},{2,0},{3,1},{4,6},{5,7},{6,4},{7,5},{8,10},{9,11},{10,... | collective-permute-start | bytes 294920 | tf_op jit(solution)/shard_map/ppermute | solution.py:238
  38.9 0.0 collective-permute-done.10.refs_4_.refs_0_
  38.9 1.4 %collective-permute-start.15 = (bf16[6,64,128]{2,1,0:T(8,128)(2,1)S(1)}, bf16[6,64,128]{2,1,0:T(8,128)(2,1)S(1)}, u32[]{:S(2)}, u32[]{:S(2)}) collective-permute-start(bf16[6,64,128]{2,1,0:T(8,128)(2,1)S(1)} %get-tuple-element.64), channel_id=1, source_target_pairs={{0,3},{1,2},{2,1},{3,0},{4,7},{5,6},{6,5},{7,4},{8,11},{9,10},{10,... | collective-permute-start | bytes 294920 | tf_op jit(solution)/shard_map/ppermute | solution.py:238
  40.2 0.0 collective-permute-done.11.refs_5_.refs_1_
  40.2 0.3 collective-permute-start.16
  40.5 0.0 collective-permute-done.12.refs_6_.refs_2_
  40.5 0.4 collective-permute-done.13.refs_7_.refs_3_
  40.9 0.3 shard_map.54
  41.2 2.7 %collective-permute-start.17 = (bf16[6,64,128]{2,1,0:T(8,128)(2,1)S(1)}, bf16[6,64,128]{2,1,0:T(8,128)(2,1)S(1)}, u32[]{:S(2)}, u32[]{:S(2)}) collective-permute-start(bf16[6,64,128]{2,1,0:T(8,128)(2,1)S(1)} %get-tuple-element.67), channel_id=1, source_target_pairs={{0,2},{1,3},{2,0},{3,1},{4,6},{5,7},{6,4},{7,5},{8,10},{9,11},{10,... | collective-permute-start | bytes 294920 | tf_op jit(solution)/shard_map/ppermute | solution.py:238
  43.9 1.4 %collective-permute-start.18 = (bf16[6,64,128]{2,1,0:T(8,128)(2,1)S(1)}, bf16[6,64,128]{2,1,0:T(8,128)(2,1)S(1)}, u32[]{:S(2)}, u32[]{:S(2)}) collective-permute-start(bf16[6,64,128]{2,1,0:T(8,128)(2,1)S(1)} %get-tuple-element.68), channel_id=1, source_target_pairs={{0,3},{1,2},{2,1},{3,0},{4,7},{5,6},{6,5},{7,4},{8,11},{9,10},{10,... | collective-permute-start | bytes 294920 | tf_op jit(solution)/shard_map/ppermute | solution.py:238
  45.3 1.8 %collective-permute-done.14.refs_1_ = bf16[6,64,128]{2,1,0:T(8,128)(2,1)S(1)} collective-permute-done((bf16[6,64,128]{2,1,0:T(8,128)(2,1)S(1)}, bf16[6,64,128]{2,1,0:T(8,128)(2,1)S(1)}, u32[]{:S(2)}, u32[]{:S(2)}) %collective-permute-start.14) | collective-permute-done | bytes 98336 | tf_op jit(solution)/shard_map/ppermute | solution.py:238
  47.1 0.5 collective-permute-start.19
  47.6 1.6 %shard_map.53 = f32[6,128,512]{2,1,0:T(8,128)} custom-call(s32[1]{0:T(128)} %bitcast.place, bf16[96,512]{1,0:T(8,128)(2,1)S(1)} %get-tuple-element.49.refs_0_, bf16[96,512]{1,0:T(8,128)(2,1)S(1)} %collective-permute-done.7.refs_1_, bf16[96,512]{1,0:T(8,128)(2,1)S(1)} %collective-permute-done.8.refs_2_, bf16[96,512]{1,0:T(8,128)(2,1)S(1)} %collective-permute-done.9.refs_3_, ...), custom_call_target="tpu_custom_call" | custom-call | flops 16777216 | bytes 1048576 | tf_op jit(solution)/shard_map/pallas_call | solution.py:314
  49.2 0.0 collective-permute-done.15.refs_2_
  49.2 0.0 collective-permute-done.16.refs_3_
  49.2 6.3 %collective-permute-done.17.refs_5_ = bf16[6,64,128]{2,1,0:T(8,128)(2,1)S(1)} collective-permute-done((bf16[6,64,128]{2,1,0:T(8,128)(2,1)S(1)}, bf16[6,64,128]{2,1,0:T(8,128)(2,1)S(1)}, u32[]{:S(2)}, u32[]{:S(2)}) %collective-permute-start.17) | collective-permute-done | bytes 98336 | tf_op jit(solution)/shard_map/ppermute | solution.py:238
  55.5 0.0 collective-permute-done.18.refs_6_
  55.5 0.0 collective-permute-done.19.refs_7_
  55.5 0.9 %shard_map.55 = (f32[256,512]{1,0:T(8,128)S(1)}, bf16[256,512]{1,0:T(8,128)(2,1)S(1)}) custom-call(s32[1]{0:T(128)} %bitcast.place, s32[1]{0:T(128)} %bitcast.2.spot, bf16[6,64,128]{2,1,0:T(8,128)(2,1)S(1)} %get-tuple-element.62.refs_0_, bf16[6,64,128]{2,1,0:T(8,128)(2,1)S(1)} %collective-permute-done.14.refs_1_, ...), custom_call_target="tpu_custom_call" | custom-call | flops 268435456 | bytes 1048576 | tf_op jit(solution)/shard_map/pallas_call | solution.py:321
  56.4 0.1 collective-permute-start.20
  56.5 1.5 %collective-permute-done.20.came = bf16[256,512]{1,0:T(8,128)(2,1)S(1)} collective-permute-done((bf16[256,512]{1,0:T(8,128)(2,1)S(1)}, bf16[256,512]{1,0:T(8,128)(2,1)S(1)}, u32[]{:S(2)}, u32[]{:S(2)}) %collective-permute-start.20) | collective-permute-done | bytes 262176 | tf_op jit(solution)/shard_map/ppermute | solution.py:238
  58.0 0.2 shard_map.56
  58.3 1.6 %collective-permute-start.21 = (bf16[64,512]{1,0:T(8,128)(2,1)S(1)}, bf16[64,512]{1,0:T(8,128)(2,1)S(1)}, u32[]{:S(2)}, u32[]{:S(2)}) collective-permute-start(bf16[64,512]{1,0:T(8,128)(2,1)S(1)} %get-tuple-element.73), channel_id=1, source_target_pairs={{0,24},{4,28},{8,16},{12,20},{16,8},{20,12},{24,0},{28,4},{1,25},{... | collective-permute-start | bytes 196616 | tf_op jit(solution)/shard_map/ppermute | solution.py:238
  59.9 1.0 %collective-permute-start.22 = (bf16[64,512]{1,0:T(8,128)(2,1)S(1)}, bf16[64,512]{1,0:T(8,128)(2,1)S(1)}, u32[]{:S(2)}, u32[]{:S(2)}) collective-permute-start(bf16[64,512]{1,0:T(8,128)(2,1)S(1)} %get-tuple-element.74), channel_id=1, source_target_pairs={{0,8},{4,12},{8,0},{12,4},{16,24},{20,28},{24,16},{28,20},{1,9},{5... | collective-permute-start | bytes 196616 | tf_op jit(solution)/shard_map/ppermute | solution.py:238
  60.9 0.9 %collective-permute-start.23 = (bf16[64,512]{1,0:T(8,128)(2,1)S(1)}, bf16[64,512]{1,0:T(8,128)(2,1)S(1)}, u32[]{:S(2)}, u32[]{:S(2)}) collective-permute-start(bf16[64,512]{1,0:T(8,128)(2,1)S(1)} %get-tuple-element.75), channel_id=1, source_target_pairs={{0,16},{4,20},{8,24},{12,28},{16,0},{20,4},{24,8},{28,12},{1,17},{... | collective-permute-start | bytes 196616 | tf_op jit(solution)/shard_map/ppermute | solution.py:238
  61.8 2.2 %collective-permute-done.21.refs_1_ = bf16[64,512]{1,0:T(8,128)(2,1)S(1)} collective-permute-done((bf16[64,512]{1,0:T(8,128)(2,1)S(1)}, bf16[64,512]{1,0:T(8,128)(2,1)S(1)}, u32[]{:S(2)}, u32[]{:S(2)}) %collective-permute-start.21) | collective-permute-done | bytes 65568 | tf_op jit(solution)/shard_map/ppermute | solution.py:238
  64.0 0.4 collective-permute-done.22.refs_2_
  64.4 0.8 collective-permute-done.23.refs_3_
  65.2 0.2 shard_map.57
  65.4 4.1 %collective-permute-start.24 = (bf16[64,128]{1,0:T(8,128)(2,1)S(1)}, bf16[64,128]{1,0:T(8,128)(2,1)S(1)}, u32[]{:S(2)}, u32[]{:S(2)}) collective-permute-start(bf16[64,128]{1,0:T(8,128)(2,1)S(1)} %get-tuple-element.77), channel_id=1, source_target_pairs={{0,2},{1,3},{2,0},{3,1},{4,6},{5,7},{6,4},{7,5},{8,10},{9,11},{10,... | collective-permute-start | bytes 49160 | tf_op jit(solution)/shard_map/ppermute | solution.py:238
  69.4 0.5 collective-permute-start.25
  69.9 0.2 collective-permute-start.26
  70.1 1.1 %collective-permute-done.24.refs_1_ = bf16[64,128]{1,0:T(8,128)(2,1)S(1)} collective-permute-done((bf16[64,128]{1,0:T(8,128)(2,1)S(1)}, bf16[64,128]{1,0:T(8,128)(2,1)S(1)}, u32[]{:S(2)}, u32[]{:S(2)}) %collective-permute-start.24) | collective-permute-done | bytes 16416 | tf_op jit(solution)/shard_map/ppermute | solution.py:238
  71.2 3.8 %collective-permute-done.25.refs_2_ = bf16[64,128]{1,0:T(8,128)(2,1)S(1)} collective-permute-done((bf16[64,128]{1,0:T(8,128)(2,1)S(1)}, bf16[64,128]{1,0:T(8,128)(2,1)S(1)}, u32[]{:S(2)}, u32[]{:S(2)}) %collective-permute-start.25) | collective-permute-done | bytes 16416 | tf_op jit(solution)/shard_map/ppermute | solution.py:238
  75.0 0.0 collective-permute-done.26.refs_3_
  75.0 0.7 shard_map.58
  (3 shorter events, 0.0 us)
Async XLA Ops:
  0.6 0.7 copy-start
  1.4 16.0 %copy-start.1 = (bf16[1024,512]{1,0:T(8,128)(2,1)S(1)}, bf16[1024,512]{1,0:T(8,128)(2,1)}, u32[]{:S(2)}) copy-start(bf16[1024,512]{1,0:T(8,128)(2,1)} %constant.11.clone.refs_8_) | copy-start | bytes 3145732
  2.9 7.4 %collective-permute-start = (bf16[104,512]{1,0:T(8,128)(2,1)S(1)}, bf16[104,512]{1,0:T(8,128)(2,1)S(1)}, u32[]{:S(2)}, u32[]{:S(2)}) collective-permute-start(bf16[104,512]{1,0:T(8,128)(2,1)S(1)} %get-tuple-element.42), channel_id=1, source_target_pairs={{0,24},{4,28},{8,16},{12,20},{16,8},{20,12},{24,0},{28,4},{1,25},{... | collective-permute-start | bytes 319496 | tf_op jit(solution)/shard_map/ppermute | solution.py:238
  6.9 6.2 %collective-permute-start.1 = (bf16[104,512]{1,0:T(8,128)(2,1)S(1)}, bf16[104,512]{1,0:T(8,128)(2,1)S(1)}, u32[]{:S(2)}, u32[]{:S(2)}) collective-permute-start(bf16[104,512]{1,0:T(8,128)(2,1)S(1)} %get-tuple-element.43), channel_id=1, source_target_pairs={{0,28},{4,24},{8,20},{12,16},{16,12},{20,8},{24,4},{28,0},{1,29},{... | collective-permute-start | bytes 319496 | tf_op jit(solution)/shard_map/ppermute | solution.py:238
  6.9 8.1 %collective-permute-start.2 = (bf16[104,512]{1,0:T(8,128)(2,1)S(1)}, bf16[104,512]{1,0:T(8,128)(2,1)S(1)}, u32[]{:S(2)}, u32[]{:S(2)}) collective-permute-start(bf16[104,512]{1,0:T(8,128)(2,1)S(1)} %get-tuple-element.44), channel_id=1, source_target_pairs={{0,8},{4,12},{8,0},{12,4},{16,24},{20,28},{24,16},{28,20},{1,9},{5... | collective-permute-start | bytes 319496 | tf_op jit(solution)/shard_map/ppermute | solution.py:238
  8.0 8.6 %collective-permute-start.3 = (bf16[104,512]{1,0:T(8,128)(2,1)S(1)}, bf16[104,512]{1,0:T(8,128)(2,1)S(1)}, u32[]{:S(2)}, u32[]{:S(2)}) collective-permute-start(bf16[104,512]{1,0:T(8,128)(2,1)S(1)} %get-tuple-element.45), channel_id=1, source_target_pairs={{0,12},{4,8},{8,4},{12,0},{16,28},{20,24},{24,20},{28,16},{1,13},{... | collective-permute-start | bytes 319496 | tf_op jit(solution)/shard_map/ppermute | solution.py:238
  8.6 8.0 %collective-permute-start.4 = (bf16[104,512]{1,0:T(8,128)(2,1)S(1)}, bf16[104,512]{1,0:T(8,128)(2,1)S(1)}, u32[]{:S(2)}, u32[]{:S(2)}) collective-permute-start(bf16[104,512]{1,0:T(8,128)(2,1)S(1)} %get-tuple-element.46), channel_id=1, source_target_pairs={{0,16},{4,20},{8,24},{12,28},{16,0},{20,4},{24,8},{28,12},{1,17},{... | collective-permute-start | bytes 319496 | tf_op jit(solution)/shard_map/ppermute | solution.py:238
  10.4 7.0 %collective-permute-start.5 = (bf16[104,512]{1,0:T(8,128)(2,1)S(1)}, bf16[104,512]{1,0:T(8,128)(2,1)S(1)}, u32[]{:S(2)}, u32[]{:S(2)}) collective-permute-start(bf16[104,512]{1,0:T(8,128)(2,1)S(1)} %get-tuple-element.47), channel_id=1, source_target_pairs={{0,20},{4,16},{8,28},{12,24},{16,4},{20,0},{24,12},{28,8},{1,21},{... | collective-permute-start | bytes 319496 | tf_op jit(solution)/shard_map/ppermute | solution.py:238
  13.1 4.3 %collective-permute-start.6 = (bf16[104,512]{1,0:T(8,128)(2,1)S(1)}, bf16[104,512]{1,0:T(8,128)(2,1)S(1)}, u32[]{:S(2)}, u32[]{:S(2)}) collective-permute-start(bf16[104,512]{1,0:T(8,128)(2,1)S(1)} %get-tuple-element.48), channel_id=1, source_target_pairs={{0,4},{4,0},{8,12},{12,8},{16,20},{20,16},{24,28},{28,24},{1,5},{5... | collective-permute-start | bytes 319496 | tf_op jit(solution)/shard_map/ppermute | solution.py:238
  26.7 5.9 %collective-permute-start.7 = (bf16[96,512]{1,0:T(8,128)(2,1)S(1)}, bf16[96,512]{1,0:T(8,128)(2,1)S(1)}, u32[]{:S(2)}, u32[]{:S(2)}) collective-permute-start(bf16[96,512]{1,0:T(8,128)(2,1)S(1)} %get-tuple-element.50), channel_id=1, source_target_pairs={{0,24},{4,28},{8,16},{12,20},{16,8},{20,12},{24,0},{28,4},{1,25},{... | collective-permute-start | bytes 294920 | tf_op jit(solution)/shard_map/ppermute | solution.py:238
  28.4 6.0 %collective-permute-start.8 = (bf16[96,512]{1,0:T(8,128)(2,1)S(1)}, bf16[96,512]{1,0:T(8,128)(2,1)S(1)}, u32[]{:S(2)}, u32[]{:S(2)}) collective-permute-start(bf16[96,512]{1,0:T(8,128)(2,1)S(1)} %get-tuple-element.51), channel_id=1, source_target_pairs={{0,28},{4,24},{8,20},{12,16},{16,12},{20,8},{24,4},{28,0},{1,29},{... | collective-permute-start | bytes 294920 | tf_op jit(solution)/shard_map/ppermute | solution.py:238
  29.1 5.3 %collective-permute-start.9 = (bf16[96,512]{1,0:T(8,128)(2,1)S(1)}, bf16[96,512]{1,0:T(8,128)(2,1)S(1)}, u32[]{:S(2)}, u32[]{:S(2)}) collective-permute-start(bf16[96,512]{1,0:T(8,128)(2,1)S(1)} %get-tuple-element.52), channel_id=1, source_target_pairs={{0,4},{4,0},{8,12},{12,8},{16,20},{20,16},{24,28},{28,24},{1,5},{5... | collective-permute-start | bytes 294920 | tf_op jit(solution)/shard_map/ppermute | solution.py:238
  29.8 9.1 %collective-permute-start.10 = (bf16[96,512]{1,0:T(8,128)(2,1)S(1)}, bf16[96,512]{1,0:T(8,128)(2,1)S(1)}, u32[]{:S(2)}, u32[]{:S(2)}) collective-permute-start(bf16[96,512]{1,0:T(8,128)(2,1)S(1)} %get-tuple-element.53), channel_id=1, source_target_pairs={{0,8},{4,12},{8,0},{12,4},{16,24},{20,28},{24,16},{28,20},{1,9},{5... | collective-permute-start | bytes 294920 | tf_op jit(solution)/shard_map/ppermute | solution.py:238
  30.7 9.5 %collective-permute-start.11 = (bf16[96,512]{1,0:T(8,128)(2,1)S(1)}, bf16[96,512]{1,0:T(8,128)(2,1)S(1)}, u32[]{:S(2)}, u32[]{:S(2)}) collective-permute-start(bf16[96,512]{1,0:T(8,128)(2,1)S(1)} %get-tuple-element.54), channel_id=1, source_target_pairs={{0,12},{4,8},{8,4},{12,0},{16,28},{20,24},{24,20},{28,16},{1,13},{... | collective-permute-start | bytes 294920 | tf_op jit(solution)/shard_map/ppermute | solution.py:238
  34.7 5.8 %collective-permute-start.12 = (bf16[96,512]{1,0:T(8,128)(2,1)S(1)}, bf16[96,512]{1,0:T(8,128)(2,1)S(1)}, u32[]{:S(2)}, u32[]{:S(2)}) collective-permute-start(bf16[96,512]{1,0:T(8,128)(2,1)S(1)} %get-tuple-element.58), channel_id=1, source_target_pairs={{0,16},{4,20},{8,24},{12,28},{16,0},{20,4},{24,8},{28,12},{1,17},{... | collective-permute-start | bytes 294920 | tf_op jit(solution)/shard_map/ppermute | solution.py:238
  35.5 5.4 %collective-permute-start.13 = (bf16[96,512]{1,0:T(8,128)(2,1)S(1)}, bf16[96,512]{1,0:T(8,128)(2,1)S(1)}, u32[]{:S(2)}, u32[]{:S(2)}) collective-permute-start(bf16[96,512]{1,0:T(8,128)(2,1)S(1)} %get-tuple-element.59), channel_id=1, source_target_pairs={{0,20},{4,16},{8,28},{12,24},{16,4},{20,0},{24,12},{28,8},{1,21},{... | collective-permute-start | bytes 294920 | tf_op jit(solution)/shard_map/ppermute | solution.py:238
  36.3 10.8 %collective-permute-start.14 = (bf16[6,64,128]{2,1,0:T(8,128)(2,1)S(1)}, bf16[6,64,128]{2,1,0:T(8,128)(2,1)S(1)}, u32[]{:S(2)}, u32[]{:S(2)}) collective-permute-start(bf16[6,64,128]{2,1,0:T(8,128)(2,1)S(1)} %get-tuple-element.63), channel_id=1, source_target_pairs={{0,2},{1,3},{2,0},{3,1},{4,6},{5,7},{6,4},{7,5},{8,10},{9,11},{10,... | collective-permute-start | bytes 294920 | tf_op jit(solution)/shard_map/ppermute | solution.py:238
  38.9 10.3 %collective-permute-start.15 = (bf16[6,64,128]{2,1,0:T(8,128)(2,1)S(1)}, bf16[6,64,128]{2,1,0:T(8,128)(2,1)S(1)}, u32[]{:S(2)}, u32[]{:S(2)}) collective-permute-start(bf16[6,64,128]{2,1,0:T(8,128)(2,1)S(1)} %get-tuple-element.64), channel_id=1, source_target_pairs={{0,3},{1,2},{2,1},{3,0},{4,7},{5,6},{6,5},{7,4},{8,11},{9,10},{10,... | collective-permute-start | bytes 294920 | tf_op jit(solution)/shard_map/ppermute | solution.py:238
  40.2 9.0 %collective-permute-start.16 = (bf16[6,64,128]{2,1,0:T(8,128)(2,1)S(1)}, bf16[6,64,128]{2,1,0:T(8,128)(2,1)S(1)}, u32[]{:S(2)}, u32[]{:S(2)}) collective-permute-start(bf16[6,64,128]{2,1,0:T(8,128)(2,1)S(1)} %get-tuple-element.65), channel_id=1, source_target_pairs={{0,1},{1,0},{2,3},{3,2},{4,5},{5,4},{6,7},{7,6},{8,9},{9,8},{10,11... | collective-permute-start | bytes 294920 | tf_op jit(solution)/shard_map/ppermute | solution.py:238
  41.2 14.3 %collective-permute-start.17 = (bf16[6,64,128]{2,1,0:T(8,128)(2,1)S(1)}, bf16[6,64,128]{2,1,0:T(8,128)(2,1)S(1)}, u32[]{:S(2)}, u32[]{:S(2)}) collective-permute-start(bf16[6,64,128]{2,1,0:T(8,128)(2,1)S(1)} %get-tuple-element.67), channel_id=1, source_target_pairs={{0,2},{1,3},{2,0},{3,1},{4,6},{5,7},{6,4},{7,5},{8,10},{9,11},{10,... | collective-permute-start | bytes 294920 | tf_op jit(solution)/shard_map/ppermute | solution.py:238
  43.9 11.6 %collective-permute-start.18 = (bf16[6,64,128]{2,1,0:T(8,128)(2,1)S(1)}, bf16[6,64,128]{2,1,0:T(8,128)(2,1)S(1)}, u32[]{:S(2)}, u32[]{:S(2)}) collective-permute-start(bf16[6,64,128]{2,1,0:T(8,128)(2,1)S(1)} %get-tuple-element.68), channel_id=1, source_target_pairs={{0,3},{1,2},{2,1},{3,0},{4,7},{5,6},{6,5},{7,4},{8,11},{9,10},{10,... | collective-permute-start | bytes 294920 | tf_op jit(solution)/shard_map/ppermute | solution.py:238
  47.1 8.4 %collective-permute-start.19 = (bf16[6,64,128]{2,1,0:T(8,128)(2,1)S(1)}, bf16[6,64,128]{2,1,0:T(8,128)(2,1)S(1)}, u32[]{:S(2)}, u32[]{:S(2)}) collective-permute-start(bf16[6,64,128]{2,1,0:T(8,128)(2,1)S(1)} %get-tuple-element.69), channel_id=1, source_target_pairs={{0,1},{1,0},{2,3},{3,2},{4,5},{5,4},{6,7},{7,6},{8,9},{9,8},{10,11... | collective-permute-start | bytes 294920 | tf_op jit(solution)/shard_map/ppermute | solution.py:238
  56.4 1.6 %collective-permute-start.20 = (bf16[256,512]{1,0:T(8,128)(2,1)S(1)}, bf16[256,512]{1,0:T(8,128)(2,1)S(1)}, u32[]{:S(2)}, u32[]{:S(2)}) collective-permute-start(bf16[256,512]{1,0:T(8,128)(2,1)S(1)} %get-tuple-element.71), channel_id=1, source_target_pairs={{0,4},{4,0},{8,12},{12,8},{16,20},{20,16},{24,28},{28,24},{1,5},{5... | collective-permute-start | bytes 786440 | tf_op jit(solution)/shard_map/ppermute | solution.py:238
  58.3 5.8 %collective-permute-start.21 = (bf16[64,512]{1,0:T(8,128)(2,1)S(1)}, bf16[64,512]{1,0:T(8,128)(2,1)S(1)}, u32[]{:S(2)}, u32[]{:S(2)}) collective-permute-start(bf16[64,512]{1,0:T(8,128)(2,1)S(1)} %get-tuple-element.73), channel_id=1, source_target_pairs={{0,24},{4,28},{8,16},{12,20},{16,8},{20,12},{24,0},{28,4},{1,25},{... | collective-permute-start | bytes 196616 | tf_op jit(solution)/shard_map/ppermute | solution.py:238
  59.9 4.6 %collective-permute-start.22 = (bf16[64,512]{1,0:T(8,128)(2,1)S(1)}, bf16[64,512]{1,0:T(8,128)(2,1)S(1)}, u32[]{:S(2)}, u32[]{:S(2)}) collective-permute-start(bf16[64,512]{1,0:T(8,128)(2,1)S(1)} %get-tuple-element.74), channel_id=1, source_target_pairs={{0,8},{4,12},{8,0},{12,4},{16,24},{20,28},{24,16},{28,20},{1,9},{5... | collective-permute-start | bytes 196616 | tf_op jit(solution)/shard_map/ppermute | solution.py:238
  60.9 4.3 %collective-permute-start.23 = (bf16[64,512]{1,0:T(8,128)(2,1)S(1)}, bf16[64,512]{1,0:T(8,128)(2,1)S(1)}, u32[]{:S(2)}, u32[]{:S(2)}) collective-permute-start(bf16[64,512]{1,0:T(8,128)(2,1)S(1)} %get-tuple-element.75), channel_id=1, source_target_pairs={{0,16},{4,20},{8,24},{12,28},{16,0},{20,4},{24,8},{28,12},{1,17},{... | collective-permute-start | bytes 196616 | tf_op jit(solution)/shard_map/ppermute | solution.py:238
  65.4 5.8 %collective-permute-start.24 = (bf16[64,128]{1,0:T(8,128)(2,1)S(1)}, bf16[64,128]{1,0:T(8,128)(2,1)S(1)}, u32[]{:S(2)}, u32[]{:S(2)}) collective-permute-start(bf16[64,128]{1,0:T(8,128)(2,1)S(1)} %get-tuple-element.77), channel_id=1, source_target_pairs={{0,2},{1,3},{2,0},{3,1},{4,6},{5,7},{6,4},{7,5},{8,10},{9,11},{10,... | collective-permute-start | bytes 49160 | tf_op jit(solution)/shard_map/ppermute | solution.py:238
  69.4 5.5 %collective-permute-start.25 = (bf16[64,128]{1,0:T(8,128)(2,1)S(1)}, bf16[64,128]{1,0:T(8,128)(2,1)S(1)}, u32[]{:S(2)}, u32[]{:S(2)}) collective-permute-start(bf16[64,128]{1,0:T(8,128)(2,1)S(1)} %get-tuple-element.78), channel_id=1, source_target_pairs={{0,3},{1,2},{2,1},{3,0},{4,7},{5,6},{6,5},{7,4},{8,11},{9,10},{10,... | collective-permute-start | bytes 49160 | tf_op jit(solution)/shard_map/ppermute | solution.py:238
  69.9 5.1 %collective-permute-start.26 = (bf16[64,128]{1,0:T(8,128)(2,1)S(1)}, bf16[64,128]{1,0:T(8,128)(2,1)S(1)}, u32[]{:S(2)}, u32[]{:S(2)}) collective-permute-start(bf16[64,128]{1,0:T(8,128)(2,1)S(1)} %get-tuple-element.79), channel_id=1, source_target_pairs={{0,1},{1,0},{2,3},{3,2},{4,5},{5,4},{6,7},{7,6},{8,9},{9,8},{10,11... | collective-permute-start | bytes 49160 | tf_op jit(solution)/shard_map/ppermute | solution.py:238

commit v2 on v1

--- a/solution.py
+++ b/solution.py
@@ -120,38 +120,44 @@
             2.0 * (value[length:] - CENTER) * (1.0 / HALF_WIDTH) + 6.0 * COEFFS[0] * SCALE
         )
 
-    def step(source, target, opening):
-        value = source[...]
+    def split(turn, rows, lanes, value):
         upper = value.astype(jnp.bfloat16)
-        left[:, :cells] = upper
-        left[:, cells:] = (value - upper.astype(jnp.float32)).astype(jnp.bfloat16)
-        tiles = [slice(lane, lane + 256) for lane in range(0, cells, 256)]
-        for lanes in tiles:
-            product[:, lanes] = jnp.dot(left[...], weights[:, lanes], preferred_element_type=jnp.float32)
+        left[turn, rows, lanes] = upper
+        lower = slice(cells + lanes.start, cells + lanes.stop)
+        left[turn, rows, lower] = (value - upper.astype(jnp.float32)).astype(jnp.bfloat16)
+
+    def step(degree, source, target):
+        turn = degree % 2
+        for lane in range(0, cells, 256):
+            lanes = slice(lane, lane + 256)
+            product[:, lanes] = jnp.dot(left[turn], weights[:, lanes], preferred_element_type=jnp.float32)
         for lane in range(0, cells, 128):
-            for offset in range(0, ORBITALS, ROWS):
-
-                def column(plane):
-                    start = (plane % total) * ORBITALS + offset
-                    return slice(start, start + ROWS), slice(lane, lane + 128)
-
-                line = [source[column(plane)] for plane in range(total)]
-                for plane in range(total):
-                    row = plane // planes * POT_ROWS + plane % planes
-                    sum_ = product[column(plane)] + field[row : row + 1, lane : lane + 128] * line[plane]
-                    for reach in range(1, 7):
-                        sum_ += (2.0 * LIFT * SCALE * COEFFS[reach]) * (
-                            line[(plane + reach) % total] + line[(plane - reach) % total]
-                        )
-                    if opening:
-                        target[column(plane)] = (0.5 / LIFT) * sum_
-                    else:
-                        target[column(plane)] = (1.0 / LIFT) * sum_ - target[column(plane)]
-
-    step(first, second, True)
-    step(second, first, False)
-    step(first, second, False)
-    step(second, first, False)
+            lanes = slice(lane, lane + 128)
+
+            def rows(plane):
+                start = (plane % total) * ORBITALS
+                return slice(start, start + ORBITALS)
+
+            line = [source[rows(plane), lanes] for plane in range(-6, 6)]
+            for plane in range(total):
+                line = line[-12:] + [source[rows(plane + 6), lanes]]
+                row = plane // planes * POT_ROWS + plane % planes
+                sum_ = product[rows(plane), lanes] + field[row : row + 1, lanes] * line[6]
+                for reach in range(1, 7):
+                    sum_ += (2.0 * LIFT * SCALE * COEFFS[reach]) * (line[6 + reach] + line[6 - reach])
+                if degree == 0:
+                    value = (0.5 / LIFT) * sum_
+                else:
+                    value = (1.0 / LIFT) * sum_ - target[rows(plane), lanes]
+                target[rows(plane), lanes] = value
+                if degree < 3:
+                    split(1 - turn, rows(plane), lanes, value)
+
+    split(0, slice(0, total * ORBITALS), slice(0, cells), first[...])
+    step(0, first, second)
+    step(1, second, first)
+    step(2, first, second)
+    step(3, second, first)
     for gap in range(domains):
         start = pl.multiple_of((place[0] ^ gap) * length, length)
         outs[gap][...] = power_code(first[pl.ds(start, length)], 3)
@@ -256,8 +262,7 @@
     lanes = cells // groups
     orbs = own * groups
     columns = orbs // domains
-    hops = lambda gap: bin(gap >> 1).count("1")
-    order = sorted(range(1, domains), key=lambda gap: (-hops(gap), gap))
+    order = [2 * (chip ^ (chip >> 1)) + core for chip in range(domains // 2) for core in range(2)][1:]
     along = sorted(range(1, groups), key=lambda gap: (-(gap >> 1), gap))
 
     def arrays(count, shape, dtype):
@@ -285,15 +290,13 @@
             pltpu.VMEM((domains * POT_ROWS, cells), jnp.float32),
             pltpu.VMEM((rows, cells), jnp.float32),
             pltpu.VMEM((rows, cells), jnp.float32),
-            pltpu.VMEM((rows, 2 * cells), jnp.bfloat16),
+            pltpu.VMEM((2, rows, 2 * cells), jnp.bfloat16),
             pltpu.VMEM((rows, cells), jnp.float32),
         ),
         flops=4 * 4 * rows * cells * cells,
     )(place, *[arrived[gap] for gap in order], weights)
-    late = [gap for gap in order if hops(gap) == 1]
-    early = [gap for gap in order if gap not in late]
-    last = late[len(late) // 2 :]
-    coded = exchange(coded, "dom", early[1:] + late[: len(late) // 2])
+    early, late = order[: domains // 2], order[domains // 2 :]
+    coded = exchange(coded, "dom", early[1:] + late)
     quarters = []
     for gaps in (early, late):
         quarter = whole_call(
@@ -305,10 +308,7 @@
         )(spot, *[coded[gap] for gap in gaps])
         if gaps is early:
             quarter = list(quarter)
-            held = lax.optimization_barrier((quarter[0], *[coded[gap] for gap in last]))
-            quarter[0] = held[0]
-            for gap, block in zip(last, held[1:]):
-                coded[gap] = swap(block, "dom", gap)
+            quarter[0], coded[late[0]] = lax.optimization_barrier((quarter[0], coded[late[0]]))
         quarter = exchange(quarter, "grp", along)
         quarters += [quarter[gap] for gap in [0] + along]
     filtered = whole_call(

time: 75.9 us -> 79.1 us (1.042)
  starting transfers between devices: 30.6 us -> 32.4 us
  Pallas kernels: 15 us -> 15.8 us
    ppermute x27, starting transfers between devices: 30.6 us -> 32.4 us  [swap(): return lax.ppermute(block, axis, [(i, i ^ gap) for i in range(count)])]
  transfers between devices with their start and end apart: 27 -> 27, of which waited for: 15 -> 16; matrix products, arithmetic and copies ran while one was open for 0% -> 0% of each run, Pallas kernels for 3% -> 3%
where the time goes in v2:
time: 79.1 us; the launch traced here: 78.9 us
  starting transfers between devices  32.4 us (41%)
  waiting for transfers between devices  29.2 us (37%)
  Pallas kernels  15.8 us (20%)
    ppermute x27, starting transfers between devices, swap(): return lax.ppermute(block, axis, [(i, i ^ gap) for i in range(count)])  32.4 us
    ppermute x27, waiting for transfers between devices, swap(): return lax.ppermute(block, axis, [(i, i ^ gap) for i in range(count)])  29.2 us
    pallas_call x1, Pallas kernels, transposed_shards(): whole_call(functools.partial(filter_kernel, domains, planes, order), arra...  9.92 us
  transfers between devices with their start and end apart: 27, of which 16 were waited for; matrix products, arithmetic and copies ran while one was open for 0% of the time, Pallas kernels for 3%

profile of v2, /device:TPU:0, one launch (start us, length us, event | category | flops | bytes accessed | tf_op | source)
XLA Modules:
  0.0 78.9 jit_solution(10184931491420317987)
XLA Ops:
  0.6 0.7 copy-done
  1.4 1.6 %shard_map.50 = (bf16[104,512]{1,0:T(8,128)(2,1)S(1)}, bf16[104,512]{1,0:T(8,128)(2,1)S(1)}, bf16[104,512]{1,0:T(8,128)(2,1)S(1)}, bf16[104,512]{1,0:T(8,128)(2,...) custom-call(s32[1]{0:T(128)} %bitcast.place, ...), custom_call_target="tpu_custom_call" | custom-call | flops 1048576 | bytes 1048576 | tf_op jit(solution)/shard_map/pallas_call | solution.py:271
  2.9 0.5 collective-permute-start
  3.5 2.6 %collective-permute-start.1 = (bf16[104,512]{1,0:T(8,128)(2,1)S(1)}, bf16[104,512]{1,0:T(8,128)(2,1)S(1)}, u32[]{:S(2)}, u32[]{:S(2)}) collective-permute-start(bf16[104,512]{1,0:T(8,128)(2,1)S(1)} %get-tuple-element.42), channel_id=1, source_target_pairs={{0,8},{4,12},{8,0},{12,4},{16,24},{20,28},{24,16},{28,20},{1,9},{5... | collective-permute-start | bytes 319496 | tf_op jit(solution)/shard_map/ppermute | solution.py:244
  6.0 0.1 collective-permute-start.2
  6.1 2.7 %collective-permute-start.3 = (bf16[104,512]{1,0:T(8,128)(2,1)S(1)}, bf16[104,512]{1,0:T(8,128)(2,1)S(1)}, u32[]{:S(2)}, u32[]{:S(2)}) collective-permute-start(bf16[104,512]{1,0:T(8,128)(2,1)S(1)} %get-tuple-element.44), channel_id=1, source_target_pairs={{0,24},{4,28},{8,16},{12,20},{16,8},{20,12},{24,0},{28,4},{1,25},{... | collective-permute-start | bytes 319496 | tf_op jit(solution)/shard_map/ppermute | solution.py:244
  8.8 0.0 collective-permute-start.4
  8.8 0.0 collective-permute-done.refs_1_
  8.8 1.7 %collective-permute-start.5 = (bf16[104,512]{1,0:T(8,128)(2,1)S(1)}, bf16[104,512]{1,0:T(8,128)(2,1)S(1)}, u32[]{:S(2)}, u32[]{:S(2)}) collective-permute-start(bf16[104,512]{1,0:T(8,128)(2,1)S(1)} %get-tuple-element.46), channel_id=1, source_target_pairs={{0,16},{4,20},{8,24},{12,28},{16,0},{20,4},{24,8},{28,12},{1,17},{... | collective-permute-start | bytes 319496 | tf_op jit(solution)/shard_map/ppermute | solution.py:244
  10.4 0.0 collective-permute-done.1.refs_2_
  10.4 0.2 collective-permute-start.6
  10.6 1.0 %collective-permute-done.2.refs_3_ = bf16[104,512]{1,0:T(8,128)(2,1)S(1)} collective-permute-done((bf16[104,512]{1,0:T(8,128)(2,1)S(1)}, bf16[104,512]{1,0:T(8,128)(2,1)S(1)}, u32[]{:S(2)}, u32[]{:S(2)}) %collective-permute-start.2) | collective-permute-done | bytes 106528 | tf_op jit(solution)/shard_map/ppermute | solution.py:244
  11.6 4.3 %collective-permute-done.3.refs_4_ = bf16[104,512]{1,0:T(8,128)(2,1)S(1)} collective-permute-done((bf16[104,512]{1,0:T(8,128)(2,1)S(1)}, bf16[104,512]{1,0:T(8,128)(2,1)S(1)}, u32[]{:S(2)}, u32[]{:S(2)}) %collective-permute-start.3) | collective-permute-done | bytes 106528 | tf_op jit(solution)/shard_map/ppermute | solution.py:244
  15.9 1.4 %collective-permute-done.4.refs_5_ = bf16[104,512]{1,0:T(8,128)(2,1)S(1)} collective-permute-done((bf16[104,512]{1,0:T(8,128)(2,1)S(1)}, bf16[104,512]{1,0:T(8,128)(2,1)S(1)}, u32[]{:S(2)}, u32[]{:S(2)}) %collective-permute-start.4) | collective-permute-done | bytes 106528 | tf_op jit(solution)/shard_map/ppermute | solution.py:244
  17.3 1.8 %collective-permute-done.5.refs_6_ = bf16[104,512]{1,0:T(8,128)(2,1)S(1)} collective-permute-done((bf16[104,512]{1,0:T(8,128)(2,1)S(1)}, bf16[104,512]{1,0:T(8,128)(2,1)S(1)}, u32[]{:S(2)}, u32[]{:S(2)}) %collective-permute-start.5) | collective-permute-done | bytes 106528 | tf_op jit(solution)/shard_map/ppermute | solution.py:244
  19.1 1.2 %collective-permute-done.6.refs_7_ = bf16[104,512]{1,0:T(8,128)(2,1)S(1)} collective-permute-done((bf16[104,512]{1,0:T(8,128)(2,1)S(1)}, bf16[104,512]{1,0:T(8,128)(2,1)S(1)}, u32[]{:S(2)}, u32[]{:S(2)}) %collective-permute-start.6) | collective-permute-done | bytes 106528 | tf_op jit(solution)/shard_map/ppermute | solution.py:244
  20.3 9.9 %shard_map.51 = (bf16[96,512]{1,0:T(8,128)(2,1)S(1)}, bf16[96,512]{1,0:T(8,128)(2,1)S(1)}, bf16[96,512]{1,0:T(8,128)(2,1)S(1)}, bf16[96,512]{1,0:T(8,128)(2,1)S(...) custom-call(s32[1]{0:T(128)} %bitcast.place, ...), custom_call_target="tpu_custom_call" | custom-call | flops 3221225472 | bytes 1048576 | tf_op jit(solution)/shard_map/pallas_call | solution.py:285
  30.2 0.4 collective-permute-start.7
  30.7 1.7 %collective-permute-start.8 = (bf16[96,512]{1,0:T(8,128)(2,1)S(1)}, bf16[96,512]{1,0:T(8,128)(2,1)S(1)}, u32[]{:S(2)}, u32[]{:S(2)}) collective-permute-start(bf16[96,512]{1,0:T(8,128)(2,1)S(1)} %get-tuple-element.50), channel_id=1, source_target_pairs={{0,8},{4,12},{8,0},{12,4},{16,24},{20,28},{24,16},{28,20},{1,9},{5... | collective-permute-start | bytes 294920 | tf_op jit(solution)/shard_map/ppermute | solution.py:244
  32.4 0.0 collective-permute-start.9
  32.4 2.6 %collective-permute-start.10 = (bf16[96,512]{1,0:T(8,128)(2,1)S(1)}, bf16[96,512]{1,0:T(8,128)(2,1)S(1)}, u32[]{:S(2)}, u32[]{:S(2)}) collective-permute-start(bf16[96,512]{1,0:T(8,128)(2,1)S(1)} %get-tuple-element.53), channel_id=1, source_target_pairs={{0,24},{4,28},{8,16},{12,20},{16,8},{20,12},{24,0},{28,4},{1,25},{... | collective-permute-start | bytes 294920 | tf_op jit(solution)/shard_map/ppermute | solution.py:244
  35.0 0.1 collective-permute-start.11
  35.1 0.0 collective-permute-done.7.refs_1_
  35.1 1.7 %collective-permute-start.12 = (bf16[96,512]{1,0:T(8,128)(2,1)S(1)}, bf16[96,512]{1,0:T(8,128)(2,1)S(1)}, u32[]{:S(2)}, u32[]{:S(2)}) collective-permute-start(bf16[96,512]{1,0:T(8,128)(2,1)S(1)} %get-tuple-element.56), channel_id=1, source_target_pairs={{0,16},{4,20},{8,24},{12,28},{16,0},{20,4},{24,8},{28,12},{1,17},{... | collective-permute-start | bytes 294920 | tf_op jit(solution)/shard_map/ppermute | solution.py:244
  36.8 0.0 collective-permute-done.8.refs_2_
  36.8 0.1 collective-permute-start.13
  36.9 0.8 collective-permute-done.9.refs_3_
  37.7 0.3 shard_map.52
  38.0 2.7 %collective-permute-start.14 = (bf16[6,64,128]{2,1,0:T(8,128)(2,1)S(1)}, bf16[6,64,128]{2,1,0:T(8,128)(2,1)S(1)}, u32[]{:S(2)}, u32[]{:S(2)}) collective-permute-start(bf16[6,64,128]{2,1,0:T(8,128)(2,1)S(1)} %get-tuple-element.61), channel_id=1, source_target_pairs={{0,2},{1,3},{2,0},{3,1},{4,6},{5,7},{6,4},{7,5},{8,10},{9,11},{10,... | collective-permute-start | bytes 294920 | tf_op jit(solution)/shard_map/ppermute | solution.py:244
  40.6 1.1 %collective-permute-done.10.refs_4_.refs_0_ = bf16[96,512]{1,0:T(8,128)(2,1)S(1)} collective-permute-done((bf16[96,512]{1,0:T(8,128)(2,1)S(1)}, bf16[96,512]{1,0:T(8,128)(2,1)S(1)}, u32[]{:S(2)}, u32[]{:S(2)}) %collective-permute-start.10) | collective-permute-done | bytes 98336 | tf_op jit(solution)/shard_map/ppermute | solution.py:244
  41.7 3.5 %collective-permute-start.15 = (bf16[6,64,128]{2,1,0:T(8,128)(2,1)S(1)}, bf16[6,64,128]{2,1,0:T(8,128)(2,1)S(1)}, u32[]{:S(2)}, u32[]{:S(2)}) collective-permute-start(bf16[6,64,128]{2,1,0:T(8,128)(2,1)S(1)} %get-tuple-element.62), channel_id=1, source_target_pairs={{0,3},{1,2},{2,1},{3,0},{4,7},{5,6},{6,5},{7,4},{8,11},{9,10},{10,... | collective-permute-start | bytes 294920 | tf_op jit(solution)/shard_map/ppermute | solution.py:244
  45.2 0.0 collective-permute-done.11.refs_5_.refs_1_
  45.3 0.0 collective-permute-start.16
  45.3 0.0 collective-permute-done.12.refs_6_.refs_2_
  45.3 0.7 collective-permute-done.13.refs_7_.refs_3_
  46.0 0.5 shard_map.54
  46.5 2.7 %collective-permute-start.17 = (bf16[6,64,128]{2,1,0:T(8,128)(2,1)S(1)}, bf16[6,64,128]{2,1,0:T(8,128)(2,1)S(1)}, u32[]{:S(2)}, u32[]{:S(2)}) collective-permute-start(bf16[6,64,128]{2,1,0:T(8,128)(2,1)S(1)} %get-tuple-element.65), channel_id=1, source_target_pairs={{0,2},{1,3},{2,0},{3,1},{4,6},{5,7},{6,4},{7,5},{8,10},{9,11},{10,... | collective-permute-start | bytes 294920 | tf_op jit(solution)/shard_map/ppermute | solution.py:244
  49.2 1.4 %collective-permute-start.18 = (bf16[6,64,128]{2,1,0:T(8,128)(2,1)S(1)}, bf16[6,64,128]{2,1,0:T(8,128)(2,1)S(1)}, u32[]{:S(2)}, u32[]{:S(2)}) collective-permute-start(bf16[6,64,128]{2,1,0:T(8,128)(2,1)S(1)} %get-tuple-element.66), channel_id=1, source_target_pairs={{0,3},{1,2},{2,1},{3,0},{4,7},{5,6},{6,5},{7,4},{8,11},{9,10},{10,... | collective-permute-start | bytes 294920 | tf_op jit(solution)/shard_map/ppermute | solution.py:244
  50.6 0.0 collective-permute-done.14.refs_1_
  50.6 0.2 collective-permute-start.19
  50.8 1.6 %shard_map.53 = f32[6,128,512]{2,1,0:T(8,128)} custom-call(s32[1]{0:T(128)} %bitcast.place, bf16[96,512]{1,0:T(8,128)(2,1)S(1)} %get-tuple-element.48.refs_0_, bf16[96,512]{1,0:T(8,128)(2,1)S(1)} %collective-permute-done.7.refs_1_, bf16[96,512]{1,0:T(8,128)(2,1)S(1)} %collective-permute-done.8.refs_2_, bf16[96,512]{1,0:T(8,128)(2,1)S(1)} %collective-permute-done.9.refs_3_, ...), custom_call_target="tpu_custom_call" | custom-call | flops 16777216 | bytes 1048576 | tf_op jit(solution)/shard_map/pallas_call | solution.py:314
  52.4 0.0 collective-permute-done.15.refs_2_
  52.4 0.0 collective-permute-done.16.refs_3_
  52.4 5.0 %collective-permute-done.17.refs_5_ = bf16[6,64,128]{2,1,0:T(8,128)(2,1)S(1)} collective-permute-done((bf16[6,64,128]{2,1,0:T(8,128)(2,1)S(1)}, bf16[6,64,128]{2,1,0:T(8,128)(2,1)S(1)}, u32[]{:S(2)}, u32[]{:S(2)}) %collective-permute-start.17) | collective-permute-done | bytes 98336 | tf_op jit(solution)/shard_map/ppermute | solution.py:244
  57.4 0.0 collective-permute-done.18.refs_6_
  57.4 1.1 %collective-permute-done.19.refs_7_ = bf16[6,64,128]{2,1,0:T(8,128)(2,1)S(1)} collective-permute-done((bf16[6,64,128]{2,1,0:T(8,128)(2,1)S(1)}, bf16[6,64,128]{2,1,0:T(8,128)(2,1)S(1)}, u32[]{:S(2)}, u32[]{:S(2)}) %collective-permute-start.19) | collective-permute-done | bytes 98336 | tf_op jit(solution)/shard_map/ppermute | solution.py:244
  58.5 0.9 %shard_map.55 = (f32[256,512]{1,0:T(8,128)S(1)}, bf16[256,512]{1,0:T(8,128)(2,1)S(1)}) custom-call(s32[1]{0:T(128)} %bitcast.place, s32[1]{0:T(128)} %bitcast.2.spot, bf16[6,64,128]{2,1,0:T(8,128)(2,1)S(1)} %get-tuple-element.60.refs_0_, bf16[6,64,128]{2,1,0:T(8,128)(2,1)S(1)} %collective-permute-done.14.refs_1_, ...), custom_call_target="tpu_custom_call" | custom-call | flops 268435456 | bytes 1048576 | tf_op jit(solution)/shard_map/pallas_call | solution.py:321
  59.3 0.1 collective-permute-start.20
  59.4 1.5 %collective-permute-done.20.came = bf16[256,512]{1,0:T(8,128)(2,1)S(1)} collective-permute-done((bf16[256,512]{1,0:T(8,128)(2,1)S(1)}, bf16[256,512]{1,0:T(8,128)(2,1)S(1)}, u32[]{:S(2)}, u32[]{:S(2)}) %collective-permute-start.20) | collective-permute-done | bytes 262176 | tf_op jit(solution)/shard_map/ppermute | solution.py:244
  60.9 0.2 shard_map.56
  61.2 1.6 %collective-permute-start.21 = (bf16[64,512]{1,0:T(8,128)(2,1)S(1)}, bf16[64,512]{1,0:T(8,128)(2,1)S(1)}, u32[]{:S(2)}, u32[]{:S(2)}) collective-permute-start(bf16[64,512]{1,0:T(8,128)(2,1)S(1)} %get-tuple-element.71), channel_id=1, source_target_pairs={{0,8},{4,12},{8,0},{12,4},{16,24},{20,28},{24,16},{28,20},{1,9},{5... | collective-permute-start | bytes 196616 | tf_op jit(solution)/shard_map/ppermute | solution.py:244
  62.8 1.7 %collective-permute-start.22 = (bf16[64,512]{1,0:T(8,128)(2,1)S(1)}, bf16[64,512]{1,0:T(8,128)(2,1)S(1)}, u32[]{:S(2)}, u32[]{:S(2)}) collective-permute-start(bf16[64,512]{1,0:T(8,128)(2,1)S(1)} %get-tuple-element.72), channel_id=1, source_target_pairs={{0,24},{4,28},{8,16},{12,20},{16,8},{20,12},{24,0},{28,4},{1,25},{... | collective-permute-start | bytes 196616 | tf_op jit(solution)/shard_map/ppermute | solution.py:244
  64.5 0.3 collective-permute-start.23
  64.7 0.8 collective-permute-done.21.refs_1_
  65.5 2.7 %collective-permute-done.22.refs_2_ = bf16[64,512]{1,0:T(8,128)(2,1)S(1)} collective-permute-done((bf16[64,512]{1,0:T(8,128)(2,1)S(1)}, bf16[64,512]{1,0:T(8,128)(2,1)S(1)}, u32[]{:S(2)}, u32[]{:S(2)}) %collective-permute-start.22) | collective-permute-done | bytes 65568 | tf_op jit(solution)/shard_map/ppermute | solution.py:244
  68.2 1.0 %collective-permute-done.23.refs_3_ = bf16[64,512]{1,0:T(8,128)(2,1)S(1)} collective-permute-done((bf16[64,512]{1,0:T(8,128)(2,1)S(1)}, bf16[64,512]{1,0:T(8,128)(2,1)S(1)}, u32[]{:S(2)}, u32[]{:S(2)}) %collective-permute-start.23) | collective-permute-done | bytes 65568 | tf_op jit(solution)/shard_map/ppermute | solution.py:244
  69.2 0.2 shard_map.57
  69.4 3.3 %collective-permute-start.24 = (bf16[64,128]{1,0:T(8,128)(2,1)S(1)}, bf16[64,128]{1,0:T(8,128)(2,1)S(1)}, u32[]{:S(2)}, u32[]{:S(2)}) collective-permute-start(bf16[64,128]{1,0:T(8,128)(2,1)S(1)} %get-tuple-element.75), channel_id=1, source_target_pairs={{0,2},{1,3},{2,0},{3,1},{4,6},{5,7},{6,4},{7,5},{8,10},{9,11},{10,... | collective-permute-start | bytes 49160 | tf_op jit(solution)/shard_map/ppermute | solution.py:244
  72.7 0.5 collective-permute-start.25
  73.1 0.2 collective-permute-start.26
  73.3 1.1 %collective-permute-done.24.refs_1_ = bf16[64,128]{1,0:T(8,128)(2,1)S(1)} collective-permute-done((bf16[64,128]{1,0:T(8,128)(2,1)S(1)}, bf16[64,128]{1,0:T(8,128)(2,1)S(1)}, u32[]{:S(2)}, u32[]{:S(2)}) %collective-permute-start.24) | collective-permute-done | bytes 16416 | tf_op jit(solution)/shard_map/ppermute | solution.py:244
  74.4 3.8 %collective-permute-done.25.refs_2_ = bf16[64,128]{1,0:T(8,128)(2,1)S(1)} collective-permute-done((bf16[64,128]{1,0:T(8,128)(2,1)S(1)}, bf16[64,128]{1,0:T(8,128)(2,1)S(1)}, u32[]{:S(2)}, u32[]{:S(2)}) %collective-permute-start.25) | collective-permute-done | bytes 16416 | tf_op jit(solution)/shard_map/ppermute | solution.py:244
  78.2 0.0 collective-permute-done.26.refs_3_
  78.2 0.7 shard_map.58
  (3 shorter events, 0.0 us)
Async XLA Ops:
  0.6 0.7 copy-start
  1.4 19.0 %copy-start.1 = (bf16[1024,512]{1,0:T(8,128)(2,1)S(1)}, bf16[1024,512]{1,0:T(8,128)(2,1)}, u32[]{:S(2)}) copy-start(bf16[1024,512]{1,0:T(8,128)(2,1)} %constant.11.clone.refs_8_) | copy-start | bytes 3145732
  2.9 5.9 %collective-permute-start = (bf16[104,512]{1,0:T(8,128)(2,1)S(1)}, bf16[104,512]{1,0:T(8,128)(2,1)S(1)}, u32[]{:S(2)}, u32[]{:S(2)}) collective-permute-start(bf16[104,512]{1,0:T(8,128)(2,1)S(1)} %get-tuple-element.41), channel_id=1, source_target_pairs={{0,4},{4,0},{8,12},{12,8},{16,20},{20,16},{24,28},{28,24},{1,5},{5... | collective-permute-start | bytes 319496 | tf_op jit(solution)/shard_map/ppermute | solution.py:244
  3.5 7.0 %collective-permute-start.1 = (bf16[104,512]{1,0:T(8,128)(2,1)S(1)}, bf16[104,512]{1,0:T(8,128)(2,1)S(1)}, u32[]{:S(2)}, u32[]{:S(2)}) collective-permute-start(bf16[104,512]{1,0:T(8,128)(2,1)S(1)} %get-tuple-element.42), channel_id=1, source_target_pairs={{0,8},{4,12},{8,0},{12,4},{16,24},{20,28},{24,16},{28,20},{1,9},{5... | collective-permute-start | bytes 319496 | tf_op jit(solution)/shard_map/ppermute | solution.py:244
  6.0 5.6 %collective-permute-start.2 = (bf16[104,512]{1,0:T(8,128)(2,1)S(1)}, bf16[104,512]{1,0:T(8,128)(2,1)S(1)}, u32[]{:S(2)}, u32[]{:S(2)}) collective-permute-start(bf16[104,512]{1,0:T(8,128)(2,1)S(1)} %get-tuple-element.43), channel_id=1, source_target_pairs={{0,12},{4,8},{8,4},{12,0},{16,28},{20,24},{24,20},{28,16},{1,13},{... | collective-permute-start | bytes 319496 | tf_op jit(solution)/shard_map/ppermute | solution.py:244
  6.1 9.8 %collective-permute-start.3 = (bf16[104,512]{1,0:T(8,128)(2,1)S(1)}, bf16[104,512]{1,0:T(8,128)(2,1)S(1)}, u32[]{:S(2)}, u32[]{:S(2)}) collective-permute-start(bf16[104,512]{1,0:T(8,128)(2,1)S(1)} %get-tuple-element.44), channel_id=1, source_target_pairs={{0,24},{4,28},{8,16},{12,20},{16,8},{20,12},{24,0},{28,4},{1,25},{... | collective-permute-start | bytes 319496 | tf_op jit(solution)/shard_map/ppermute | solution.py:244
  8.8 8.5 %collective-permute-start.4 = (bf16[104,512]{1,0:T(8,128)(2,1)S(1)}, bf16[104,512]{1,0:T(8,128)(2,1)S(1)}, u32[]{:S(2)}, u32[]{:S(2)}) collective-permute-start(bf16[104,512]{1,0:T(8,128)(2,1)S(1)} %get-tuple-element.45), channel_id=1, source_target_pairs={{0,28},{4,24},{8,20},{12,16},{16,12},{20,8},{24,4},{28,0},{1,29},{... | collective-permute-start | bytes 319496 | tf_op jit(solution)/shard_map/ppermute | solution.py:244
  8.8 10.4 %collective-permute-start.5 = (bf16[104,512]{1,0:T(8,128)(2,1)S(1)}, bf16[104,512]{1,0:T(8,128)(2,1)S(1)}, u32[]{:S(2)}, u32[]{:S(2)}) collective-permute-start(bf16[104,512]{1,0:T(8,128)(2,1)S(1)} %get-tuple-element.46), channel_id=1, source_target_pairs={{0,16},{4,20},{8,24},{12,28},{16,0},{20,4},{24,8},{28,12},{1,17},{... | collective-permute-start | bytes 319496 | tf_op jit(solution)/shard_map/ppermute | solution.py:244
  10.4 9.9 %collective-permute-start.6 = (bf16[104,512]{1,0:T(8,128)(2,1)S(1)}, bf16[104,512]{1,0:T(8,128)(2,1)S(1)}, u32[]{:S(2)}, u32[]{:S(2)}) collective-permute-start(bf16[104,512]{1,0:T(8,128)(2,1)S(1)} %get-tuple-element.47), channel_id=1, source_target_pairs={{0,20},{4,16},{8,28},{12,24},{16,4},{20,0},{24,12},{28,8},{1,21},{... | collective-permute-start | bytes 319496 | tf_op jit(solution)/shard_map/ppermute | solution.py:244
  30.2 4.9 %collective-permute-start.7 = (bf16[96,512]{1,0:T(8,128)(2,1)S(1)}, bf16[96,512]{1,0:T(8,128)(2,1)S(1)}, u32[]{:S(2)}, u32[]{:S(2)}) collective-permute-start(bf16[96,512]{1,0:T(8,128)(2,1)S(1)} %get-tuple-element.49), channel_id=1, source_target_pairs={{0,4},{4,0},{8,12},{12,8},{16,20},{20,16},{24,28},{28,24},{1,5},{5... | collective-permute-start | bytes 294920 | tf_op jit(solution)/shard_map/ppermute | solution.py:244
  30.7 6.1 %collective-permute-start.8 = (bf16[96,512]{1,0:T(8,128)(2,1)S(1)}, bf16[96,512]{1,0:T(8,128)(2,1)S(1)}, u32[]{:S(2)}, u32[]{:S(2)}) collective-permute-start(bf16[96,512]{1,0:T(8,128)(2,1)S(1)} %get-tuple-element.50), channel_id=1, source_target_pairs={{0,8},{4,12},{8,0},{12,4},{16,24},{20,28},{24,16},{28,20},{1,9},{5... | collective-permute-start | bytes 294920 | tf_op jit(solution)/shard_map/ppermute | solution.py:244
  32.4 5.3 %collective-permute-start.9 = (bf16[96,512]{1,0:T(8,128)(2,1)S(1)}, bf16[96,512]{1,0:T(8,128)(2,1)S(1)}, u32[]{:S(2)}, u32[]{:S(2)}) collective-permute-start(bf16[96,512]{1,0:T(8,128)(2,1)S(1)} %get-tuple-element.51), channel_id=1, source_target_pairs={{0,12},{4,8},{8,4},{12,0},{16,28},{20,24},{24,20},{28,16},{1,13},{... | collective-permute-start | bytes 294920 | tf_op jit(solution)/shard_map/ppermute | solution.py:244
  32.4 9.3 %collective-permute-start.10 = (bf16[96,512]{1,0:T(8,128)(2,1)S(1)}, bf16[96,512]{1,0:T(8,128)(2,1)S(1)}, u32[]{:S(2)}, u32[]{:S(2)}) collective-permute-start(bf16[96,512]{1,0:T(8,128)(2,1)S(1)} %get-tuple-element.53), channel_id=1, source_target_pairs={{0,24},{4,28},{8,16},{12,20},{16,8},{20,12},{24,0},{28,4},{1,25},{... | collective-permute-start | bytes 294920 | tf_op jit(solution)/shard_map/ppermute | solution.py:244
  35.0 10.2 %collective-permute-start.11 = (bf16[96,512]{1,0:T(8,128)(2,1)S(1)}, bf16[96,512]{1,0:T(8,128)(2,1)S(1)}, u32[]{:S(2)}, u32[]{:S(2)}) collective-permute-start(bf16[96,512]{1,0:T(8,128)(2,1)S(1)} %get-tuple-element.55), channel_id=1, source_target_pairs={{0,28},{4,24},{8,20},{12,16},{16,12},{20,8},{24,4},{28,0},{1,29},{... | collective-permute-start | bytes 294920 | tf_op jit(solution)/shard_map/ppermute | solution.py:244
  35.1 10.2 %collective-permute-start.12 = (bf16[96,512]{1,0:T(8,128)(2,1)S(1)}, bf16[96,512]{1,0:T(8,128)(2,1)S(1)}, u32[]{:S(2)}, u32[]{:S(2)}) collective-permute-start(bf16[96,512]{1,0:T(8,128)(2,1)S(1)} %get-tuple-element.56), channel_id=1, source_target_pairs={{0,16},{4,20},{8,24},{12,28},{16,0},{20,4},{24,8},{28,12},{1,17},{... | collective-permute-start | bytes 294920 | tf_op jit(solution)/shard_map/ppermute | solution.py:244
  36.8 9.2 %collective-permute-start.13 = (bf16[96,512]{1,0:T(8,128)(2,1)S(1)}, bf16[96,512]{1,0:T(8,128)(2,1)S(1)}, u32[]{:S(2)}, u32[]{:S(2)}) collective-permute-start(bf16[96,512]{1,0:T(8,128)(2,1)S(1)} %get-tuple-element.57), channel_id=1, source_target_pairs={{0,20},{4,16},{8,28},{12,24},{16,4},{20,0},{24,12},{28,8},{1,21},{... | collective-permute-start | bytes 294920 | tf_op jit(solution)/shard_map/ppermute | solution.py:244
  38.0 12.6 %collective-permute-start.14 = (bf16[6,64,128]{2,1,0:T(8,128)(2,1)S(1)}, bf16[6,64,128]{2,1,0:T(8,128)(2,1)S(1)}, u32[]{:S(2)}, u32[]{:S(2)}) collective-permute-start(bf16[6,64,128]{2,1,0:T(8,128)(2,1)S(1)} %get-tuple-element.61), channel_id=1, source_target_pairs={{0,2},{1,3},{2,0},{3,1},{4,6},{5,7},{6,4},{7,5},{8,10},{9,11},{10,... | collective-permute-start | bytes 294920 | tf_op jit(solution)/shard_map/ppermute | solution.py:244
  41.7 10.6 %collective-permute-start.15 = (bf16[6,64,128]{2,1,0:T(8,128)(2,1)S(1)}, bf16[6,64,128]{2,1,0:T(8,128)(2,1)S(1)}, u32[]{:S(2)}, u32[]{:S(2)}) collective-permute-start(bf16[6,64,128]{2,1,0:T(8,128)(2,1)S(1)} %get-tuple-element.62), channel_id=1, source_target_pairs={{0,3},{1,2},{2,1},{3,0},{4,7},{5,6},{6,5},{7,4},{8,11},{9,10},{10,... | collective-permute-start | bytes 294920 | tf_op jit(solution)/shard_map/ppermute | solution.py:244
  45.3 7.1 %collective-permute-start.16 = (bf16[6,64,128]{2,1,0:T(8,128)(2,1)S(1)}, bf16[6,64,128]{2,1,0:T(8,128)(2,1)S(1)}, u32[]{:S(2)}, u32[]{:S(2)}) collective-permute-start(bf16[6,64,128]{2,1,0:T(8,128)(2,1)S(1)} %get-tuple-element.63), channel_id=1, source_target_pairs={{0,1},{1,0},{2,3},{3,2},{4,5},{5,4},{6,7},{7,6},{8,9},{9,8},{10,11... | collective-permute-start | bytes 294920 | tf_op jit(solution)/shard_map/ppermute | solution.py:244
  46.5 10.9 %collective-permute-start.17 = (bf16[6,64,128]{2,1,0:T(8,128)(2,1)S(1)}, bf16[6,64,128]{2,1,0:T(8,128)(2,1)S(1)}, u32[]{:S(2)}, u32[]{:S(2)}) collective-permute-start(bf16[6,64,128]{2,1,0:T(8,128)(2,1)S(1)} %get-tuple-element.65), channel_id=1, source_target_pairs={{0,2},{1,3},{2,0},{3,1},{4,6},{5,7},{6,4},{7,5},{8,10},{9,11},{10,... | collective-permute-start | bytes 294920 | tf_op jit(solution)/shard_map/ppermute | solution.py:244
  49.2 8.2 %collective-permute-start.18 = (bf16[6,64,128]{2,1,0:T(8,128)(2,1)S(1)}, bf16[6,64,128]{2,1,0:T(8,128)(2,1)S(1)}, u32[]{:S(2)}, u32[]{:S(2)}) collective-permute-start(bf16[6,64,128]{2,1,0:T(8,128)(2,1)S(1)} %get-tuple-element.66), channel_id=1, source_target_pairs={{0,3},{1,2},{2,1},{3,0},{4,7},{5,6},{6,5},{7,4},{8,11},{9,10},{10,... | collective-permute-start | bytes 294920 | tf_op jit(solution)/shard_map/ppermute | solution.py:244
  50.6 7.9 %collective-permute-start.19 = (bf16[6,64,128]{2,1,0:T(8,128)(2,1)S(1)}, bf16[6,64,128]{2,1,0:T(8,128)(2,1)S(1)}, u32[]{:S(2)}, u32[]{:S(2)}) collective-permute-start(bf16[6,64,128]{2,1,0:T(8,128)(2,1)S(1)} %get-tuple-element.67), channel_id=1, source_target_pairs={{0,1},{1,0},{2,3},{3,2},{4,5},{5,4},{6,7},{7,6},{8,9},{9,8},{10,11... | collective-permute-start | bytes 294920 | tf_op jit(solution)/shard_map/ppermute | solution.py:244
  59.3 1.6 %collective-permute-start.20 = (bf16[256,512]{1,0:T(8,128)(2,1)S(1)}, bf16[256,512]{1,0:T(8,128)(2,1)S(1)}, u32[]{:S(2)}, u32[]{:S(2)}) collective-permute-start(bf16[256,512]{1,0:T(8,128)(2,1)S(1)} %get-tuple-element.69), channel_id=1, source_target_pairs={{0,4},{4,0},{8,12},{12,8},{16,20},{20,16},{24,28},{28,24},{1,5},{5... | collective-permute-start | bytes 786440 | tf_op jit(solution)/shard_map/ppermute | solution.py:244
  61.2 4.3 %collective-permute-start.21 = (bf16[64,512]{1,0:T(8,128)(2,1)S(1)}, bf16[64,512]{1,0:T(8,128)(2,1)S(1)}, u32[]{:S(2)}, u32[]{:S(2)}) collective-permute-start(bf16[64,512]{1,0:T(8,128)(2,1)S(1)} %get-tuple-element.71), channel_id=1, source_target_pairs={{0,8},{4,12},{8,0},{12,4},{16,24},{20,28},{24,16},{28,20},{1,9},{5... | collective-permute-start | bytes 196616 | tf_op jit(solution)/shard_map/ppermute | solution.py:244
  62.8 5.4 %collective-permute-start.22 = (bf16[64,512]{1,0:T(8,128)(2,1)S(1)}, bf16[64,512]{1,0:T(8,128)(2,1)S(1)}, u32[]{:S(2)}, u32[]{:S(2)}) collective-permute-start(bf16[64,512]{1,0:T(8,128)(2,1)S(1)} %get-tuple-element.72), channel_id=1, source_target_pairs={{0,24},{4,28},{8,16},{12,20},{16,8},{20,12},{24,0},{28,4},{1,25},{... | collective-permute-start | bytes 196616 | tf_op jit(solution)/shard_map/ppermute | solution.py:244
  64.5 4.7 %collective-permute-start.23 = (bf16[64,512]{1,0:T(8,128)(2,1)S(1)}, bf16[64,512]{1,0:T(8,128)(2,1)S(1)}, u32[]{:S(2)}, u32[]{:S(2)}) collective-permute-start(bf16[64,512]{1,0:T(8,128)(2,1)S(1)} %get-tuple-element.73), channel_id=1, source_target_pairs={{0,16},{4,20},{8,24},{12,28},{16,0},{20,4},{24,8},{28,12},{1,17},{... | collective-permute-start | bytes 196616 | tf_op jit(solution)/shard_map/ppermute | solution.py:244
  69.4 5.0 %collective-permute-start.24 = (bf16[64,128]{1,0:T(8,128)(2,1)S(1)}, bf16[64,128]{1,0:T(8,128)(2,1)S(1)}, u32[]{:S(2)}, u32[]{:S(2)}) collective-permute-start(bf16[64,128]{1,0:T(8,128)(2,1)S(1)} %get-tuple-element.75), channel_id=1, source_target_pairs={{0,2},{1,3},{2,0},{3,1},{4,6},{5,7},{6,4},{7,5},{8,10},{9,11},{10,... | collective-permute-start | bytes 49160 | tf_op jit(solution)/shard_map/ppermute | solution.py:244
  72.7 5.5 %collective-permute-start.25 = (bf16[64,128]{1,0:T(8,128)(2,1)S(1)}, bf16[64,128]{1,0:T(8,128)(2,1)S(1)}, u32[]{:S(2)}, u32[]{:S(2)}) collective-permute-start(bf16[64,128]{1,0:T(8,128)(2,1)S(1)} %get-tuple-element.76), channel_id=1, source_target_pairs={{0,3},{1,2},{2,1},{3,0},{4,7},{5,6},{6,5},{7,4},{8,11},{9,10},{10,... | collective-permute-start | bytes 49160 | tf_op jit(solution)/shard_map/ppermute | solution.py:244
  73.1 5.1 %collective-permute-start.26 = (bf16[64,128]{1,0:T(8,128)(2,1)S(1)}, bf16[64,128]{1,0:T(8,128)(2,1)S(1)}, u32[]{:S(2)}, u32[]{:S(2)}) collective-permute-start(bf16[64,128]{1,0:T(8,128)(2,1)S(1)} %get-tuple-element.77), channel_id=1, source_target_pairs={{0,1},{1,0},{2,3},{3,2},{4,5},{5,4},{6,7},{7,6},{8,9},{9,8},{10,11... | collective-permute-start | bytes 49160 | tf_op jit(solution)/shard_map/ppermute | solution.py:244

commit v3 on v1

--- a/solution.py
+++ b/solution.py
@@ -213,24 +213,25 @@
         out[...] = power_code(value, 2) if index else value
 
 
-def combine_kernel(groups, spot, *refs):
-    parts, outs, total = refs[: -groups - 1], refs[-groups - 1 : -1], refs[-1]
+def combine_kernel(kept_gaps, sent_gaps, spot, *refs):
+    parts, (kept, sent, total) = refs[:-3], refs[-3:]
     sum_ = parts[0][...]
     for part in parts[1:]:
         sum_ += power_decode(part[...], 2)
     total[...] = sum_
-    lanes = outs[0].shape[1]
-    for gap in range(groups):
-        start = pl.multiple_of((spot[0] ^ gap) * lanes, lanes)
-        value = total[:, pl.ds(start, lanes)]
-        outs[gap][...] = power_code(value, 2) if gap else value
-
-
-def finish_kernel(*refs):
-    sum_ = refs[0][...]
-    for part in refs[1:-1]:
-        sum_ += power_decode(part[...], 2)
-    refs[-1][...] = sum_
+    lanes = kept.shape[1] // len(kept_gaps)
+    for slot, (near, far) in enumerate(zip(kept_gaps, sent_gaps)):
+        columns = slice(slot * lanes, (slot + 1) * lanes)
+        kept[:, columns] = total[:, pl.ds(pl.multiple_of((spot[0] ^ near) * lanes, lanes), lanes)]
+        sent[:, columns] = power_code(total[:, pl.ds(pl.multiple_of((spot[0] ^ far) * lanes, lanes), lanes)], 2)
+
+
+def halve_kernel(kept, came, *outs):
+    width = outs[0].shape[1]
+    value = kept[...] + power_decode(came[...], 2)
+    outs[0][...] = value[:, :width]
+    if len(outs) > 1:
+        outs[1][...] = power_code(value[:, width:], 2)
 
 
 def swap(block, axis, gap):
@@ -292,8 +293,7 @@
     )(place, *[arrived[gap] for gap in order], weights)
     late = [gap for gap in order if hops(gap) == 1]
     early = [gap for gap in order if gap not in late]
-    last = late[len(late) // 2 :]
-    coded = exchange(coded, "dom", early[1:] + late[: len(late) // 2])
+    coded = exchange(coded, "dom", early[1:] + late)
     quarters = []
     for gaps in (early, late):
         quarter = whole_call(
@@ -305,10 +305,7 @@
         )(spot, *[coded[gap] for gap in gaps])
         if gaps is early:
             quarter = list(quarter)
-            held = lax.optimization_barrier((quarter[0], *[coded[gap] for gap in last]))
-            quarter[0] = held[0]
-            for gap, block in zip(last, held[1:]):
-                coded[gap] = swap(block, "dom", gap)
+            quarter[0], coded[late[0]] = lax.optimization_barrier((quarter[0], coded[late[0]]))
         quarter = exchange(quarter, "grp", along)
         quarters += [quarter[gap] for gap in [0] + along]
     filtered = whole_call(
@@ -333,17 +330,30 @@
         flops=1 << 20,
     )(kept, swap(sent, "dom", 1))
     parts = [merged[0]] + [swap(merged[gap // 2], "dom", gap) for gap in order if gap and gap % 2 == 0]
-    combined = whole_call(
-        functools.partial(combine_kernel, groups),
-        arrays(1, (columns, own), jnp.float32) + arrays(groups - 1, (columns, own), jnp.bfloat16),
+    odd = [2 * gap + 1 for gap in range(groups // 2)]
+    even = [2 * gap for gap in range(groups // 2)]
+    width = own * groups // 2
+    kept, sent = whole_call(
+        functools.partial(combine_kernel, even, odd),
+        arrays(1, (columns, width), jnp.float32) + arrays(1, (columns, width), jnp.bfloat16),
         "s" + "v" * chips,
         (pltpu.VMEM((columns, orbs), jnp.float32),),
         flops=1 << 20,
     )(spot, *parts)
-    combined = exchange(combined, "grp", along)
-    correlation = whole_call(
-        finish_kernel, arrays(1, (columns, own), jnp.float32)[0], "v" * groups, flops=1 << 16
-    )(*[combined[gap] for gap in [0] + along])
+    gap = 1
+    while True:
+        came = swap(sent, "grp", gap)
+        gap *= 2
+        if gap == groups:
+            break
+        width //= 2
+        kept, sent = whole_call(
+            halve_kernel,
+            arrays(1, (columns, width), jnp.float32) + arrays(1, (columns, width), jnp.bfloat16),
+            "vv",
+            flops=1 << 18,
+        )(kept, came)
+    correlation = whole_call(halve_kernel, arrays(1, (columns, own), jnp.float32), "vv", flops=1 << 16)(kept, came)[0]
     return filtered.transpose(1, 0, 2), correlation.T
 
 

time: 75.9 us -> 75.6 us (level)
  waiting for transfers between devices: 28.5 us -> 25.7 us
  starting transfers between devices: 30.6 us -> 33.1 us
    ppermute x27 -> x26, waiting for transfers between devices: 28.5 us -> 25.7 us  [swap(): return lax.ppermute(block, axis, [(i, i ^ gap) for i in range(count)])]
    ppermute x27 -> x26, starting transfers between devices: 30.6 us -> 33.1 us  [swap(): return lax.ppermute(block, axis, [(i, i ^ gap) for i in range(count)])]
  transfers between devices with their start and end apart: 27 -> 26, of which waited for: 15 -> 14; matrix products, arithmetic and copies ran while one was open for 0% -> 0% of each run, Pallas kernels for 3% -> 3%
where the time goes in v3:
time: 75.6 us; the launch traced here: 75.3 us
  starting transfers between devices  33.1 us (44%)
  waiting for transfers between devices  25.7 us (34%)
  Pallas kernels  15.1 us (20%)
    ppermute x26, starting transfers between devices, swap(): return lax.ppermute(block, axis, [(i, i ^ gap) for i in range(count)])  33.1 us
    ppermute x26, waiting for transfers between devices, swap(): return lax.ppermute(block, axis, [(i, i ^ gap) for i in range(count)])  25.7 us
    pallas_call x1, Pallas kernels, transposed_shards(): whole_call(functools.partial(filter_kernel, domains, planes, order), arra...  9.33 us
    pallas_call x1, Pallas kernels, transposed_shards(): whole_call(functools.partial(pack_kernel, domains), arrays(domains, (leng...  1.57 us
    pallas_call x1, Pallas kernels, transposed_shards(): whole_call(functools.partial(write_kernel, planes, early + late), arrays(...  1.56 us
  transfers between devices with their start and end apart: 26, of which 14 were waited for; matrix products, arithmetic and copies ran while one was open for 0% of the time, Pallas kernels for 3%

profile of v3, /device:TPU:0, one launch (start us, length us, event | category | flops | bytes accessed | tf_op | source)
XLA Modules:
  0.0 75.3 jit_solution(7977800958059910797)
XLA Ops:
  0.6 0.0 copy-start
  0.6 0.7 copy-done
  1.4 1.6 %shard_map.50 = (bf16[104,512]{1,0:T(8,128)(2,1)S(1)}, bf16[104,512]{1,0:T(8,128)(2,1)S(1)}, bf16[104,512]{1,0:T(8,128)(2,1)S(1)}, bf16[104,512]{1,0:T(8,128)(2,...) custom-call(s32[1]{0:T(128)} %bitcast.place, ...), custom_call_target="tpu_custom_call" | custom-call | flops 1048576 | bytes 1048576 | tf_op jit(solution)/shard_map/pallas_call | solution.py:267
  2.9 4.0 %collective-permute-start = (bf16[104,512]{1,0:T(8,128)(2,1)S(1)}, bf16[104,512]{1,0:T(8,128)(2,1)S(1)}, u32[]{:S(2)}, u32[]{:S(2)}) collective-permute-start(bf16[104,512]{1,0:T(8,128)(2,1)S(1)} %get-tuple-element.41), channel_id=1, source_target_pairs={{0,24},{4,28},{8,16},{12,20},{16,8},{20,12},{24,0},{28,4},{1,25},{... | collective-permute-start | bytes 319496 | tf_op jit(solution)/shard_map/ppermute | solution.py:239
  6.9 0.0 collective-permute-start.1
  6.9 1.1 %collective-permute-start.2 = (bf16[104,512]{1,0:T(8,128)(2,1)S(1)}, bf16[104,512]{1,0:T(8,128)(2,1)S(1)}, u32[]{:S(2)}, u32[]{:S(2)}) collective-permute-start(bf16[104,512]{1,0:T(8,128)(2,1)S(1)} %get-tuple-element.43), channel_id=1, source_target_pairs={{0,8},{4,12},{8,0},{12,4},{16,24},{20,28},{24,16},{28,20},{1,9},{5... | collective-permute-start | bytes 319496 | tf_op jit(solution)/shard_map/ppermute | solution.py:239
  8.0 0.6 collective-permute-start.3
  8.6 1.7 %collective-permute-start.4 = (bf16[104,512]{1,0:T(8,128)(2,1)S(1)}, bf16[104,512]{1,0:T(8,128)(2,1)S(1)}, u32[]{:S(2)}, u32[]{:S(2)}) collective-permute-start(bf16[104,512]{1,0:T(8,128)(2,1)S(1)} %get-tuple-element.45), channel_id=1, source_target_pairs={{0,16},{4,20},{8,24},{12,28},{16,0},{20,4},{24,8},{28,12},{1,17},{... | collective-permute-start | bytes 319496 | tf_op jit(solution)/shard_map/ppermute | solution.py:239
  10.4 0.0 collective-permute-done.refs_1_
  10.4 0.0 collective-permute-start.5
  10.4 2.7 %collective-permute-done.1.refs_2_ = bf16[104,512]{1,0:T(8,128)(2,1)S(1)} collective-permute-done((bf16[104,512]{1,0:T(8,128)(2,1)S(1)}, bf16[104,512]{1,0:T(8,128)(2,1)S(1)}, u32[]{:S(2)}, u32[]{:S(2)}) %collective-permute-start.1) | collective-permute-done | bytes 106528 | tf_op jit(solution)/shard_map/ppermute | solution.py:239
  13.1 0.0 collective-permute-start.6
  13.1 1.9 %collective-permute-done.2.refs_3_ = bf16[104,512]{1,0:T(8,128)(2,1)S(1)} collective-permute-done((bf16[104,512]{1,0:T(8,128)(2,1)S(1)}, bf16[104,512]{1,0:T(8,128)(2,1)S(1)}, u32[]{:S(2)}, u32[]{:S(2)}) %collective-permute-start.2) | collective-permute-done | bytes 106528 | tf_op jit(solution)/shard_map/ppermute | solution.py:239
  15.0 1.7 %collective-permute-done.3.refs_4_ = bf16[104,512]{1,0:T(8,128)(2,1)S(1)} collective-permute-done((bf16[104,512]{1,0:T(8,128)(2,1)S(1)}, bf16[104,512]{1,0:T(8,128)(2,1)S(1)}, u32[]{:S(2)}, u32[]{:S(2)}) %collective-permute-start.3) | collective-permute-done | bytes 106528 | tf_op jit(solution)/shard_map/ppermute | solution.py:239
  16.6 0.0 collective-permute-done.4.refs_5_
  16.7 0.7 collective-permute-done.5.refs_6_
  17.3 0.0 collective-permute-done.6.refs_7_
  17.3 0.0 copy-done.1
  17.3 9.3 %shard_map.51 = (bf16[96,512]{1,0:T(8,128)(2,1)S(1)}, bf16[96,512]{1,0:T(8,128)(2,1)S(1)}, bf16[96,512]{1,0:T(8,128)(2,1)S(1)}, bf16[96,512]{1,0:T(8,128)(2,1)S(...) custom-call(s32[1]{0:T(128)} %bitcast.place, ...), custom_call_target="tpu_custom_call" | custom-call | flops 3221225472 | bytes 1048576 | tf_op jit(solution)/shard_map/pallas_call | solution.py:281
  26.7 1.7 %collective-permute-start.7 = (bf16[96,512]{1,0:T(8,128)(2,1)S(1)}, bf16[96,512]{1,0:T(8,128)(2,1)S(1)}, u32[]{:S(2)}, u32[]{:S(2)}) collective-permute-start(bf16[96,512]{1,0:T(8,128)(2,1)S(1)} %get-tuple-element.49), channel_id=1, source_target_pairs={{0,24},{4,28},{8,16},{12,20},{16,8},{20,12},{24,0},{28,4},{1,25},{... | collective-permute-start | bytes 294920 | tf_op jit(solution)/shard_map/ppermute | solution.py:239
  28.4 0.7 collective-permute-start.8
  29.1 0.7 collective-permute-start.9
  29.8 0.9 %collective-permute-start.10 = (bf16[96,512]{1,0:T(8,128)(2,1)S(1)}, bf16[96,512]{1,0:T(8,128)(2,1)S(1)}, u32[]{:S(2)}, u32[]{:S(2)}) collective-permute-start(bf16[96,512]{1,0:T(8,128)(2,1)S(1)} %get-tuple-element.53), channel_id=1, source_target_pairs={{0,8},{4,12},{8,0},{12,4},{16,24},{20,28},{24,16},{28,20},{1,9},{5... | collective-permute-start | bytes 294920 | tf_op jit(solution)/shard_map/ppermute | solution.py:239
  30.7 0.4 collective-permute-start.11
  31.1 1.5 %collective-permute-done.7.refs_1_ = bf16[96,512]{1,0:T(8,128)(2,1)S(1)} collective-permute-done((bf16[96,512]{1,0:T(8,128)(2,1)S(1)}, bf16[96,512]{1,0:T(8,128)(2,1)S(1)}, u32[]{:S(2)}, u32[]{:S(2)}) %collective-permute-start.7) | collective-permute-done | bytes 98336 | tf_op jit(solution)/shard_map/ppermute | solution.py:239
  32.6 1.2 %collective-permute-start.12 = (bf16[96,512]{1,0:T(8,128)(2,1)S(1)}, bf16[96,512]{1,0:T(8,128)(2,1)S(1)}, u32[]{:S(2)}, u32[]{:S(2)}) collective-permute-start(bf16[96,512]{1,0:T(8,128)(2,1)S(1)} %get-tuple-element.56), channel_id=1, source_target_pairs={{0,16},{4,20},{8,24},{12,28},{16,0},{20,4},{24,8},{28,12},{1,17},{... | collective-permute-start | bytes 294920 | tf_op jit(solution)/shard_map/ppermute | solution.py:239
  33.8 0.7 collective-permute-done.8.refs_2_
  34.4 0.9 %collective-permute-start.13 = (bf16[96,512]{1,0:T(8,128)(2,1)S(1)}, bf16[96,512]{1,0:T(8,128)(2,1)S(1)}, u32[]{:S(2)}, u32[]{:S(2)}) collective-permute-start(bf16[96,512]{1,0:T(8,128)(2,1)S(1)} %get-tuple-element.57), channel_id=1, source_target_pairs={{0,20},{4,16},{8,28},{12,24},{16,4},{20,0},{24,12},{28,8},{1,21},{... | collective-permute-start | bytes 294920 | tf_op jit(solution)/shard_map/ppermute | solution.py:239
  35.3 0.0 collective-permute-done.9.refs_3_
  35.3 0.3 shard_map.52
  35.6 2.6 %collective-permute-start.14 = (bf16[6,64,128]{2,1,0:T(8,128)(2,1)S(1)}, bf16[6,64,128]{2,1,0:T(8,128)(2,1)S(1)}, u32[]{:S(2)}, u32[]{:S(2)}) collective-permute-start(bf16[6,64,128]{2,1,0:T(8,128)(2,1)S(1)} %get-tuple-element.61), channel_id=1, source_target_pairs={{0,2},{1,3},{2,0},{3,1},{4,6},{5,7},{6,4},{7,5},{8,10},{9,11},{10,... | collective-permute-start | bytes 294920 | tf_op jit(solution)/shard_map/ppermute | solution.py:239
  38.3 0.0 collective-permute-done.10.refs_4_.refs_0_
  38.3 1.8 %collective-permute-start.15 = (bf16[6,64,128]{2,1,0:T(8,128)(2,1)S(1)}, bf16[6,64,128]{2,1,0:T(8,128)(2,1)S(1)}, u32[]{:S(2)}, u32[]{:S(2)}) collective-permute-start(bf16[6,64,128]{2,1,0:T(8,128)(2,1)S(1)} %get-tuple-element.62), channel_id=1, source_target_pairs={{0,3},{1,2},{2,1},{3,0},{4,7},{5,6},{6,5},{7,4},{8,11},{9,10},{10,... | collective-permute-start | bytes 294920 | tf_op jit(solution)/shard_map/ppermute | solution.py:239
  40.1 0.0 collective-permute-done.11.refs_5_.refs_1_
  40.1 0.0 collective-permute-start.16
  40.1 0.0 collective-permute-done.12.refs_6_.refs_2_
  40.1 0.0 collective-permute-done.13.refs_7_.refs_3_
  40.1 0.3 shard_map.54
  40.5 2.6 %collective-permute-start.17 = (bf16[6,64,128]{2,1,0:T(8,128)(2,1)S(1)}, bf16[6,64,128]{2,1,0:T(8,128)(2,1)S(1)}, u32[]{:S(2)}, u32[]{:S(2)}) collective-permute-start(bf16[6,64,128]{2,1,0:T(8,128)(2,1)S(1)} %get-tuple-element.65), channel_id=1, source_target_pairs={{0,2},{1,3},{2,0},{3,1},{4,6},{5,7},{6,4},{7,5},{8,10},{9,11},{10,... | collective-permute-start | bytes 294920 | tf_op jit(solution)/shard_map/ppermute | solution.py:239
  43.1 1.8 %collective-permute-start.18 = (bf16[6,64,128]{2,1,0:T(8,128)(2,1)S(1)}, bf16[6,64,128]{2,1,0:T(8,128)(2,1)S(1)}, u32[]{:S(2)}, u32[]{:S(2)}) collective-permute-start(bf16[6,64,128]{2,1,0:T(8,128)(2,1)S(1)} %get-tuple-element.66), channel_id=1, source_target_pairs={{0,3},{1,2},{2,1},{3,0},{4,7},{5,6},{6,5},{7,4},{8,11},{9,10},{10,... | collective-permute-start | bytes 294920 | tf_op jit(solution)/shard_map/ppermute | solution.py:239
  44.9 2.9 %collective-permute-done.14.refs_1_ = bf16[6,64,128]{2,1,0:T(8,128)(2,1)S(1)} collective-permute-done((bf16[6,64,128]{2,1,0:T(8,128)(2,1)S(1)}, bf16[6,64,128]{2,1,0:T(8,128)(2,1)S(1)}, u32[]{:S(2)}, u32[]{:S(2)}) %collective-permute-start.14) | collective-permute-done | bytes 98336 | tf_op jit(solution)/shard_map/ppermute | solution.py:239
  47.8 0.0 collective-permute-start.19
  47.8 1.6 %shard_map.53 = f32[6,128,512]{2,1,0:T(8,128)} custom-call(s32[1]{0:T(128)} %bitcast.place, bf16[96,512]{1,0:T(8,128)(2,1)S(1)} %get-tuple-element.48.refs_0_, bf16[96,512]{1,0:T(8,128)(2,1)S(1)} %collective-permute-done.7.refs_1_, bf16[96,512]{1,0:T(8,128)(2,1)S(1)} %collective-permute-done.8.refs_2_, bf16[96,512]{1,0:T(8,128)(2,1)S(1)} %collective-permute-done.9.refs_3_, ...), custom_call_target="tpu_custom_call" | custom-call | flops 16777216 | bytes 1048576 | tf_op jit(solution)/shard_map/pallas_call | solution.py:311
  49.3 0.0 collective-permute-done.15.refs_2_
  49.3 0.0 collective-permute-done.16.refs_3_
  49.3 5.6 %collective-permute-done.17.refs_5_ = bf16[6,64,128]{2,1,0:T(8,128)(2,1)S(1)} collective-permute-done((bf16[6,64,128]{2,1,0:T(8,128)(2,1)S(1)}, bf16[6,64,128]{2,1,0:T(8,128)(2,1)S(1)}, u32[]{:S(2)}, u32[]{:S(2)}) %collective-permute-start.17) | collective-permute-done | bytes 98336 | tf_op jit(solution)/shard_map/ppermute | solution.py:239
  54.9 0.0 collective-permute-done.18.refs_6_
  54.9 0.0 collective-permute-done.19.refs_7_
  54.9 0.9 %shard_map.55 = (f32[256,512]{1,0:T(8,128)S(1)}, bf16[256,512]{1,0:T(8,128)(2,1)S(1)}) custom-call(s32[1]{0:T(128)} %bitcast.place, s32[1]{0:T(128)} %bitcast.2.spot, bf16[6,64,128]{2,1,0:T(8,128)(2,1)S(1)} %get-tuple-element.60.refs_0_, bf16[6,64,128]{2,1,0:T(8,128)(2,1)S(1)} %collective-permute-done.14.refs_1_, ...), custom_call_target="tpu_custom_call" | custom-call | flops 268435456 | bytes 1048576 | tf_op jit(solution)/shard_map/pallas_call | solution.py:318
  55.8 0.1 collective-permute-start.20
  55.9 1.5 %collective-permute-done.20.came = bf16[256,512]{1,0:T(8,128)(2,1)S(1)} collective-permute-done((bf16[256,512]{1,0:T(8,128)(2,1)S(1)}, bf16[256,512]{1,0:T(8,128)(2,1)S(1)}, u32[]{:S(2)}, u32[]{:S(2)}) %collective-permute-start.20) | collective-permute-done | bytes 262176 | tf_op jit(solution)/shard_map/ppermute | solution.py:239
  57.4 0.2 shard_map.56
  57.6 1.6 %collective-permute-start.21 = (bf16[64,512]{1,0:T(8,128)(2,1)S(1)}, bf16[64,512]{1,0:T(8,128)(2,1)S(1)}, u32[]{:S(2)}, u32[]{:S(2)}) collective-permute-start(bf16[64,512]{1,0:T(8,128)(2,1)S(1)} %get-tuple-element.71), channel_id=1, source_target_pairs={{0,24},{4,28},{8,16},{12,20},{16,8},{20,12},{24,0},{28,4},{1,25},{... | collective-permute-start | bytes 196616 | tf_op jit(solution)/shard_map/ppermute | solution.py:239
  59.2 0.8 %collective-permute-start.22 = (bf16[64,512]{1,0:T(8,128)(2,1)S(1)}, bf16[64,512]{1,0:T(8,128)(2,1)S(1)}, u32[]{:S(2)}, u32[]{:S(2)}) collective-permute-start(bf16[64,512]{1,0:T(8,128)(2,1)S(1)} %get-tuple-element.72), channel_id=1, source_target_pairs={{0,8},{4,12},{8,0},{12,4},{16,24},{20,28},{24,16},{28,20},{1,9},{5... | collective-permute-start | bytes 196616 | tf_op jit(solution)/shard_map/ppermute | solution.py:239
  60.0 1.1 %collective-permute-start.23 = (bf16[64,512]{1,0:T(8,128)(2,1)S(1)}, bf16[64,512]{1,0:T(8,128)(2,1)S(1)}, u32[]{:S(2)}, u32[]{:S(2)}) collective-permute-start(bf16[64,512]{1,0:T(8,128)(2,1)S(1)} %get-tuple-element.73), channel_id=1, source_target_pairs={{0,16},{4,20},{8,24},{12,28},{16,0},{20,4},{24,8},{28,12},{1,17},{... | collective-permute-start | bytes 196616 | tf_op jit(solution)/shard_map/ppermute | solution.py:239
  61.2 2.3 %collective-permute-done.21.refs_1_ = bf16[64,512]{1,0:T(8,128)(2,1)S(1)} collective-permute-done((bf16[64,512]{1,0:T(8,128)(2,1)S(1)}, bf16[64,512]{1,0:T(8,128)(2,1)S(1)}, u32[]{:S(2)}, u32[]{:S(2)}) %collective-permute-start.21) | collective-permute-done | bytes 65568 | tf_op jit(solution)/shard_map/ppermute | solution.py:239
  63.5 0.2 collective-permute-done.22.refs_2_
  63.7 0.6 collective-permute-done.23.refs_3_
  64.3 0.2 shard_map.57
  64.5 2.4 %collective-permute-start.24 = (bf16[64,256]{1,0:T(8,128)(2,1)S(1)}, bf16[64,256]{1,0:T(8,128)(2,1)S(1)}, u32[]{:S(2)}, u32[]{:S(2)}) collective-permute-start(bf16[64,256]{1,0:T(8,128)(2,1)S(1)} %get-tuple-element.75), channel_id=1, source_target_pairs={{0,1},{1,0},{2,3},{3,2},{4,5},{5,4},{6,7},{7,6},{8,9},{9,8},{10,11... | collective-permute-start | bytes 98312 | tf_op jit(solution)/shard_map/ppermute | solution.py:239
  66.9 1.9 %collective-permute-done.24.came = bf16[64,256]{1,0:T(8,128)(2,1)S(1)} collective-permute-done((bf16[64,256]{1,0:T(8,128)(2,1)S(1)}, bf16[64,256]{1,0:T(8,128)(2,1)S(1)}, u32[]{:S(2)}, u32[]{:S(2)}) %collective-permute-start.24) | collective-permute-done | bytes 32800 | tf_op jit(solution)/shard_map/ppermute | solution.py:239
  68.8 4.2 %collective-permute-start.25 = (bf16[64,128]{1,0:T(8,128)(2,1)S(1)}, bf16[64,128]{1,0:T(8,128)(2,1)S(1)}, u32[]{:S(2)}, u32[]{:S(2)}) collective-permute-start(bf16[64,128]{1,0:T(8,128)(2,1)S(1)} %get-tuple-element.77), channel_id=1, source_target_pairs={{0,2},{1,3},{2,0},{3,1},{4,6},{5,7},{6,4},{7,5},{8,10},{9,11},{10,... | collective-permute-start | bytes 49160 | tf_op jit(solution)/shard_map/ppermute | solution.py:239
  73.0 1.7 %collective-permute-done.25.came = bf16[64,128]{1,0:T(8,128)(2,1)S(1)} collective-permute-done((bf16[64,128]{1,0:T(8,128)(2,1)S(1)}, bf16[64,128]{1,0:T(8,128)(2,1)S(1)}, u32[]{:S(2)}, u32[]{:S(2)}) %collective-permute-start.25) | collective-permute-done | bytes 16416 | tf_op jit(solution)/shard_map/ppermute | solution.py:239
  74.7 0.6 shard_map.59
  (2 shorter events, 0.0 us)
Async XLA Ops:
  0.6 0.7 copy-start
  1.4 16.0 %copy-start.1 = (bf16[1024,512]{1,0:T(8,128)(2,1)S(1)}, bf16[1024,512]{1,0:T(8,128)(2,1)}, u32[]{:S(2)}) copy-start(bf16[1024,512]{1,0:T(8,128)(2,1)} %constant.11.clone.refs_8_) | copy-start | bytes 3145732
  2.9 7.4 %collective-permute-start = (bf16[104,512]{1,0:T(8,128)(2,1)S(1)}, bf16[104,512]{1,0:T(8,128)(2,1)S(1)}, u32[]{:S(2)}, u32[]{:S(2)}) collective-permute-start(bf16[104,512]{1,0:T(8,128)(2,1)S(1)} %get-tuple-element.41), channel_id=1, source_target_pairs={{0,24},{4,28},{8,16},{12,20},{16,8},{20,12},{24,0},{28,4},{1,25},{... | collective-permute-start | bytes 319496 | tf_op jit(solution)/shard_map/ppermute | solution.py:239
  6.9 6.2 %collective-permute-start.1 = (bf16[104,512]{1,0:T(8,128)(2,1)S(1)}, bf16[104,512]{1,0:T(8,128)(2,1)S(1)}, u32[]{:S(2)}, u32[]{:S(2)}) collective-permute-start(bf16[104,512]{1,0:T(8,128)(2,1)S(1)} %get-tuple-element.42), channel_id=1, source_target_pairs={{0,28},{4,24},{8,20},{12,16},{16,12},{20,8},{24,4},{28,0},{1,29},{... | collective-permute-start | bytes 319496 | tf_op jit(solution)/shard_map/ppermute | solution.py:239
  6.9 8.1 %collective-permute-start.2 = (bf16[104,512]{1,0:T(8,128)(2,1)S(1)}, bf16[104,512]{1,0:T(8,128)(2,1)S(1)}, u32[]{:S(2)}, u32[]{:S(2)}) collective-permute-start(bf16[104,512]{1,0:T(8,128)(2,1)S(1)} %get-tuple-element.43), channel_id=1, source_target_pairs={{0,8},{4,12},{8,0},{12,4},{16,24},{20,28},{24,16},{28,20},{1,9},{5... | collective-permute-start | bytes 319496 | tf_op jit(solution)/shard_map/ppermute | solution.py:239
  8.0 8.6 %collective-permute-start.3 = (bf16[104,512]{1,0:T(8,128)(2,1)S(1)}, bf16[104,512]{1,0:T(8,128)(2,1)S(1)}, u32[]{:S(2)}, u32[]{:S(2)}) collective-permute-start(bf16[104,512]{1,0:T(8,128)(2,1)S(1)} %get-tuple-element.44), channel_id=1, source_target_pairs={{0,12},{4,8},{8,4},{12,0},{16,28},{20,24},{24,20},{28,16},{1,13},{... | collective-permute-start | bytes 319496 | tf_op jit(solution)/shard_map/ppermute | solution.py:239
  8.6 8.0 %collective-permute-start.4 = (bf16[104,512]{1,0:T(8,128)(2,1)S(1)}, bf16[104,512]{1,0:T(8,128)(2,1)S(1)}, u32[]{:S(2)}, u32[]{:S(2)}) collective-permute-start(bf16[104,512]{1,0:T(8,128)(2,1)S(1)} %get-tuple-element.45), channel_id=1, source_target_pairs={{0,16},{4,20},{8,24},{12,28},{16,0},{20,4},{24,8},{28,12},{1,17},{... | collective-permute-start | bytes 319496 | tf_op jit(solution)/shard_map/ppermute | solution.py:239
  10.4 7.0 %collective-permute-start.5 = (bf16[104,512]{1,0:T(8,128)(2,1)S(1)}, bf16[104,512]{1,0:T(8,128)(2,1)S(1)}, u32[]{:S(2)}, u32[]{:S(2)}) collective-permute-start(bf16[104,512]{1,0:T(8,128)(2,1)S(1)} %get-tuple-element.46), channel_id=1, source_target_pairs={{0,20},{4,16},{8,28},{12,24},{16,4},{20,0},{24,12},{28,8},{1,21},{... | collective-permute-start | bytes 319496 | tf_op jit(solution)/shard_map/ppermute | solution.py:239
  13.1 4.3 %collective-permute-start.6 = (bf16[104,512]{1,0:T(8,128)(2,1)S(1)}, bf16[104,512]{1,0:T(8,128)(2,1)S(1)}, u32[]{:S(2)}, u32[]{:S(2)}) collective-permute-start(bf16[104,512]{1,0:T(8,128)(2,1)S(1)} %get-tuple-element.47), channel_id=1, source_target_pairs={{0,4},{4,0},{8,12},{12,8},{16,20},{20,16},{24,28},{28,24},{1,5},{5... | collective-permute-start | bytes 319496 | tf_op jit(solution)/shard_map/ppermute | solution.py:239
  26.7 5.9 %collective-permute-start.7 = (bf16[96,512]{1,0:T(8,128)(2,1)S(1)}, bf16[96,512]{1,0:T(8,128)(2,1)S(1)}, u32[]{:S(2)}, u32[]{:S(2)}) collective-permute-start(bf16[96,512]{1,0:T(8,128)(2,1)S(1)} %get-tuple-element.49), channel_id=1, source_target_pairs={{0,24},{4,28},{8,16},{12,20},{16,8},{20,12},{24,0},{28,4},{1,25},{... | collective-permute-start | bytes 294920 | tf_op jit(solution)/shard_map/ppermute | solution.py:239
  28.4 6.0 %collective-permute-start.8 = (bf16[96,512]{1,0:T(8,128)(2,1)S(1)}, bf16[96,512]{1,0:T(8,128)(2,1)S(1)}, u32[]{:S(2)}, u32[]{:S(2)}) collective-permute-start(bf16[96,512]{1,0:T(8,128)(2,1)S(1)} %get-tuple-element.50), channel_id=1, source_target_pairs={{0,28},{4,24},{8,20},{12,16},{16,12},{20,8},{24,4},{28,0},{1,29},{... | collective-permute-start | bytes 294920 | tf_op jit(solution)/shard_map/ppermute | solution.py:239
  29.1 6.2 %collective-permute-start.9 = (bf16[96,512]{1,0:T(8,128)(2,1)S(1)}, bf16[96,512]{1,0:T(8,128)(2,1)S(1)}, u32[]{:S(2)}, u32[]{:S(2)}) collective-permute-start(bf16[96,512]{1,0:T(8,128)(2,1)S(1)} %get-tuple-element.51), channel_id=1, source_target_pairs={{0,4},{4,0},{8,12},{12,8},{16,20},{20,16},{24,28},{28,24},{1,5},{5... | collective-permute-start | bytes 294920 | tf_op jit(solution)/shard_map/ppermute | solution.py:239
  29.8 8.5 %collective-permute-start.10 = (bf16[96,512]{1,0:T(8,128)(2,1)S(1)}, bf16[96,512]{1,0:T(8,128)(2,1)S(1)}, u32[]{:S(2)}, u32[]{:S(2)}) collective-permute-start(bf16[96,512]{1,0:T(8,128)(2,1)S(1)} %get-tuple-element.53), channel_id=1, source_target_pairs={{0,8},{4,12},{8,0},{12,4},{16,24},{20,28},{24,16},{28,20},{1,9},{5... | collective-permute-start | bytes 294920 | tf_op jit(solution)/shard_map/ppermute | solution.py:239
  30.7 9.4 %collective-permute-start.11 = (bf16[96,512]{1,0:T(8,128)(2,1)S(1)}, bf16[96,512]{1,0:T(8,128)(2,1)S(1)}, u32[]{:S(2)}, u32[]{:S(2)}) collective-permute-start(bf16[96,512]{1,0:T(8,128)(2,1)S(1)} %get-tuple-element.55), channel_id=1, source_target_pairs={{0,12},{4,8},{8,4},{12,0},{16,28},{20,24},{24,20},{28,16},{1,13},{... | collective-permute-start | bytes 294920 | tf_op jit(solution)/shard_map/ppermute | solution.py:239
  32.6 7.5 %collective-permute-start.12 = (bf16[96,512]{1,0:T(8,128)(2,1)S(1)}, bf16[96,512]{1,0:T(8,128)(2,1)S(1)}, u32[]{:S(2)}, u32[]{:S(2)}) collective-permute-start(bf16[96,512]{1,0:T(8,128)(2,1)S(1)} %get-tuple-element.56), channel_id=1, source_target_pairs={{0,16},{4,20},{8,24},{12,28},{16,0},{20,4},{24,8},{28,12},{1,17},{... | collective-permute-start | bytes 294920 | tf_op jit(solution)/shard_map/ppermute | solution.py:239
  34.4 5.7 %collective-permute-start.13 = (bf16[96,512]{1,0:T(8,128)(2,1)S(1)}, bf16[96,512]{1,0:T(8,128)(2,1)S(1)}, u32[]{:S(2)}, u32[]{:S(2)}) collective-permute-start(bf16[96,512]{1,0:T(8,128)(2,1)S(1)} %get-tuple-element.57), channel_id=1, source_target_pairs={{0,20},{4,16},{8,28},{12,24},{16,4},{20,0},{24,12},{28,8},{1,21},{... | collective-permute-start | bytes 294920 | tf_op jit(solution)/shard_map/ppermute | solution.py:239
  35.6 12.1 %collective-permute-start.14 = (bf16[6,64,128]{2,1,0:T(8,128)(2,1)S(1)}, bf16[6,64,128]{2,1,0:T(8,128)(2,1)S(1)}, u32[]{:S(2)}, u32[]{:S(2)}) collective-permute-start(bf16[6,64,128]{2,1,0:T(8,128)(2,1)S(1)} %get-tuple-element.61), channel_id=1, source_target_pairs={{0,2},{1,3},{2,0},{3,1},{4,6},{5,7},{6,4},{7,5},{8,10},{9,11},{10,... | collective-permute-start | bytes 294920 | tf_op jit(solution)/shard_map/ppermute | solution.py:239
  38.3 11.1 %collective-permute-start.15 = (bf16[6,64,128]{2,1,0:T(8,128)(2,1)S(1)}, bf16[6,64,128]{2,1,0:T(8,128)(2,1)S(1)}, u32[]{:S(2)}, u32[]{:S(2)}) collective-permute-start(bf16[6,64,128]{2,1,0:T(8,128)(2,1)S(1)} %get-tuple-element.62), channel_id=1, source_target_pairs={{0,3},{1,2},{2,1},{3,0},{4,7},{5,6},{6,5},{7,4},{8,11},{9,10},{10,... | collective-permute-start | bytes 294920 | tf_op jit(solution)/shard_map/ppermute | solution.py:239
  40.1 9.2 %collective-permute-start.16 = (bf16[6,64,128]{2,1,0:T(8,128)(2,1)S(1)}, bf16[6,64,128]{2,1,0:T(8,128)(2,1)S(1)}, u32[]{:S(2)}, u32[]{:S(2)}) collective-permute-start(bf16[6,64,128]{2,1,0:T(8,128)(2,1)S(1)} %get-tuple-element.63), channel_id=1, source_target_pairs={{0,1},{1,0},{2,3},{3,2},{4,5},{5,4},{6,7},{7,6},{8,9},{9,8},{10,11... | collective-permute-start | bytes 294920 | tf_op jit(solution)/shard_map/ppermute | solution.py:239
  40.5 14.4 %collective-permute-start.17 = (bf16[6,64,128]{2,1,0:T(8,128)(2,1)S(1)}, bf16[6,64,128]{2,1,0:T(8,128)(2,1)S(1)}, u32[]{:S(2)}, u32[]{:S(2)}) collective-permute-start(bf16[6,64,128]{2,1,0:T(8,128)(2,1)S(1)} %get-tuple-element.65), channel_id=1, source_target_pairs={{0,2},{1,3},{2,0},{3,1},{4,6},{5,7},{6,4},{7,5},{8,10},{9,11},{10,... | collective-permute-start | bytes 294920 | tf_op jit(solution)/shard_map/ppermute | solution.py:239
  43.1 11.8 %collective-permute-start.18 = (bf16[6,64,128]{2,1,0:T(8,128)(2,1)S(1)}, bf16[6,64,128]{2,1,0:T(8,128)(2,1)S(1)}, u32[]{:S(2)}, u32[]{:S(2)}) collective-permute-start(bf16[6,64,128]{2,1,0:T(8,128)(2,1)S(1)} %get-tuple-element.66), channel_id=1, source_target_pairs={{0,3},{1,2},{2,1},{3,0},{4,7},{5,6},{6,5},{7,4},{8,11},{9,10},{10,... | collective-permute-start | bytes 294920 | tf_op jit(solution)/shard_map/ppermute | solution.py:239
  47.8 7.1 %collective-permute-start.19 = (bf16[6,64,128]{2,1,0:T(8,128)(2,1)S(1)}, bf16[6,64,128]{2,1,0:T(8,128)(2,1)S(1)}, u32[]{:S(2)}, u32[]{:S(2)}) collective-permute-start(bf16[6,64,128]{2,1,0:T(8,128)(2,1)S(1)} %get-tuple-element.67), channel_id=1, source_target_pairs={{0,1},{1,0},{2,3},{3,2},{4,5},{5,4},{6,7},{7,6},{8,9},{9,8},{10,11... | collective-permute-start | bytes 294920 | tf_op jit(solution)/shard_map/ppermute | solution.py:239
  55.8 1.6 %collective-permute-start.20 = (bf16[256,512]{1,0:T(8,128)(2,1)S(1)}, bf16[256,512]{1,0:T(8,128)(2,1)S(1)}, u32[]{:S(2)}, u32[]{:S(2)}) collective-permute-start(bf16[256,512]{1,0:T(8,128)(2,1)S(1)} %get-tuple-element.69), channel_id=1, source_target_pairs={{0,4},{4,0},{8,12},{12,8},{16,20},{20,16},{24,28},{28,24},{1,5},{5... | collective-permute-start | bytes 786440 | tf_op jit(solution)/shard_map/ppermute | solution.py:239
  57.6 5.9 %collective-permute-start.21 = (bf16[64,512]{1,0:T(8,128)(2,1)S(1)}, bf16[64,512]{1,0:T(8,128)(2,1)S(1)}, u32[]{:S(2)}, u32[]{:S(2)}) collective-permute-start(bf16[64,512]{1,0:T(8,128)(2,1)S(1)} %get-tuple-element.71), channel_id=1, source_target_pairs={{0,24},{4,28},{8,16},{12,20},{16,8},{20,12},{24,0},{28,4},{1,25},{... | collective-permute-start | bytes 196616 | tf_op jit(solution)/shard_map/ppermute | solution.py:239
  59.2 4.5 %collective-permute-start.22 = (bf16[64,512]{1,0:T(8,128)(2,1)S(1)}, bf16[64,512]{1,0:T(8,128)(2,1)S(1)}, u32[]{:S(2)}, u32[]{:S(2)}) collective-permute-start(bf16[64,512]{1,0:T(8,128)(2,1)S(1)} %get-tuple-element.72), channel_id=1, source_target_pairs={{0,8},{4,12},{8,0},{12,4},{16,24},{20,28},{24,16},{28,20},{1,9},{5... | collective-permute-start | bytes 196616 | tf_op jit(solution)/shard_map/ppermute | solution.py:239
  60.0 4.3 %collective-permute-start.23 = (bf16[64,512]{1,0:T(8,128)(2,1)S(1)}, bf16[64,512]{1,0:T(8,128)(2,1)S(1)}, u32[]{:S(2)}, u32[]{:S(2)}) collective-permute-start(bf16[64,512]{1,0:T(8,128)(2,1)S(1)} %get-tuple-element.73), channel_id=1, source_target_pairs={{0,16},{4,20},{8,24},{12,28},{16,0},{20,4},{24,8},{28,12},{1,17},{... | collective-permute-start | bytes 196616 | tf_op jit(solution)/shard_map/ppermute | solution.py:239
  64.5 4.3 %collective-permute-start.24 = (bf16[64,256]{1,0:T(8,128)(2,1)S(1)}, bf16[64,256]{1,0:T(8,128)(2,1)S(1)}, u32[]{:S(2)}, u32[]{:S(2)}) collective-permute-start(bf16[64,256]{1,0:T(8,128)(2,1)S(1)} %get-tuple-element.75), channel_id=1, source_target_pairs={{0,1},{1,0},{2,3},{3,2},{4,5},{5,4},{6,7},{7,6},{8,9},{9,8},{10,11... | collective-permute-start | bytes 98312 | tf_op jit(solution)/shard_map/ppermute | solution.py:239
  68.8 5.9 %collective-permute-start.25 = (bf16[64,128]{1,0:T(8,128)(2,1)S(1)}, bf16[64,128]{1,0:T(8,128)(2,1)S(1)}, u32[]{:S(2)}, u32[]{:S(2)}) collective-permute-start(bf16[64,128]{1,0:T(8,128)(2,1)S(1)} %get-tuple-element.77), channel_id=1, source_target_pairs={{0,2},{1,3},{2,0},{3,1},{4,6},{5,7},{6,4},{7,5},{8,10},{9,11},{10,... | collective-permute-start | bytes 49160 | tf_op jit(solution)/shard_map/ppermute | solution.py:239

commit v4 on v1

--- a/solution.py
+++ b/solution.py
@@ -292,8 +292,7 @@
     )(place, *[arrived[gap] for gap in order], weights)
     late = [gap for gap in order if hops(gap) == 1]
     early = [gap for gap in order if gap not in late]
-    last = late[len(late) // 2 :]
-    coded = exchange(coded, "dom", early[1:] + late[: len(late) // 2])
+    coded = exchange(coded, "dom", early[1:] + late)
     quarters = []
     for gaps in (early, late):
         quarter = whole_call(
@@ -305,10 +304,7 @@
         )(spot, *[coded[gap] for gap in gaps])
         if gaps is early:
             quarter = list(quarter)
-            held = lax.optimization_barrier((quarter[0], *[coded[gap] for gap in last]))
-            quarter[0] = held[0]
-            for gap, block in zip(last, held[1:]):
-                coded[gap] = swap(block, "dom", gap)
+            quarter[0], coded[late[0]] = lax.optimization_barrier((quarter[0], coded[late[0]]))
         quarter = exchange(quarter, "grp", along)
         quarters += [quarter[gap] for gap in [0] + along]
     filtered = whole_call(

time: 75.9 us -> 75.2 us (level)
  waiting for transfers between devices: 28.5 us -> 27 us
  starting transfers between devices: 30.6 us -> 31.4 us
    ppermute x27, waiting for transfers between devices: 28.5 us -> 27 us  [swap(): return lax.ppermute(block, axis, [(i, i ^ gap) for i in range(count)])]
    ppermute x27, starting transfers between devices: 30.6 us -> 31.4 us  [swap(): return lax.ppermute(block, axis, [(i, i ^ gap) for i in range(count)])]
  transfers between devices with their start and end apart: 27 -> 27, of which waited for: 15 -> 14; matrix products, arithmetic and copies ran while one was open for 0% -> 0% of each run, Pallas kernels for 3% -> 3%
where the time goes in v4:
time: 75.2 us; the launch traced here: 75 us
  starting transfers between devices  31.4 us (42%)
  waiting for transfers between devices  27 us (36%)
  Pallas kernels  15.1 us (20%)
    ppermute x27, starting transfers between devices, swap(): return lax.ppermute(block, axis, [(i, i ^ gap) for i in range(count)])  31.4 us
    ppermute x27, waiting for transfers between devices, swap(): return lax.ppermute(block, axis, [(i, i ^ gap) for i in range(count)])  27 us
    pallas_call x1, Pallas kernels, transposed_shards(): whole_call(functools.partial(filter_kernel, domains, planes, order), arra...  9.33 us
    pallas_call x1, Pallas kernels, transposed_shards(): whole_call(functools.partial(pack_kernel, domains), arrays(domains, (leng...  1.57 us
    pallas_call x1, Pallas kernels, transposed_shards(): whole_call(functools.partial(write_kernel, planes, early + late), arrays(...  1.56 us
  transfers between devices with their start and end apart: 27, of which 14 were waited for; matrix products, arithmetic and copies ran while one was open for 0% of the time, Pallas kernels for 3%

profile of v4, /device:TPU:0, one launch (start us, length us, event | category | flops | bytes accessed | tf_op | source)
XLA Modules:
  0.0 75.0 jit_solution(6281881954579440292)
XLA Ops:
  0.6 0.7 copy-done
  1.4 1.6 %shard_map.50 = (bf16[104,512]{1,0:T(8,128)(2,1)S(1)}, bf16[104,512]{1,0:T(8,128)(2,1)S(1)}, bf16[104,512]{1,0:T(8,128)(2,1)S(1)}, bf16[104,512]{1,0:T(8,128)(2,...) custom-call(s32[1]{0:T(128)} %bitcast.place, ...), custom_call_target="tpu_custom_call" | custom-call | flops 1048576 | bytes 1048576 | tf_op jit(solution)/shard_map/pallas_call | solution.py:266
  2.9 4.0 %collective-permute-start = (bf16[104,512]{1,0:T(8,128)(2,1)S(1)}, bf16[104,512]{1,0:T(8,128)(2,1)S(1)}, u32[]{:S(2)}, u32[]{:S(2)}) collective-permute-start(bf16[104,512]{1,0:T(8,128)(2,1)S(1)} %get-tuple-element.41), channel_id=1, source_target_pairs={{0,24},{4,28},{8,16},{12,20},{16,8},{20,12},{24,0},{28,4},{1,25},{... | collective-permute-start | bytes 319496 | tf_op jit(solution)/shard_map/ppermute | solution.py:238
  6.9 0.0 collective-permute-start.1
  6.9 1.1 %collective-permute-start.2 = (bf16[104,512]{1,0:T(8,128)(2,1)S(1)}, bf16[104,512]{1,0:T(8,128)(2,1)S(1)}, u32[]{:S(2)}, u32[]{:S(2)}) collective-permute-start(bf16[104,512]{1,0:T(8,128)(2,1)S(1)} %get-tuple-element.43), channel_id=1, source_target_pairs={{0,8},{4,12},{8,0},{12,4},{16,24},{20,28},{24,16},{28,20},{1,9},{5... | collective-permute-start | bytes 319496 | tf_op jit(solution)/shard_map/ppermute | solution.py:238
  8.0 0.6 collective-permute-start.3
  8.6 1.7 %collective-permute-start.4 = (bf16[104,512]{1,0:T(8,128)(2,1)S(1)}, bf16[104,512]{1,0:T(8,128)(2,1)S(1)}, u32[]{:S(2)}, u32[]{:S(2)}) collective-permute-start(bf16[104,512]{1,0:T(8,128)(2,1)S(1)} %get-tuple-element.45), channel_id=1, source_target_pairs={{0,16},{4,20},{8,24},{12,28},{16,0},{20,4},{24,8},{28,12},{1,17},{... | collective-permute-start | bytes 319496 | tf_op jit(solution)/shard_map/ppermute | solution.py:238
  10.4 0.0 collective-permute-done.refs_1_
  10.4 0.0 collective-permute-start.5
  10.4 2.7 %collective-permute-done.1.refs_2_ = bf16[104,512]{1,0:T(8,128)(2,1)S(1)} collective-permute-done((bf16[104,512]{1,0:T(8,128)(2,1)S(1)}, bf16[104,512]{1,0:T(8,128)(2,1)S(1)}, u32[]{:S(2)}, u32[]{:S(2)}) %collective-permute-start.1) | collective-permute-done | bytes 106528 | tf_op jit(solution)/shard_map/ppermute | solution.py:238
  13.1 0.0 collective-permute-start.6
  13.1 1.9 %collective-permute-done.2.refs_3_ = bf16[104,512]{1,0:T(8,128)(2,1)S(1)} collective-permute-done((bf16[104,512]{1,0:T(8,128)(2,1)S(1)}, bf16[104,512]{1,0:T(8,128)(2,1)S(1)}, u32[]{:S(2)}, u32[]{:S(2)}) %collective-permute-start.2) | collective-permute-done | bytes 106528 | tf_op jit(solution)/shard_map/ppermute | solution.py:238
  15.0 1.7 %collective-permute-done.3.refs_4_ = bf16[104,512]{1,0:T(8,128)(2,1)S(1)} collective-permute-done((bf16[104,512]{1,0:T(8,128)(2,1)S(1)}, bf16[104,512]{1,0:T(8,128)(2,1)S(1)}, u32[]{:S(2)}, u32[]{:S(2)}) %collective-permute-start.3) | collective-permute-done | bytes 106528 | tf_op jit(solution)/shard_map/ppermute | solution.py:238
  16.6 0.0 collective-permute-done.4.refs_5_
  16.7 0.7 collective-permute-done.5.refs_6_
  17.3 0.0 collective-permute-done.6.refs_7_
  17.3 9.3 %shard_map.51 = (bf16[96,512]{1,0:T(8,128)(2,1)S(1)}, bf16[96,512]{1,0:T(8,128)(2,1)S(1)}, bf16[96,512]{1,0:T(8,128)(2,1)S(1)}, bf16[96,512]{1,0:T(8,128)(2,1)S(...) custom-call(s32[1]{0:T(128)} %bitcast.place, ...), custom_call_target="tpu_custom_call" | custom-call | flops 3221225472 | bytes 1048576 | tf_op jit(solution)/shard_map/pallas_call | solution.py:280
  26.7 1.7 %collective-permute-start.7 = (bf16[96,512]{1,0:T(8,128)(2,1)S(1)}, bf16[96,512]{1,0:T(8,128)(2,1)S(1)}, u32[]{:S(2)}, u32[]{:S(2)}) collective-permute-start(bf16[96,512]{1,0:T(8,128)(2,1)S(1)} %get-tuple-element.49), channel_id=1, source_target_pairs={{0,24},{4,28},{8,16},{12,20},{16,8},{20,12},{24,0},{28,4},{1,25},{... | collective-permute-start | bytes 294920 | tf_op jit(solution)/shard_map/ppermute | solution.py:238
  28.4 0.7 collective-permute-start.8
  29.1 0.7 collective-permute-start.9
  29.8 0.9 %collective-permute-start.10 = (bf16[96,512]{1,0:T(8,128)(2,1)S(1)}, bf16[96,512]{1,0:T(8,128)(2,1)S(1)}, u32[]{:S(2)}, u32[]{:S(2)}) collective-permute-start(bf16[96,512]{1,0:T(8,128)(2,1)S(1)} %get-tuple-element.53), channel_id=1, source_target_pairs={{0,8},{4,12},{8,0},{12,4},{16,24},{20,28},{24,16},{28,20},{1,9},{5... | collective-permute-start | bytes 294920 | tf_op jit(solution)/shard_map/ppermute | solution.py:238
  30.7 0.4 collective-permute-start.11
  31.1 1.5 %collective-permute-done.7.refs_1_ = bf16[96,512]{1,0:T(8,128)(2,1)S(1)} collective-permute-done((bf16[96,512]{1,0:T(8,128)(2,1)S(1)}, bf16[96,512]{1,0:T(8,128)(2,1)S(1)}, u32[]{:S(2)}, u32[]{:S(2)}) %collective-permute-start.7) | collective-permute-done | bytes 98336 | tf_op jit(solution)/shard_map/ppermute | solution.py:238
  32.6 1.2 %collective-permute-start.12 = (bf16[96,512]{1,0:T(8,128)(2,1)S(1)}, bf16[96,512]{1,0:T(8,128)(2,1)S(1)}, u32[]{:S(2)}, u32[]{:S(2)}) collective-permute-start(bf16[96,512]{1,0:T(8,128)(2,1)S(1)} %get-tuple-element.56), channel_id=1, source_target_pairs={{0,16},{4,20},{8,24},{12,28},{16,0},{20,4},{24,8},{28,12},{1,17},{... | collective-permute-start | bytes 294920 | tf_op jit(solution)/shard_map/ppermute | solution.py:238
  33.8 0.7 collective-permute-done.8.refs_2_
  34.4 0.9 %collective-permute-start.13 = (bf16[96,512]{1,0:T(8,128)(2,1)S(1)}, bf16[96,512]{1,0:T(8,128)(2,1)S(1)}, u32[]{:S(2)}, u32[]{:S(2)}) collective-permute-start(bf16[96,512]{1,0:T(8,128)(2,1)S(1)} %get-tuple-element.57), channel_id=1, source_target_pairs={{0,20},{4,16},{8,28},{12,24},{16,4},{20,0},{24,12},{28,8},{1,21},{... | collective-permute-start | bytes 294920 | tf_op jit(solution)/shard_map/ppermute | solution.py:238
  35.3 0.0 collective-permute-done.9.refs_3_
  35.3 0.3 shard_map.52
  35.6 2.6 %collective-permute-start.14 = (bf16[6,64,128]{2,1,0:T(8,128)(2,1)S(1)}, bf16[6,64,128]{2,1,0:T(8,128)(2,1)S(1)}, u32[]{:S(2)}, u32[]{:S(2)}) collective-permute-start(bf16[6,64,128]{2,1,0:T(8,128)(2,1)S(1)} %get-tuple-element.61), channel_id=1, source_target_pairs={{0,2},{1,3},{2,0},{3,1},{4,6},{5,7},{6,4},{7,5},{8,10},{9,11},{10,... | collective-permute-start | bytes 294920 | tf_op jit(solution)/shard_map/ppermute | solution.py:238
  38.3 0.0 collective-permute-done.10.refs_4_.refs_0_
  38.3 1.8 %collective-permute-start.15 = (bf16[6,64,128]{2,1,0:T(8,128)(2,1)S(1)}, bf16[6,64,128]{2,1,0:T(8,128)(2,1)S(1)}, u32[]{:S(2)}, u32[]{:S(2)}) collective-permute-start(bf16[6,64,128]{2,1,0:T(8,128)(2,1)S(1)} %get-tuple-element.62), channel_id=1, source_target_pairs={{0,3},{1,2},{2,1},{3,0},{4,7},{5,6},{6,5},{7,4},{8,11},{9,10},{10,... | collective-permute-start | bytes 294920 | tf_op jit(solution)/shard_map/ppermute | solution.py:238
  40.1 0.0 collective-permute-done.11.refs_5_.refs_1_
  40.1 0.0 collective-permute-start.16
  40.1 0.0 collective-permute-done.12.refs_6_.refs_2_
  40.1 0.0 collective-permute-done.13.refs_7_.refs_3_
  40.1 0.3 shard_map.54
  40.5 2.6 %collective-permute-start.17 = (bf16[6,64,128]{2,1,0:T(8,128)(2,1)S(1)}, bf16[6,64,128]{2,1,0:T(8,128)(2,1)S(1)}, u32[]{:S(2)}, u32[]{:S(2)}) collective-permute-start(bf16[6,64,128]{2,1,0:T(8,128)(2,1)S(1)} %get-tuple-element.65), channel_id=1, source_target_pairs={{0,2},{1,3},{2,0},{3,1},{4,6},{5,7},{6,4},{7,5},{8,10},{9,11},{10,... | collective-permute-start | bytes 294920 | tf_op jit(solution)/shard_map/ppermute | solution.py:238
  43.1 1.8 %collective-permute-start.18 = (bf16[6,64,128]{2,1,0:T(8,128)(2,1)S(1)}, bf16[6,64,128]{2,1,0:T(8,128)(2,1)S(1)}, u32[]{:S(2)}, u32[]{:S(2)}) collective-permute-start(bf16[6,64,128]{2,1,0:T(8,128)(2,1)S(1)} %get-tuple-element.66), channel_id=1, source_target_pairs={{0,3},{1,2},{2,1},{3,0},{4,7},{5,6},{6,5},{7,4},{8,11},{9,10},{10,... | collective-permute-start | bytes 294920 | tf_op jit(solution)/shard_map/ppermute | solution.py:238
  44.9 2.9 %collective-permute-done.14.refs_1_ = bf16[6,64,128]{2,1,0:T(8,128)(2,1)S(1)} collective-permute-done((bf16[6,64,128]{2,1,0:T(8,128)(2,1)S(1)}, bf16[6,64,128]{2,1,0:T(8,128)(2,1)S(1)}, u32[]{:S(2)}, u32[]{:S(2)}) %collective-permute-start.14) | collective-permute-done | bytes 98336 | tf_op jit(solution)/shard_map/ppermute | solution.py:238
  47.8 0.0 collective-permute-start.19
  47.8 1.6 %shard_map.53 = f32[6,128,512]{2,1,0:T(8,128)} custom-call(s32[1]{0:T(128)} %bitcast.place, bf16[96,512]{1,0:T(8,128)(2,1)S(1)} %get-tuple-element.48.refs_0_, bf16[96,512]{1,0:T(8,128)(2,1)S(1)} %collective-permute-done.7.refs_1_, bf16[96,512]{1,0:T(8,128)(2,1)S(1)} %collective-permute-done.8.refs_2_, bf16[96,512]{1,0:T(8,128)(2,1)S(1)} %collective-permute-done.9.refs_3_, ...), custom_call_target="tpu_custom_call" | custom-call | flops 16777216 | bytes 1048576 | tf_op jit(solution)/shard_map/pallas_call | solution.py:310
  49.3 0.0 collective-permute-done.15.refs_2_
  49.3 0.0 collective-permute-done.16.refs_3_
  49.3 5.6 %collective-permute-done.17.refs_5_ = bf16[6,64,128]{2,1,0:T(8,128)(2,1)S(1)} collective-permute-done((bf16[6,64,128]{2,1,0:T(8,128)(2,1)S(1)}, bf16[6,64,128]{2,1,0:T(8,128)(2,1)S(1)}, u32[]{:S(2)}, u32[]{:S(2)}) %collective-permute-start.17) | collective-permute-done | bytes 98336 | tf_op jit(solution)/shard_map/ppermute | solution.py:238
  54.9 0.0 collective-permute-done.18.refs_6_
  54.9 0.0 collective-permute-done.19.refs_7_
  54.9 0.9 %shard_map.55 = (f32[256,512]{1,0:T(8,128)S(1)}, bf16[256,512]{1,0:T(8,128)(2,1)S(1)}) custom-call(s32[1]{0:T(128)} %bitcast.place, s32[1]{0:T(128)} %bitcast.2.spot, bf16[6,64,128]{2,1,0:T(8,128)(2,1)S(1)} %get-tuple-element.60.refs_0_, bf16[6,64,128]{2,1,0:T(8,128)(2,1)S(1)} %collective-permute-done.14.refs_1_, ...), custom_call_target="tpu_custom_call" | custom-call | flops 268435456 | bytes 1048576 | tf_op jit(solution)/shard_map/pallas_call | solution.py:317
  55.8 0.1 collective-permute-start.20
  55.9 1.5 %collective-permute-done.20.came = bf16[256,512]{1,0:T(8,128)(2,1)S(1)} collective-permute-done((bf16[256,512]{1,0:T(8,128)(2,1)S(1)}, bf16[256,512]{1,0:T(8,128)(2,1)S(1)}, u32[]{:S(2)}, u32[]{:S(2)}) %collective-permute-start.20) | collective-permute-done | bytes 262176 | tf_op jit(solution)/shard_map/ppermute | solution.py:238
  57.4 0.2 shard_map.56
  57.6 1.6 %collective-permute-start.21 = (bf16[64,512]{1,0:T(8,128)(2,1)S(1)}, bf16[64,512]{1,0:T(8,128)(2,1)S(1)}, u32[]{:S(2)}, u32[]{:S(2)}) collective-permute-start(bf16[64,512]{1,0:T(8,128)(2,1)S(1)} %get-tuple-element.71), channel_id=1, source_target_pairs={{0,24},{4,28},{8,16},{12,20},{16,8},{20,12},{24,0},{28,4},{1,25},{... | collective-permute-start | bytes 196616 | tf_op jit(solution)/shard_map/ppermute | solution.py:238
  59.2 0.8 %collective-permute-start.22 = (bf16[64,512]{1,0:T(8,128)(2,1)S(1)}, bf16[64,512]{1,0:T(8,128)(2,1)S(1)}, u32[]{:S(2)}, u32[]{:S(2)}) collective-permute-start(bf16[64,512]{1,0:T(8,128)(2,1)S(1)} %get-tuple-element.72), channel_id=1, source_target_pairs={{0,8},{4,12},{8,0},{12,4},{16,24},{20,28},{24,16},{28,20},{1,9},{5... | collective-permute-start | bytes 196616 | tf_op jit(solution)/shard_map/ppermute | solution.py:238
  60.0 1.1 %collective-permute-start.23 = (bf16[64,512]{1,0:T(8,128)(2,1)S(1)}, bf16[64,512]{1,0:T(8,128)(2,1)S(1)}, u32[]{:S(2)}, u32[]{:S(2)}) collective-permute-start(bf16[64,512]{1,0:T(8,128)(2,1)S(1)} %get-tuple-element.73), channel_id=1, source_target_pairs={{0,16},{4,20},{8,24},{12,28},{16,0},{20,4},{24,8},{28,12},{1,17},{... | collective-permute-start | bytes 196616 | tf_op jit(solution)/shard_map/ppermute | solution.py:238
  61.2 2.3 %collective-permute-done.21.refs_1_ = bf16[64,512]{1,0:T(8,128)(2,1)S(1)} collective-permute-done((bf16[64,512]{1,0:T(8,128)(2,1)S(1)}, bf16[64,512]{1,0:T(8,128)(2,1)S(1)}, u32[]{:S(2)}, u32[]{:S(2)}) %collective-permute-start.21) | collective-permute-done | bytes 65568 | tf_op jit(solution)/shard_map/ppermute | solution.py:238
  63.5 0.2 collective-permute-done.22.refs_2_
  63.7 0.6 collective-permute-done.23.refs_3_
  64.3 0.2 shard_map.57
  64.5 4.3 %collective-permute-start.24 = (bf16[64,128]{1,0:T(8,128)(2,1)S(1)}, bf16[64,128]{1,0:T(8,128)(2,1)S(1)}, u32[]{:S(2)}, u32[]{:S(2)}) collective-permute-start(bf16[64,128]{1,0:T(8,128)(2,1)S(1)} %get-tuple-element.75), channel_id=1, source_target_pairs={{0,2},{1,3},{2,0},{3,1},{4,6},{5,7},{6,4},{7,5},{8,10},{9,11},{10,... | collective-permute-start | bytes 49160 | tf_op jit(solution)/shard_map/ppermute | solution.py:238
  68.8 0.5 collective-permute-start.25
  69.2 0.2 collective-permute-start.26
  69.4 1.1 %collective-permute-done.24.refs_1_ = bf16[64,128]{1,0:T(8,128)(2,1)S(1)} collective-permute-done((bf16[64,128]{1,0:T(8,128)(2,1)S(1)}, bf16[64,128]{1,0:T(8,128)(2,1)S(1)}, u32[]{:S(2)}, u32[]{:S(2)}) %collective-permute-start.24) | collective-permute-done | bytes 16416 | tf_op jit(solution)/shard_map/ppermute | solution.py:238
  70.5 3.8 %collective-permute-done.25.refs_2_ = bf16[64,128]{1,0:T(8,128)(2,1)S(1)} collective-permute-done((bf16[64,128]{1,0:T(8,128)(2,1)S(1)}, bf16[64,128]{1,0:T(8,128)(2,1)S(1)}, u32[]{:S(2)}, u32[]{:S(2)}) %collective-permute-start.25) | collective-permute-done | bytes 16416 | tf_op jit(solution)/shard_map/ppermute | solution.py:238
  74.3 0.0 collective-permute-done.26.refs_3_
  74.3 0.7 shard_map.58
  (3 shorter events, 0.0 us)
Async XLA Ops:
  0.6 0.7 copy-start
  1.4 16.0 %copy-start.1 = (bf16[1024,512]{1,0:T(8,128)(2,1)S(1)}, bf16[1024,512]{1,0:T(8,128)(2,1)}, u32[]{:S(2)}) copy-start(bf16[1024,512]{1,0:T(8,128)(2,1)} %constant.11.clone.refs_8_) | copy-start | bytes 3145732
  2.9 7.4 %collective-permute-start = (bf16[104,512]{1,0:T(8,128)(2,1)S(1)}, bf16[104,512]{1,0:T(8,128)(2,1)S(1)}, u32[]{:S(2)}, u32[]{:S(2)}) collective-permute-start(bf16[104,512]{1,0:T(8,128)(2,1)S(1)} %get-tuple-element.41), channel_id=1, source_target_pairs={{0,24},{4,28},{8,16},{12,20},{16,8},{20,12},{24,0},{28,4},{1,25},{... | collective-permute-start | bytes 319496 | tf_op jit(solution)/shard_map/ppermute | solution.py:238
  6.9 6.2 %collective-permute-start.1 = (bf16[104,512]{1,0:T(8,128)(2,1)S(1)}, bf16[104,512]{1,0:T(8,128)(2,1)S(1)}, u32[]{:S(2)}, u32[]{:S(2)}) collective-permute-start(bf16[104,512]{1,0:T(8,128)(2,1)S(1)} %get-tuple-element.42), channel_id=1, source_target_pairs={{0,28},{4,24},{8,20},{12,16},{16,12},{20,8},{24,4},{28,0},{1,29},{... | collective-permute-start | bytes 319496 | tf_op jit(solution)/shard_map/ppermute | solution.py:238
  6.9 8.1 %collective-permute-start.2 = (bf16[104,512]{1,0:T(8,128)(2,1)S(1)}, bf16[104,512]{1,0:T(8,128)(2,1)S(1)}, u32[]{:S(2)}, u32[]{:S(2)}) collective-permute-start(bf16[104,512]{1,0:T(8,128)(2,1)S(1)} %get-tuple-element.43), channel_id=1, source_target_pairs={{0,8},{4,12},{8,0},{12,4},{16,24},{20,28},{24,16},{28,20},{1,9},{5... | collective-permute-start | bytes 319496 | tf_op jit(solution)/shard_map/ppermute | solution.py:238
  8.0 8.6 %collective-permute-start.3 = (bf16[104,512]{1,0:T(8,128)(2,1)S(1)}, bf16[104,512]{1,0:T(8,128)(2,1)S(1)}, u32[]{:S(2)}, u32[]{:S(2)}) collective-permute-start(bf16[104,512]{1,0:T(8,128)(2,1)S(1)} %get-tuple-element.44), channel_id=1, source_target_pairs={{0,12},{4,8},{8,4},{12,0},{16,28},{20,24},{24,20},{28,16},{1,13},{... | collective-permute-start | bytes 319496 | tf_op jit(solution)/shard_map/ppermute | solution.py:238
  8.6 8.0 %collective-permute-start.4 = (bf16[104,512]{1,0:T(8,128)(2,1)S(1)}, bf16[104,512]{1,0:T(8,128)(2,1)S(1)}, u32[]{:S(2)}, u32[]{:S(2)}) collective-permute-start(bf16[104,512]{1,0:T(8,128)(2,1)S(1)} %get-tuple-element.45), channel_id=1, source_target_pairs={{0,16},{4,20},{8,24},{12,28},{16,0},{20,4},{24,8},{28,12},{1,17},{... | collective-permute-start | bytes 319496 | tf_op jit(solution)/shard_map/ppermute | solution.py:238
  10.4 7.0 %collective-permute-start.5 = (bf16[104,512]{1,0:T(8,128)(2,1)S(1)}, bf16[104,512]{1,0:T(8,128)(2,1)S(1)}, u32[]{:S(2)}, u32[]{:S(2)}) collective-permute-start(bf16[104,512]{1,0:T(8,128)(2,1)S(1)} %get-tuple-element.46), channel_id=1, source_target_pairs={{0,20},{4,16},{8,28},{12,24},{16,4},{20,0},{24,12},{28,8},{1,21},{... | collective-permute-start | bytes 319496 | tf_op jit(solution)/shard_map/ppermute | solution.py:238
  13.1 4.3 %collective-permute-start.6 = (bf16[104,512]{1,0:T(8,128)(2,1)S(1)}, bf16[104,512]{1,0:T(8,128)(2,1)S(1)}, u32[]{:S(2)}, u32[]{:S(2)}) collective-permute-start(bf16[104,512]{1,0:T(8,128)(2,1)S(1)} %get-tuple-element.47), channel_id=1, source_target_pairs={{0,4},{4,0},{8,12},{12,8},{16,20},{20,16},{24,28},{28,24},{1,5},{5... | collective-permute-start | bytes 319496 | tf_op jit(solution)/shard_map/ppermute | solution.py:238
  26.7 5.9 %collective-permute-start.7 = (bf16[96,512]{1,0:T(8,128)(2,1)S(1)}, bf16[96,512]{1,0:T(8,128)(2,1)S(1)}, u32[]{:S(2)}, u32[]{:S(2)}) collective-permute-start(bf16[96,512]{1,0:T(8,128)(2,1)S(1)} %get-tuple-element.49), channel_id=1, source_target_pairs={{0,24},{4,28},{8,16},{12,20},{16,8},{20,12},{24,0},{28,4},{1,25},{... | collective-permute-start | bytes 294920 | tf_op jit(solution)/shard_map/ppermute | solution.py:238
  28.4 6.0 %collective-permute-start.8 = (bf16[96,512]{1,0:T(8,128)(2,1)S(1)}, bf16[96,512]{1,0:T(8,128)(2,1)S(1)}, u32[]{:S(2)}, u32[]{:S(2)}) collective-permute-start(bf16[96,512]{1,0:T(8,128)(2,1)S(1)} %get-tuple-element.50), channel_id=1, source_target_pairs={{0,28},{4,24},{8,20},{12,16},{16,12},{20,8},{24,4},{28,0},{1,29},{... | collective-permute-start | bytes 294920 | tf_op jit(solution)/shard_map/ppermute | solution.py:238
  29.1 6.2 %collective-permute-start.9 = (bf16[96,512]{1,0:T(8,128)(2,1)S(1)}, bf16[96,512]{1,0:T(8,128)(2,1)S(1)}, u32[]{:S(2)}, u32[]{:S(2)}) collective-permute-start(bf16[96,512]{1,0:T(8,128)(2,1)S(1)} %get-tuple-element.51), channel_id=1, source_target_pairs={{0,4},{4,0},{8,12},{12,8},{16,20},{20,16},{24,28},{28,24},{1,5},{5... | collective-permute-start | bytes 294920 | tf_op jit(solution)/shard_map/ppermute | solution.py:238
  29.8 8.5 %collective-permute-start.10 = (bf16[96,512]{1,0:T(8,128)(2,1)S(1)}, bf16[96,512]{1,0:T(8,128)(2,1)S(1)}, u32[]{:S(2)}, u32[]{:S(2)}) collective-permute-start(bf16[96,512]{1,0:T(8,128)(2,1)S(1)} %get-tuple-element.53), channel_id=1, source_target_pairs={{0,8},{4,12},{8,0},{12,4},{16,24},{20,28},{24,16},{28,20},{1,9},{5... | collective-permute-start | bytes 294920 | tf_op jit(solution)/shard_map/ppermute | solution.py:238
  30.7 9.4 %collective-permute-start.11 = (bf16[96,512]{1,0:T(8,128)(2,1)S(1)}, bf16[96,512]{1,0:T(8,128)(2,1)S(1)}, u32[]{:S(2)}, u32[]{:S(2)}) collective-permute-start(bf16[96,512]{1,0:T(8,128)(2,1)S(1)} %get-tuple-element.55), channel_id=1, source_target_pairs={{0,12},{4,8},{8,4},{12,0},{16,28},{20,24},{24,20},{28,16},{1,13},{... | collective-permute-start | bytes 294920 | tf_op jit(solution)/shard_map/ppermute | solution.py:238
  32.6 7.5 %collective-permute-start.12 = (bf16[96,512]{1,0:T(8,128)(2,1)S(1)}, bf16[96,512]{1,0:T(8,128)(2,1)S(1)}, u32[]{:S(2)}, u32[]{:S(2)}) collective-permute-start(bf16[96,512]{1,0:T(8,128)(2,1)S(1)} %get-tuple-element.56), channel_id=1, source_target_pairs={{0,16},{4,20},{8,24},{12,28},{16,0},{20,4},{24,8},{28,12},{1,17},{... | collective-permute-start | bytes 294920 | tf_op jit(solution)/shard_map/ppermute | solution.py:238
  34.4 5.7 %collective-permute-start.13 = (bf16[96,512]{1,0:T(8,128)(2,1)S(1)}, bf16[96,512]{1,0:T(8,128)(2,1)S(1)}, u32[]{:S(2)}, u32[]{:S(2)}) collective-permute-start(bf16[96,512]{1,0:T(8,128)(2,1)S(1)} %get-tuple-element.57), channel_id=1, source_target_pairs={{0,20},{4,16},{8,28},{12,24},{16,4},{20,0},{24,12},{28,8},{1,21},{... | collective-permute-start | bytes 294920 | tf_op jit(solution)/shard_map/ppermute | solution.py:238
  35.6 12.1 %collective-permute-start.14 = (bf16[6,64,128]{2,1,0:T(8,128)(2,1)S(1)}, bf16[6,64,128]{2,1,0:T(8,128)(2,1)S(1)}, u32[]{:S(2)}, u32[]{:S(2)}) collective-permute-start(bf16[6,64,128]{2,1,0:T(8,128)(2,1)S(1)} %get-tuple-element.61), channel_id=1, source_target_pairs={{0,2},{1,3},{2,0},{3,1},{4,6},{5,7},{6,4},{7,5},{8,10},{9,11},{10,... | collective-permute-start | bytes 294920 | tf_op jit(solution)/shard_map/ppermute | solution.py:238
  38.3 11.1 %collective-permute-start.15 = (bf16[6,64,128]{2,1,0:T(8,128)(2,1)S(1)}, bf16[6,64,128]{2,1,0:T(8,128)(2,1)S(1)}, u32[]{:S(2)}, u32[]{:S(2)}) collective-permute-start(bf16[6,64,128]{2,1,0:T(8,128)(2,1)S(1)} %get-tuple-element.62), channel_id=1, source_target_pairs={{0,3},{1,2},{2,1},{3,0},{4,7},{5,6},{6,5},{7,4},{8,11},{9,10},{10,... | collective-permute-start | bytes 294920 | tf_op jit(solution)/shard_map/ppermute | solution.py:238
  40.1 9.2 %collective-permute-start.16 = (bf16[6,64,128]{2,1,0:T(8,128)(2,1)S(1)}, bf16[6,64,128]{2,1,0:T(8,128)(2,1)S(1)}, u32[]{:S(2)}, u32[]{:S(2)}) collective-permute-start(bf16[6,64,128]{2,1,0:T(8,128)(2,1)S(1)} %get-tuple-element.63), channel_id=1, source_target_pairs={{0,1},{1,0},{2,3},{3,2},{4,5},{5,4},{6,7},{7,6},{8,9},{9,8},{10,11... | collective-permute-start | bytes 294920 | tf_op jit(solution)/shard_map/ppermute | solution.py:238
  40.5 14.4 %collective-permute-start.17 = (bf16[6,64,128]{2,1,0:T(8,128)(2,1)S(1)}, bf16[6,64,128]{2,1,0:T(8,128)(2,1)S(1)}, u32[]{:S(2)}, u32[]{:S(2)}) collective-permute-start(bf16[6,64,128]{2,1,0:T(8,128)(2,1)S(1)} %get-tuple-element.65), channel_id=1, source_target_pairs={{0,2},{1,3},{2,0},{3,1},{4,6},{5,7},{6,4},{7,5},{8,10},{9,11},{10,... | collective-permute-start | bytes 294920 | tf_op jit(solution)/shard_map/ppermute | solution.py:238
  43.1 11.8 %collective-permute-start.18 = (bf16[6,64,128]{2,1,0:T(8,128)(2,1)S(1)}, bf16[6,64,128]{2,1,0:T(8,128)(2,1)S(1)}, u32[]{:S(2)}, u32[]{:S(2)}) collective-permute-start(bf16[6,64,128]{2,1,0:T(8,128)(2,1)S(1)} %get-tuple-element.66), channel_id=1, source_target_pairs={{0,3},{1,2},{2,1},{3,0},{4,7},{5,6},{6,5},{7,4},{8,11},{9,10},{10,... | collective-permute-start | bytes 294920 | tf_op jit(solution)/shard_map/ppermute | solution.py:238
  47.8 7.1 %collective-permute-start.19 = (bf16[6,64,128]{2,1,0:T(8,128)(2,1)S(1)}, bf16[6,64,128]{2,1,0:T(8,128)(2,1)S(1)}, u32[]{:S(2)}, u32[]{:S(2)}) collective-permute-start(bf16[6,64,128]{2,1,0:T(8,128)(2,1)S(1)} %get-tuple-element.67), channel_id=1, source_target_pairs={{0,1},{1,0},{2,3},{3,2},{4,5},{5,4},{6,7},{7,6},{8,9},{9,8},{10,11... | collective-permute-start | bytes 294920 | tf_op jit(solution)/shard_map/ppermute | solution.py:238
  55.8 1.6 %collective-permute-start.20 = (bf16[256,512]{1,0:T(8,128)(2,1)S(1)}, bf16[256,512]{1,0:T(8,128)(2,1)S(1)}, u32[]{:S(2)}, u32[]{:S(2)}) collective-permute-start(bf16[256,512]{1,0:T(8,128)(2,1)S(1)} %get-tuple-element.69), channel_id=1, source_target_pairs={{0,4},{4,0},{8,12},{12,8},{16,20},{20,16},{24,28},{28,24},{1,5},{5... | collective-permute-start | bytes 786440 | tf_op jit(solution)/shard_map/ppermute | solution.py:238
  57.6 5.9 %collective-permute-start.21 = (bf16[64,512]{1,0:T(8,128)(2,1)S(1)}, bf16[64,512]{1,0:T(8,128)(2,1)S(1)}, u32[]{:S(2)}, u32[]{:S(2)}) collective-permute-start(bf16[64,512]{1,0:T(8,128)(2,1)S(1)} %get-tuple-element.71), channel_id=1, source_target_pairs={{0,24},{4,28},{8,16},{12,20},{16,8},{20,12},{24,0},{28,4},{1,25},{... | collective-permute-start | bytes 196616 | tf_op jit(solution)/shard_map/ppermute | solution.py:238
  59.2 4.5 %collective-permute-start.22 = (bf16[64,512]{1,0:T(8,128)(2,1)S(1)}, bf16[64,512]{1,0:T(8,128)(2,1)S(1)}, u32[]{:S(2)}, u32[]{:S(2)}) collective-permute-start(bf16[64,512]{1,0:T(8,128)(2,1)S(1)} %get-tuple-element.72), channel_id=1, source_target_pairs={{0,8},{4,12},{8,0},{12,4},{16,24},{20,28},{24,16},{28,20},{1,9},{5... | collective-permute-start | bytes 196616 | tf_op jit(solution)/shard_map/ppermute | solution.py:238
  60.0 4.3 %collective-permute-start.23 = (bf16[64,512]{1,0:T(8,128)(2,1)S(1)}, bf16[64,512]{1,0:T(8,128)(2,1)S(1)}, u32[]{:S(2)}, u32[]{:S(2)}) collective-permute-start(bf16[64,512]{1,0:T(8,128)(2,1)S(1)} %get-tuple-element.73), channel_id=1, source_target_pairs={{0,16},{4,20},{8,24},{12,28},{16,0},{20,4},{24,8},{28,12},{1,17},{... | collective-permute-start | bytes 196616 | tf_op jit(solution)/shard_map/ppermute | solution.py:238
  64.5 6.0 %collective-permute-start.24 = (bf16[64,128]{1,0:T(8,128)(2,1)S(1)}, bf16[64,128]{1,0:T(8,128)(2,1)S(1)}, u32[]{:S(2)}, u32[]{:S(2)}) collective-permute-start(bf16[64,128]{1,0:T(8,128)(2,1)S(1)} %get-tuple-element.75), channel_id=1, source_target_pairs={{0,2},{1,3},{2,0},{3,1},{4,6},{5,7},{6,4},{7,5},{8,10},{9,11},{10,... | collective-permute-start | bytes 49160 | tf_op jit(solution)/shard_map/ppermute | solution.py:238
  68.8 5.5 %collective-permute-start.25 = (bf16[64,128]{1,0:T(8,128)(2,1)S(1)}, bf16[64,128]{1,0:T(8,128)(2,1)S(1)}, u32[]{:S(2)}, u32[]{:S(2)}) collective-permute-start(bf16[64,128]{1,0:T(8,128)(2,1)S(1)} %get-tuple-element.76), channel_id=1, source_target_pairs={{0,3},{1,2},{2,1},{3,0},{4,7},{5,6},{6,5},{7,4},{8,11},{9,10},{10,... | collective-permute-start | bytes 49160 | tf_op jit(solution)/shard_map/ppermute | solution.py:238
  69.2 5.1 %collective-permute-start.26 = (bf16[64,128]{1,0:T(8,128)(2,1)S(1)}, bf16[64,128]{1,0:T(8,128)(2,1)S(1)}, u32[]{:S(2)}, u32[]{:S(2)}) collective-permute-start(bf16[64,128]{1,0:T(8,128)(2,1)S(1)} %get-tuple-element.77), channel_id=1, source_target_pairs={{0,1},{1,0},{2,3},{3,2},{4,5},{5,4},{6,7},{7,6},{8,9},{9,8},{10,11... | collective-permute-start | bytes 49160 | tf_op jit(solution)/shard_map/ppermute | solution.py:238
